TPU v7x, 128 devices: a whole 4x4x4 slice. The times are simulated.
128 devices in a mesh: row: 8 (over y_lo, z), col: 2 (over core), fib: 8 (over y_hi, x).
Axes of the slice: x: 4, y: 4 (y_hi: 2, y_lo: 2; y = y_hi * 2 + y_lo), z: 4, core: 2. Of those that a mesh axis runs over, the one named last changes fastest.
Arguments:
- features: bfloat16 [32768, 1024], P(('row', 'col'), 'fib'), may hold values from -6 to 6
- pre_activation: bfloat16 [32768, 1024], P(('row', 'col'), 'fib'), may hold values from -8 to 8
- out_grad: bfloat16 [32768, 1024], P(('row', 'col'), 'fib'), may hold values from -1.5 to 1.5
- weight: bfloat16 [1024, 1024], P('fib'), may hold values from -0.1875 to 0.1875
- tile_values: bfloat16 [8, 2, 128, 256, 256], P('row', 'col'), may hold values from 0.0019989014 to 0.059814453
- tile_rows: int32 [8, 2, 128], P('row', 'col'), may hold values from 0 to 15, as said below
- tile_cols: int32 [8, 2, 128], P('row', 'col'), may hold values from 0 to 63, as said below
- tile_counts: int32 [8, 2], P('row', 'col'), may hold values from 16 to 128, as said below
Outputs:
- grad_features: bfloat16 [32768, 1024], P(('row', 'col'), 'fib')
- grad_weight: float32 [1024, 1024], P('fib')
Inputs may be any that keep to these rules, and one draw needn't show every extreme that they name: `tile_rows`: within one block the used slots name distinct tiles, rows below 16. `tile_cols`: columns below 64. `tile_counts`: some block uses all 128 slots.
All inputs are finite; a program needn't handle non-finite values.
Results may differ from a plain program's by a relative error of at most 0.0058.
Values may be sent and summed in bfloat16 or wider, within the bound.
A program may use at most 128 MiB of HBM per device.

v0:
```python
import jax
import jax.numpy as jnp
from jax import lax
from jax.sharding import PartitionSpec as P


def split_up(value, dim, peers):
    before, after = (value.shape[:dim], value.shape[dim + 1 :])
    return jnp.moveaxis(value.reshape(*before, peers, -1, *after), dim, 0)


def summed_on_arrival(value, axis, dim):
    peers = lax.axis_size(axis)
    pieces = lax.all_to_all(split_up(value, dim, peers), axis, 0, 0, tiled=True)
    return jnp.sum(pieces, axis=0)


def total_of_pieces(value, axis):
    return lax.all_gather(value, axis).sum(0)


def from_everyone(value, axis):
    peers = lax.axis_size(axis)
    return lax.all_to_all(
        jnp.broadcast_to(value[None], (peers, *value.shape)), axis, 0, 0, tiled=True
    )


def joined_along(pieces, dim):
    dims = list(pieces.shape[1:])
    dims[dim] *= pieces.shape[0]
    return jnp.moveaxis(pieces, 0, dim).reshape(dims)


def gather_directly(value, axis, dim):
    pieces = from_everyone(value, axis)
    return joined_along(pieces, dim)


def place_group(running, products, target, valid, offset):
    out_tiles = running.shape[0]
    local = target - offset
    placing = (
        (local[:, None] == jnp.arange(out_tiles, dtype=jnp.int32)[None, :]) & valid[:, None]
    ).astype(jnp.float32)
    return running + jnp.einsum("st,sif->tif", placing, products, precision=lax.Precision.HIGHEST)


def group_products(tile_block, row_index, col_index, panels_all, first, slot_group, transpose):
    block_vals = lax.dynamic_slice_in_dim(tile_block, first, slot_group, 0)
    block_rows = lax.dynamic_slice_in_dim(row_index, first, slot_group, 0)
    block_cols = lax.dynamic_slice_in_dim(col_index, first, slot_group, 0)
    if transpose:
        products = jnp.einsum(
            "sij,sif->sjf", block_vals, panels_all[block_rows], preferred_element_type=jnp.float32
        )
        return (products, block_cols)
    products = jnp.einsum(
        "sij,sjf->sif", block_vals, panels_all[block_cols], preferred_element_type=jnp.float32
    )
    return (products, block_rows)


def group_total(tile_block, slot_group):
    return tile_block.shape[0] // slot_group


def tile_products(tile_block, row_index, col_index, live_count, panel_source, out_tiles, transpose):
    tile_size = tile_block.shape[1]
    feature_cols = panel_source.shape[1]
    panels_all = panel_source.reshape(-1, tile_size, feature_cols)
    slot_group = 16

    def one_block(block_index, running):
        first = block_index * slot_group
        products, target = group_products(
            tile_block, row_index, col_index, panels_all, first, slot_group, transpose
        )
        valid = first + jnp.arange(slot_group, dtype=jnp.int32) < live_count
        return place_group(running, products, target, valid, 0)

    initial = jnp.zeros((out_tiles, tile_size, feature_cols), jnp.float32)
    running = lax.fori_loop(0, group_total(tile_block, slot_group), one_block, initial)
    return running.reshape(out_tiles * tile_size, feature_cols)


def on_device(
    features, pre_activation, out_grad, weight, tile_values, tile_rows, tile_cols, tile_counts
):
    tile_block = tile_values[0, 0]
    row_index = tile_rows[0, 0]
    col_index = tile_cols[0, 0]
    live_count = tile_counts[0, 0]
    node_dev = features.shape[0]
    tile_size = tile_block.shape[1]
    row_tiles = node_dev * lax.axis_size("col") // tile_size
    col_tiles = node_dev * lax.axis_size("row") // tile_size
    column_block = lax.all_gather(features, "row", axis=0, tiled=True)
    partial_value = tile_products(
        tile_block, row_index, col_index, live_count, column_block, row_tiles, False
    )
    aggregated = summed_on_arrival(partial_value, "col", 0).astype(jnp.bfloat16)
    pre_value = pre_activation.astype(jnp.float32)
    sigmoid_value = jax.nn.sigmoid(pre_value)
    grad_local = (
        out_grad.astype(jnp.float32) * sigmoid_value * (1.0 + pre_value * (1.0 - sigmoid_value))
    ).astype(jnp.bfloat16)
    full_grad = lax.all_gather(grad_local, "fib", axis=1, tiled=True)
    weight_part = lax.dot_general(
        aggregated, full_grad, (((0,), (0,)), ((), ())), preferred_element_type=jnp.float32
    )
    grad_weight = total_of_pieces(weight_part, ("row", "col"))
    projected = lax.dot_general(
        full_grad, weight, (((1,), (1,)), ((), ())), preferred_element_type=jnp.float32
    ).astype(jnp.bfloat16)
    row_block = gather_directly(projected, "col", 0)
    transposed = tile_products(
        tile_block, row_index, col_index, live_count, row_block, col_tiles, True
    )
    grad_features = lax.psum_scatter(transposed, "row", scatter_dimension=0, tiled=True).astype(
        jnp.bfloat16
    )
    return (grad_features, grad_weight)


def solution(mesh):
    in_specs = (
        P(("row", "col"), "fib"),
        P(("row", "col"), "fib"),
        P(("row", "col"), "fib"),
        P("fib", None),
        P("row", "col", None, None, None),
        P("row", "col", None),
        P("row", "col", None),
        P("row", "col"),
    )
    out_specs = (P(("row", "col"), "fib"), P("fib", None))
    return jax.shard_map(
        on_device, mesh=mesh, in_specs=in_specs, out_specs=out_specs, check_vma=False
    )
```

profile of v0, /device:TPU:1, one launch (start us, length us, event | category | flops | bytes accessed | tf_op | source)
XLA Modules:
  0.0 379.1 jit_solution(10993640622262767804)
XLA Ops:
  10.5 55.2 %all-gather.7.cloned.1.call-done = bf16[16384,128]{1,0:T(8,128)(2,1)} async-done(((bf16[2048,128]{1,0:T(8,128)(2,1)}), bf16[16384,128]{1,0:T(8,128)(2,1)}) %all-gather.7.cloned.1.call-update) | async-done | bytes 4194320 | tf_op jit(solution)/shard_map/all_gather | solution.py:98
  65.7 76.0 %while.29 = (s32[]{:T(128)}, f32[16,256,128]{2,0,1:T(8,128)S(1)}, s32[128]{0:T(128)S(1)}, s32[]{:T(128)}, bf16[128,256,256]{2,1,0:T(8,128)(2,1)}, /*index=5*/s32...) while((s32[]{:T(128)}, f32[16,256,128]{2,0,1:T(8,128)S(1)}, ...), condition=%wide.region_4.0_spmd.clone, body=%wide.region_3.0_spmd.clone.sunk | while | flops 370148960 | bytes 13636257 | solution.py:83
  71.8 3.4 select_add_fusion.5
  81.5 3.4 select_add_fusion.5
  91.0 3.4 select_add_fusion.5
  100.5 3.4 select_add_fusion.5
  110.0 3.4 select_add_fusion.5
  119.5 3.4 select_add_fusion.5
  142.4 5.7 %all_to_all.10 = f32[2,2048,128]{2,1,0:T(8,128)S(1)} all-to-all(f32[2,2048,128]{2,1,0:T(8,128)S(1)} %bitcast.33), channel_id=1, replica_groups=mesh['row'=8,'col'=2,'fib'=8] {'col'}, dimensions={0} | all-to-all | bytes 4194304 | tf_op jit(solution)/shard_map/all_to_all | solution.py:14
  148.2 3.7 fusion.29
  152.1 3.4 convolution_convert_fusion
  155.6 4.7 %all_to_all.11 = bf16[2,2048,128]{2,1,0:T(8,128)(2,1)S(1)} all-to-all(bf16[2,2048,128]{2,1,0:T(8,128)(2,1)S(1)} %broadcast_in_dim.45), channel_id=1, replica_groups=mesh['row'=8,'col'=2,'fib'=8] {'col'}, dimensions={0} | all-to-all | bytes 2097152 | tf_op jit(solution)/shard_map/all_to_all | solution.py:24
  160.3 106.9 %while.28 = (s32[]{:T(128)}, f32[64,256,128]{2,0,1:T(8,128)}, s32[128]{0:T(128)S(1)}, s32[]{:T(128)}, bf16[128,256,256]{2,1,0:T(8,128)(2,1)}, /*index=5*/s32[128...) while((s32[]{:T(128)}, f32[64,256,128]{2,0,1:T(8,128)}, ...), condition=%wide.region_1.0_spmd.clone, body=%wide.region_0.0_spmd.clone.sunk | while | flops 675286144 | bytes 26219168 | solution.py:83
  164.2 7.5 %select_add_fusion.4 = f32[64,256,128]{2,0,1:T(8,128)} fusion(f32[64,256,128]{2,0,1:T(8,128)} %get-tuple-element.426, pred[]{:T(512)S(6)} %compare.6, f32[16,256,128]{2,1,0:T(8,128)S(1)} %fusion.50, s32[16]{0:T(128)S(1)} %dynamic_slice.62, pred[16]{0:T(512)(128)(4,1)S(1)} %add_compare_fusion.4), kind=kOutput, calls=%fused_computation.2.clone.1 | convolution fusion | flops 406849536 | bytes 18874448 | tf_op jit(solution)/shard_map/while/body/eval_jaxpr/st,sif->tif/dot_general | solution.py:46
  175.8 9.7 %select_add_fusion.4 = f32[64,256,128]{2,0,1:T(8,128)} fusion(f32[64,256,128]{2,0,1:T(8,128)} %get-tuple-element.426, pred[]{:T(512)S(6)} %compare.6, f32[16,256,128]{2,1,0:T(8,128)S(1)} %fusion.50, s32[16]{0:T(128)S(1)} %dynamic_slice.62, pred[16]{0:T(512)(128)(4,1)S(1)} %add_compare_fusion.4), kind=kOutput, calls=%fused_computation.2.clone.1 | convolution fusion | flops 406849536 | bytes 18874448 | tf_op jit(solution)/shard_map/while/body/eval_jaxpr/st,sif->tif/dot_general | solution.py:46
  189.5 9.7 %select_add_fusion.4 = f32[64,256,128]{2,0,1:T(8,128)} fusion(f32[64,256,128]{2,0,1:T(8,128)} %get-tuple-element.426, pred[]{:T(512)S(6)} %compare.6, f32[16,256,128]{2,1,0:T(8,128)S(1)} %fusion.50, s32[16]{0:T(128)S(1)} %dynamic_slice.62, pred[16]{0:T(512)(128)(4,1)S(1)} %add_compare_fusion.4), kind=kOutput, calls=%fused_computation.2.clone.1 | convolution fusion | flops 406849536 | bytes 18874448 | tf_op jit(solution)/shard_map/while/body/eval_jaxpr/st,sif->tif/dot_general | solution.py:46
  203.2 9.7 %select_add_fusion.4 = f32[64,256,128]{2,0,1:T(8,128)} fusion(f32[64,256,128]{2,0,1:T(8,128)} %get-tuple-element.426, pred[]{:T(512)S(6)} %compare.6, f32[16,256,128]{2,1,0:T(8,128)S(1)} %fusion.50, s32[16]{0:T(128)S(1)} %dynamic_slice.62, pred[16]{0:T(512)(128)(4,1)S(1)} %add_compare_fusion.4), kind=kOutput, calls=%fused_computation.2.clone.1 | convolution fusion | flops 406849536 | bytes 18874448 | tf_op jit(solution)/shard_map/while/body/eval_jaxpr/st,sif->tif/dot_general | solution.py:46
  216.8 9.7 %select_add_fusion.4 = f32[64,256,128]{2,0,1:T(8,128)} fusion(f32[64,256,128]{2,0,1:T(8,128)} %get-tuple-element.426, pred[]{:T(512)S(6)} %compare.6, f32[16,256,128]{2,1,0:T(8,128)S(1)} %fusion.50, s32[16]{0:T(128)S(1)} %dynamic_slice.62, pred[16]{0:T(512)(128)(4,1)S(1)} %add_compare_fusion.4), kind=kOutput, calls=%fused_computation.2.clone.1 | convolution fusion | flops 406849536 | bytes 18874448 | tf_op jit(solution)/shard_map/while/body/eval_jaxpr/st,sif->tif/dot_general | solution.py:46
  230.4 9.7 %select_add_fusion.4 = f32[64,256,128]{2,0,1:T(8,128)} fusion(f32[64,256,128]{2,0,1:T(8,128)} %get-tuple-element.426, pred[]{:T(512)S(6)} %compare.6, f32[16,256,128]{2,1,0:T(8,128)S(1)} %fusion.50, s32[16]{0:T(128)S(1)} %dynamic_slice.62, pred[16]{0:T(512)(128)(4,1)S(1)} %add_compare_fusion.4), kind=kOutput, calls=%fused_computation.2.clone.1 | convolution fusion | flops 406849536 | bytes 18874448 | tf_op jit(solution)/shard_map/while/body/eval_jaxpr/st,sif->tif/dot_general | solution.py:46
  244.0 9.7 %select_add_fusion.4 = f32[64,256,128]{2,0,1:T(8,128)} fusion(f32[64,256,128]{2,0,1:T(8,128)} %get-tuple-element.426, pred[]{:T(512)S(6)} %compare.6, f32[16,256,128]{2,1,0:T(8,128)S(1)} %fusion.50, s32[16]{0:T(128)S(1)} %dynamic_slice.62, pred[16]{0:T(512)(128)(4,1)S(1)} %add_compare_fusion.4), kind=kOutput, calls=%fused_computation.2.clone.1 | convolution fusion | flops 406849536 | bytes 18874448 | tf_op jit(solution)/shard_map/while/body/eval_jaxpr/st,sif->tif/dot_general | solution.py:46
  257.6 9.7 %select_add_fusion.4 = f32[64,256,128]{2,0,1:T(8,128)} fusion(f32[64,256,128]{2,0,1:T(8,128)} %get-tuple-element.426, pred[]{:T(512)S(6)} %compare.6, f32[16,256,128]{2,1,0:T(8,128)S(1)} %fusion.50, s32[16]{0:T(128)S(1)} %dynamic_slice.62, pred[16]{0:T(512)(128)(4,1)S(1)} %add_compare_fusion.4), kind=kOutput, calls=%fused_computation.2.clone.1 | convolution fusion | flops 406849536 | bytes 18874448 | tf_op jit(solution)/shard_map/while/body/eval_jaxpr/st,sif->tif/dot_general | solution.py:46
  267.2 11.5 %copy.11 = f32[64,256,128]{2,1,0:T(8,128)} copy(f32[64,256,128]{2,0,1:T(8,128)} %get-tuple-element.250) | data formatting | bytes 16777216 | tf_op jit(solution)/shard_map/while | solution.py:83
  278.8 5.1 %reduce_sum.19 = f32[128,1024]{1,0:T(8,128)} reduce(f32[16,128,1024]{2,1,0:T(8,128)} %bitcast.32, f32[]{:T(128)} %constant.71.clone.1), dimensions={0}, to_apply=%region_6.0 | reduce | flops 1966080 | bytes 8912900 | tf_op jit(solution)/shard_map/reduce_sum | solution.py:19
  283.8 86.7 %reduce-scatter.2.cloned.1.call-done = f32[2048,128]{1,0:T(8,128)} async-done(((f32[16384,128]{1,0:T(8,128)}), f32[2048,128]{1,0:T(8,128)}) %reduce-scatter.2.cloned.1.call-update) | async-done | bytes 1048592 | tf_op jit(solution)/shard_map/reduce_scatter | solution.py:120
  (123 shorter events, 93.2 us)
Async XLA Ops:
  7.2 144.9 %copy-start = (bf16[128,1024]{1,0:T(8,128)(2,1)S(1)}, bf16[128,1024]{1,0:T(8,128)(2,1)}, u32[]{:S(2)}) copy-start(bf16[128,1024]{1,0:T(8,128)(2,1)} %param.15) | copy-start | bytes 786436
  7.2 58.6 %copy-start.3 = (s32[1,1,128]{2,1,0:T(1,128)S(1)}, s32[1,1,128]{2,1,0:T(1,128)}, u32[]{:S(2)}) copy-start(s32[1,1,128]{2,1,0:T(1,128)} %param.18) | copy-start | bytes 1540
  7.2 58.6 %copy-start.2 = (s32[1,1,128]{2,1,0:T(1,128)S(1)}, s32[1,1,128]{2,1,0:T(1,128)}, u32[]{:S(2)}) copy-start(s32[1,1,128]{2,1,0:T(1,128)} %param.17) | copy-start | bytes 1540
  7.2 58.5 %all-gather.7.cloned.1.call-start = ((), (), s32[]{:S(2)}) async-start(), calls=%async_computation.5 | async-start | bytes 4718592 | tf_op jit(solution)/shard_map/all_gather | solution.py:98
  7.9 140.3 %all-gather.5.cloned.1.call-start = ((), (), s32[]{:S(2)}) async-start(), calls=%async_computation.3 | async-start | bytes 4718592 | tf_op jit(solution)/shard_map/all_gather | solution.py:108
  10.4 268.3 %all-gather.9.cloned.1.call-start = ((), (), s32[]{:S(2)}) async-start(), calls=%async_computation.6 | async-start | bytes 8912896 | tf_op jit(solution)/shard_map/all_gather | solution.py:19
  152.0 218.5 %reduce-scatter.2.cloned.1.call-start = ((), (), s32[]{:S(2)}) async-start(), calls=%async_computation.4 | async-start | bytes 9437184 | tf_op jit(solution)/shard_map/reduce_scatter | solution.py:120
  278.7 93.8 %copy-start.1 = (bf16[128,1024]{1,0:T(8,128)(2,1)S(1)}, bf16[128,1024]{1,0:T(8,128)(2,1)}, u32[]{:S(2)}) copy-start(bf16[128,1024]{1,0:T(8,128)(2,1)} %param.15) | copy-start | bytes 786436
Sparse Core Ops, SparseCore 0:
  9.7 56.0 all-gather.6
  68.5 75.8 all-gather.4
  152.1 50.9 all-gather.8
  278.8 91.6 reduce-scatter.1
where the time goes:
time: 380 us; the launch traced here: 379 us
  matrix products  147 us (39%)
  waiting for transfers between devices  143 us (38%)
  local copies, waits for them, and re-layouts  43.3 us (11%)
  other arithmetic  21.5 us (6%)
  between operations  13.9 us (4%)
  blocking collectives  10.4 us (3%)
    dot_general x16, matrix products, place_group(): jnp.einsum('st,sif->tif', placing, products, precision=lax.Precision.HIGH...  102 us
    reduce_scatter x1, waiting for transfers between devices, on_device(): lax.psum_scatter(transposed, 'row', scatter_dimension=0, tiled=True)  86.7 us
    all_gather x1, waiting for transfers between devices, on_device(): column_block = lax.all_gather(features, 'row', axis=0, tiled=True)  55.2 us
    gather x8, local copies, waits for them, and re-layouts, group_products(): panels_all[block_cols]  23.9 us
    dot_general x8, matrix products, group_products(): jnp.einsum('sij,sif->sjf', block_vals, panels_all[block_rows], preferred_...  19 us
    dot_general x8, matrix products, group_products(): jnp.einsum('sij,sjf->sif', block_vals, panels_all[block_cols], preferred_...  18.4 us
    while x2, local copies, waits for them, and re-layouts, tile_products(): lax.fori_loop(0, group_total(tile_block, slot_group), one_block, initial)  12.1 us
    lt x16, other arithmetic, one_block(): valid = first + jnp.arange(slot_group, dtype=jnp.int32) < live_count  10.4 us
  transfers between devices with their start and end apart: 4, of which 2 were waited for; matrix products, arithmetic and copies ran while one was open for 54% of the time, Pallas kernels for 0%

commit v1 on v0

v1 whole, which is shorter than its diff:
```python
import jax
import jax.numpy as jnp
from jax import lax
from jax.experimental import pallas as pl
from jax.experimental.pallas import tpu as pltpu
from jax.sharding import PartitionSpec as P

GROUP = 8


def tile_kernel(rows_ref, cols_ref, count_ref, grad_ref, tiles_ref, out_ref, held, total, sems):
    slots, tile, _ = tiles_ref.shape
    groups = slots // GROUP
    out_tiles = out_ref.shape[0]
    row_tiles = grad_ref.shape[0]
    count = jnp.clip(count_ref[0, 0], 0, slots)
    used = (count + GROUP - 1) // GROUP

    def copy(g):
        part = pl.ds(g * GROUP, GROUP)
        return pltpu.make_async_copy(tiles_ref.at[part], held.at[part], sems.at[g])

    @pl.loop(0, used)
    def _(g):
        copy(g).start()

    @pl.loop(0, out_tiles + 1)
    def _(t):
        total[t] = jnp.zeros(total.shape[1:], total.dtype)

    @pl.loop(0, used)
    def _(g):
        copy(g).wait()
        for j in range(GROUP):
            slot = g * GROUP + j
            row = jnp.clip(rows_ref[0, 0, slot], 0, row_tiles - 1)
            col = jnp.clip(cols_ref[0, 0, slot], 0, out_tiles - 1)
            target = jnp.where(slot < count, col, out_tiles)
            total[target] += jnp.dot(
                grad_ref[row], held[slot], preferred_element_type=jnp.float32
            )

    @pl.loop(0, out_tiles)
    def _(t):
        out_ref[t] = total[t].astype(out_ref.dtype)


def tile_products(rows, cols, count, grad, tiles, out_tiles):
    slots, tile, _ = tiles.shape
    width = grad.shape[1]
    smem = pl.BlockSpec(memory_space=pltpu.SMEM)
    vmem = pl.BlockSpec(memory_space=pltpu.VMEM)
    return pl.pallas_call(
        tile_kernel,
        out_shape=jax.ShapeDtypeStruct((out_tiles, width, tile), jnp.bfloat16),
        in_specs=[smem, smem, smem, vmem, pl.BlockSpec(memory_space=pl.ANY)],
        out_specs=vmem,
        scratch_shapes=[
            pltpu.VMEM((slots, tile, tile), jnp.bfloat16),
            pltpu.VMEM((out_tiles + 1, width, tile), jnp.float32),
            pltpu.SemaphoreType.DMA((slots // GROUP,)),
        ],
        compiler_params=pltpu.CompilerParams(vmem_limit_bytes=40 << 20),
        cost_estimate=pl.CostEstimate(
            flops=2 * slots * width * tile * tile,
            bytes_accessed=2 * slots * tile * tile,
            transcendentals=0,
        ),
        name="tile_products",
    )(rows, cols, count, grad, tiles)


def on_device(features, pre_activation, out_grad, weight, tiles, rows, cols, counts):
    nodes, width = features.shape
    tile = tiles.shape[-1]
    fib = lax.axis_size("fib")
    own_tiles = nodes // tile
    pre = pre_activation.astype(jnp.float32)
    sigmoid = jax.nn.sigmoid(pre)
    grad = (out_grad.astype(jnp.float32) * sigmoid * (1.0 + pre * (1.0 - sigmoid))).astype(
        jnp.bfloat16
    )
    grad = grad.reshape(own_tiles, tile, width).transpose(0, 2, 1)
    grad = lax.all_gather(grad, "col", axis=0, tiled=True)
    partial_t = tile_products(
        rows, cols, counts, grad, tiles[0, 0], own_tiles * lax.axis_size("row")
    )
    summed = lax.psum_scatter(partial_t, "row", scatter_dimension=0, tiled=True)
    whole = lax.all_gather(summed, "fib", axis=0)
    left = weight.reshape(width, fib, width)
    grad_features = jnp.einsum("ifo,fton->tni", left, whole, preferred_element_type=jnp.float32)
    grad_features = grad_features.astype(jnp.bfloat16).reshape(nodes, width)
    part = jnp.einsum(
        "fton,tni->foi",
        whole,
        features.reshape(own_tiles, tile, width),
        preferred_element_type=jnp.float32,
    )
    part = part.reshape(fib * width, width)
    piece = lax.psum_scatter(part, ("row", "col"), scatter_dimension=0, tiled=True)
    grad_weight = lax.all_gather(piece, ("row", "col"), axis=0, tiled=True).T
    return grad_features, grad_weight


def solution(mesh):
    in_specs = (
        P(("row", "col"), "fib"),
        P(("row", "col"), "fib"),
        P(("row", "col"), "fib"),
        P("fib", None),
        P("row", "col", None, None, None),
        P("row", "col", None),
        P("row", "col", None),
        P("row", "col"),
    )
    out_specs = (P(("row", "col"), "fib"), P("fib", None))
    return jax.shard_map(
        on_device, mesh=mesh, in_specs=in_specs, out_specs=out_specs, check_vma=False
    )
```

time: 380 us -> 254 us (0.67)
  matrix products: 147 us -> 6.41 us
  waiting for transfers between devices: 143 us -> 192 us
  local copies, waits for them, and re-layouts: 43.3 us -> 11.3 us
  other arithmetic: 21.5 us -> 1.76 us
  blocking collectives: 10.4 us -> 22 us
  Pallas kernels: 0 us -> 5.12 us
    dot_general x34 -> x2, matrix products: 147 us -> 6.41 us  [the longest x1 4.29 us: on_device(): jnp.einsum('ifo,fton->tni', left, whole, preferred_element_type=jnp.float32)]
    all_gather x3 -> x2, waiting for transfers between devices: 55.3 us -> 86.9 us  [the longest x1 72 us: on_device(): whole = lax.all_gather(summed, 'fib', axis=0)]
    gather x16 -> x0, local copies, waits for them, and re-layouts: 29.8 us -> none  [the longest x8 23.9 us: group_products(): panels_all[block_cols]]
    all_gather x0 -> x1, blocking collectives: none -> 22 us  [on_device(): grad_weight = lax.all_gather(piece, ('row', 'col'), axis=0, tiled=True).T]
    reduce_scatter x1 -> x2, waiting for transfers between devices: 86.7 us -> 105 us  [the longest x1 54 us: on_device(): summed = lax.psum_scatter(partial_t, 'row', scatter_dimension=0, tiled=True)]
    while x2 -> x0, local copies, waits for them, and re-layouts: 12.1 us -> none  [tile_products(): lax.fori_loop(0, group_total(tile_block, slot_group), one_block, initial)]
    lt x16 -> x0, other arithmetic: 10.4 us -> none  [one_block(): valid = first + jnp.arange(slot_group, dtype=jnp.int32) < live_count]
    all_to_all x2 -> x0, blocking collectives: 10.4 us -> none  [the longest x1 5.66 us: summed_on_arrival(): pieces = lax.all_to_all(split_up(value, dim, peers), axis, 0, 0, tiled=True)]
  transfers between devices with their start and end apart: 4 -> 4, of which waited for: 2 -> 4; matrix products, arithmetic and copies ran while one was open for 54% -> 2% of each run, Pallas kernels for 0% -> 0%
where the time goes in v1:
time: 254 us; the launch traced here: 253 us
  waiting for transfers between devices  192 us (76%)
  blocking collectives  22 us (9%)
  between operations  14.5 us (6%)
  local copies, waits for them, and re-layouts  11.3 us (4%)
  matrix products  6.41 us (3%)
  Pallas kernels  5.12 us (2%)
    all_gather x1, waiting for transfers between devices, on_device(): whole = lax.all_gather(summed, 'fib', axis=0)  72 us
    reduce_scatter x1, waiting for transfers between devices, on_device(): summed = lax.psum_scatter(partial_t, 'row', scatter_dimension=0, tiled=True)  54 us
    reduce_scatter x1, waiting for transfers between devices, on_device(): lax.psum_scatter(part, ('row', 'col'), scatter_dimension=0, tiled=True)  51.2 us
    all_gather x1, blocking collectives, on_device(): grad_weight = lax.all_gather(piece, ('row', 'col'), axis=0, tiled=True).T  22 us
    all_gather x1, waiting for transfers between devices, on_device(): grad = lax.all_gather(grad, 'col', axis=0, tiled=True)  14.9 us
    unnamed x14, local copies, waits for them, and re-layouts  5.53 us
    pallas_call x1, Pallas kernels, tile_products(): pl.pallas_call(tile_kernel, out_shape=jax.ShapeDtypeStruct((out_tiles, wi...  5.12 us
  transfers between devices with their start and end apart: 4, of which 4 were waited for; matrix products, arithmetic and copies ran while one was open for 2% of the time, Pallas kernels for 0%

profile of v1, /device:TPU:1, one launch (start us, length us, event | category | flops | bytes accessed | tf_op | source)
XLA Modules:
  0.0 253.4 jit_solution(14165463108623610406)
XLA Ops:
  7.2 0.0 all-gather.4.cloned.1.call-start
  7.2 1.8 fusion.11
  9.0 1.0 copy.23
  10.0 0.0 all-gather.4.cloned.1.call-update
  10.0 0.0 reduce-scatter.3.cloned.1.call-start
  10.7 14.9 %all-gather.4.cloned.1.call-done.grad_ref = bf16[16,128,256]{2,1,0:T(8,128)(2,1)} async-done(((bf16[8,128,256]{2,1,0:T(8,128)(2,1)}), bf16[16,128,256]{2,1,0:T(8,128)(2,1)}) %all-gather.4.cloned.1.call-update) | async-done | bytes 1048592 | tf_op jit(solution)/shard_map/all_gather | solution.py:84
  25.7 1.2 copy-done.2
  26.9 0.7 copy-done.3
  27.5 0.7 copy-done.4
  28.2 5.1 %tile_products.1 = bf16[64,128,256]{2,1,0:T(8,128)(2,1)S(1)} custom-call(s32[1,1,128]{2,1,0:T(1,128)S(1)} %copy-done.3, s32[1,1,128]{2,1,0:T(1,128)S(1)} %copy-done.4, s32[1,1]{1,0:T(1,128)S(6)} %copy.40.count_ref, bf16[16,128,256]{2,1,0:T(8,128)(2,1)S(1)} %copy-done.2, bf16[128,256,256]{2,1,0:T(8,128)(2,1)} %bitcast.25), custom_call_target="tpu_custom_call" | custom-call | flops 2147483648 | bytes 16777216 | tf_op jit(solution)/shard_map/tile_products/pallas_call | solution.py:53
  33.3 1.9 copy-done.1
  35.3 0.0 reduce-scatter.3.cloned.1.call-update
  35.3 0.0 all-gather.6.cloned.1.call-start
  35.4 54.0 %reduce-scatter.3.cloned.1.call-done = bf16[8,128,256]{2,1,0:T(8,128)(2,1)} async-done(((bf16[64,128,256]{2,1,0:T(8,128)(2,1)}), bf16[8,128,256]{2,1,0:T(8,128)(2,1)}) %reduce-scatter.3.cloned.1.call-update) | async-done | bytes 524304 | tf_op jit(solution)/shard_map/reduce_scatter | solution.py:88
  89.3 0.0 all-gather.6.cloned.1.call-update
  89.4 0.0 reduce-scatter.5.cloned.1.call-start
  89.4 72.0 %all-gather.6.cloned.1.call-done = bf16[64,128,256]{2,1,0:T(8,128)(2,1)} async-done(((bf16[8,128,256]{2,1,0:T(8,128)(2,1)}), bf16[64,128,256]{2,1,0:T(8,128)(2,1)}) %all-gather.6.cloned.1.call-update) | async-done | bytes 4194320 | tf_op jit(solution)/shard_map/all_gather | solution.py:89
  161.4 4.7 %copy.26 = bf16[8,128,256,8]{2,3,1,0:T(8,128)(2,1)S(1)} copy(bf16[8,128,256,8]{2,1,3,0:T(8,128)(2,1)} %bitcast.26) | data formatting | bytes 8388608 | tf_op jit(solution)/shard_map/fton,tni->foi/dot_general | solution.py:93
  166.2 2.1 fusion.3
  168.3 0.0 reduce-scatter.5.cloned.1.call-update
  168.4 4.3 %fusion.2 = bf16[8,256,128]{2,1,0:T(8,128)(2,1)} fusion(bf16[8,8,128,256]{3,2,1,0:T(8,128)(2,1)} %bitcast.27, bf16[128,8,128,1]{2,1,0,3:T(8,128)(2,1)S(1)} %bitcast.32), kind=kOutput, calls=%fused_computation.5 | convolution fusion | flops 537133056 | bytes 4980736 | tf_op jit(solution)/shard_map/ifo,fton->tni/dot_general | solution.py:91
  172.7 51.2 %reduce-scatter.5.cloned.1.call-done = f32[64,128]{1,0:T(8,128)} async-done(((f32[1024,128]{1,0:T(8,128)}), f32[64,128]{1,0:T(8,128)}) %reduce-scatter.5.cloned.1.call-update) | async-done | bytes 32784 | tf_op jit(solution)/shard_map/reduce_scatter | solution.py:100
  223.8 22.0 %all_gather.15 = f32[1024,128]{1,0:T(8,128)S(1)} all-gather(f32[64,128]{1,0:T(8,128)} %reduce-scatter.5.cloned.1.call-done), channel_id=1, replica_groups=mesh['row'=8,'col'=2,'fib'=8] {'row','col'}, dimensions={0}, use_global_device_ids=true | all-gather | bytes 557056 | tf_op jit(solution)/shard_map/all_gather | solution.py:101
  245.9 1.0 copy.28
  (9 shorter events, 0.1 us)
Async XLA Ops:
  7.2 159.0 %copy-start = (bf16[2048,128]{1,0:T(8,128)(2,1)S(1)}, bf16[2048,128]{1,0:T(8,128)(2,1)}, u32[]{:S(2)}) copy-start(bf16[2048,128]{1,0:T(8,128)(2,1)} %param.8) | copy-start | bytes 1572868
  7.2 18.5 %all-gather.4.cloned.1.call-start = ((), (), s32[]{:S(2)}) async-start(), calls=%async_computation.2 | async-start | bytes 1572864 | tf_op jit(solution)/shard_map/all_gather | solution.py:84
  10.0 79.3 %reduce-scatter.3.cloned.1.call-start = ((), (), s32[]{:S(2)}) async-start(), calls=%async_computation.3 | async-start | bytes 4718592 | tf_op jit(solution)/shard_map/reduce_scatter | solution.py:88
  25.7 1.2 copy-start.2
  26.9 0.7 copy-start.3
  27.5 0.7 copy-start.4
  33.3 2.0 copy-start.1
  35.3 126.1 %all-gather.6.cloned.1.call-start = ((), (), s32[]{:S(2)}) async-start(), calls=%async_computation.5 | async-start | bytes 4718592 | tf_op jit(solution)/shard_map/all_gather | solution.py:89
  89.4 134.5 %reduce-scatter.5.cloned.1.call-start = ((), (), s32[]{:S(2)}) async-start(), calls=%async_computation.4 | async-start | bytes 557056 | tf_op jit(solution)/shard_map/reduce_scatter | solution.py:100
  166.2 2.2 copy-start.5
Sparse Core Ops, SparseCore 0:
  10.2 15.3 all-gather.3
  35.4 53.8 reduce-scatter.2
  91.7 69.6 all-gather.5
  168.5 55.3 reduce-scatter.4

commit v2 on v1

--- a/solution.py
+++ b/solution.py
@@ -1,3 +1,5 @@
+import functools
+
 import jax
 import jax.numpy as jnp
 from jax import lax
@@ -6,6 +8,74 @@
 from jax.sharding import PartitionSpec as P
 
 GROUP = 8
+RING = 4
+MESH = pl.DeviceIdType.MESH
+SMEM = pl.BlockSpec(memory_space=pltpu.SMEM)
+VMEM = pl.BlockSpec(memory_space=pltpu.VMEM)
+
+
+def greet(peers):
+    barrier = pltpu.get_barrier_semaphore()
+    for peer in peers:
+        pl.semaphore_signal(barrier, inc=1, device_id=peer, device_id_type=MESH)
+    pl.semaphore_wait(barrier, len(peers))
+
+
+def position():
+    return lax.axis_index("row"), lax.axis_index("col"), lax.axis_index("fib")
+
+
+def grad_kernel(pre_ref, out_grad_ref, grad_ref, send_sems, recv_sems):
+    row, col, fib = position()
+    own_tiles = grad_ref.shape[0] // 2
+    tile = grad_ref.shape[2]
+    partner = (row, 1 - col, fib)
+    greet([partner])
+
+    def copy(t):
+        slot = grad_ref.at[col * own_tiles + t]
+        return pltpu.make_async_remote_copy(
+            slot, slot, send_sems.at[t], recv_sems.at[t], device_id=partner, device_id_type=MESH
+        )
+
+    @pl.loop(0, own_tiles)
+    def _(t):
+        part = pl.ds(pl.multiple_of(t * tile, tile), tile)
+        pre = pre_ref[part, :].astype(jnp.float32)
+        sigmoid = jax.nn.sigmoid(pre)
+        grad = out_grad_ref[part, :].astype(jnp.float32) * sigmoid * (1.0 + pre * (1.0 - sigmoid))
+        grad_ref[col * own_tiles + t] = grad.T.astype(grad_ref.dtype)
+        copy(t).start()
+
+    def arrived(t):
+        slot = grad_ref.at[(1 - col) * own_tiles + t]
+        return pltpu.make_async_remote_copy(
+            slot, slot, send_sems.at[t], recv_sems.at[t], device_id=partner, device_id_type=MESH
+        )
+
+    @pl.loop(0, own_tiles)
+    def _(t):
+        copy(t).wait_send()
+        arrived(t).wait_recv()
+
+
+def local_grads(pre, out_grad, tile):
+    nodes, width = pre.shape
+    own_tiles = nodes // tile
+    return pl.pallas_call(
+        grad_kernel,
+        out_shape=jax.ShapeDtypeStruct((2 * own_tiles, width, tile), jnp.bfloat16),
+        in_specs=[VMEM, VMEM],
+        out_specs=VMEM,
+        scratch_shapes=[pltpu.SemaphoreType.DMA((own_tiles,))] * 2,
+        compiler_params=pltpu.CompilerParams(
+            collective_id=0, has_side_effects=True, vmem_limit_bytes=16 << 20
+        ),
+        cost_estimate=pl.CostEstimate(
+            flops=10 * nodes * width, bytes_accessed=8 * nodes * width, transcendentals=nodes * width
+        ),
+        name="local_grads",
+    )(pre, out_grad)
 
 
 def tile_kernel(rows_ref, cols_ref, count_ref, grad_ref, tiles_ref, out_ref, held, total, sems):
@@ -48,13 +118,11 @@
 def tile_products(rows, cols, count, grad, tiles, out_tiles):
     slots, tile, _ = tiles.shape
     width = grad.shape[1]
-    smem = pl.BlockSpec(memory_space=pltpu.SMEM)
-    vmem = pl.BlockSpec(memory_space=pltpu.VMEM)
     return pl.pallas_call(
         tile_kernel,
         out_shape=jax.ShapeDtypeStruct((out_tiles, width, tile), jnp.bfloat16),
-        in_specs=[smem, smem, smem, vmem, pl.BlockSpec(memory_space=pl.ANY)],
-        out_specs=vmem,
+        in_specs=[SMEM, SMEM, SMEM, VMEM, pl.BlockSpec(memory_space=pl.ANY)],
+        out_specs=VMEM,
         scratch_shapes=[
             pltpu.VMEM((slots, tile, tile), jnp.bfloat16),
             pltpu.VMEM((out_tiles + 1, width, tile), jnp.float32),
@@ -70,35 +138,263 @@
     )(rows, cols, count, grad, tiles)
 
 
+def flow_kernel(
+    part_ref, weight_ref, feat_ref, gf_ref, gw_ref,
+    first, second, merged, half, pair_in, total, whole, send_sems, recv_sems,
+):
+    row, col, fib = position()
+    l, z = row // RING, lax.rem(row, RING)
+    h, x = fib // RING, lax.rem(fib, RING)
+    chunks, tile = part_ref.shape[2], part_ref.shape[4]
+    z_up, z_down, z_far = (lax.rem(z + d, RING) for d in (1, RING - 1, 2))
+    x_up, x_down, x_far = (lax.rem(x + d, RING) for d in (1, RING - 1, 2))
+    to_z_up, to_z_down = (l * RING + z_up, col, fib), (l * RING + z_down, col, fib)
+    to_x_up, to_x_down = (row, col, h * RING + x_up), (row, col, h * RING + x_down)
+    to_pair = ((1 - l) * RING + z, col, fib)
+    to_cross = ((1 - l) * RING + z, col, (1 - h) * RING + x)
+    greet([to_z_up, to_z_down, to_x_up, to_x_down, to_pair, to_cross])
+
+    def copy(kind, t, source, target, peer):
+        return pltpu.make_async_remote_copy(
+            source,
+            target,
+            send_sems.at[kind, t],
+            recv_sems.at[kind, t],
+            device_id=peer,
+            device_id_type=MESH,
+        )
+
+    def link(kind, t):
+        if kind == 0:
+            return copy(0, t, part_ref.at[0, z_far, t], first.at[0, t], to_z_up)
+        if kind == 1:
+            return copy(1, t, part_ref.at[1, z_far, t], first.at[1, t], to_z_down)
+        if kind == 2:
+            return copy(2, t, part_ref.at[1, z_up, t], second.at[0, t, 1], to_z_up)
+        if kind == 3:
+            return copy(3, t, part_ref.at[0, z_down, t], second.at[1, t, 0], to_z_down)
+        if kind == 4:
+            return copy(4, t, merged.at[0, t], second.at[0, t, 0], to_z_up)
+        if kind == 5:
+            return copy(5, t, merged.at[1, t], second.at[1, t, 1], to_z_down)
+        if kind == 6:
+            return copy(6, t, half.at[t], pair_in.at[t], to_pair)
+        if kind == 7:
+            return copy(7, t, total.at[t], whole.at[t, x, h], to_pair)
+        if kind == 8:
+            return copy(8, t, total.at[t], whole.at[t, x, h], to_cross)
+        if kind == 9:
+            return copy(9, t, whole.at[t, x], whole.at[t, x], to_x_up)
+        if kind == 10:
+            return copy(10, t, whole.at[t, x], whole.at[t, x], to_x_down)
+        if kind == 11:
+            return copy(11, t, whole.at[t, x_down, 0], whole.at[t, x_down, 0], to_x_up)
+        return copy(12, t, whole.at[t, x_up, 1], whole.at[t, x_up, 1], to_x_down)
+
+    def arrived(kind, t):
+        if kind == 7:
+            slot = whole.at[t, x, h]
+        elif kind == 8:
+            slot = whole.at[t, x, 1 - h]
+        elif kind == 9:
+            slot = whole.at[t, x_down]
+        elif kind == 10:
+            slot = whole.at[t, x_up]
+        elif kind == 11:
+            slot = whole.at[t, x_far, 0]
+        elif kind == 12:
+            slot = whole.at[t, x_far, 1]
+        else:
+            link(kind, t).wait_recv()
+            return
+        copy(kind, t, slot, slot, to_pair).wait_recv()
+
+    def added(*refs):
+        terms = [r[...].astype(jnp.float32) for r in refs]
+        return functools.reduce(lambda a, b: a + b, terms)
+
+    gw_ref[...] = jnp.zeros_like(gw_ref)
+
+    def send_shares(t):
+        for kind in range(4):
+            link(kind, t).start()
+
+    def merge(t):
+        arrived(0, t)
+        merged[0, t] = added(part_ref.at[0, z_up, t], first.at[0, t]).astype(merged.dtype)
+        link(4, t).start()
+        arrived(1, t)
+        merged[1, t] = added(part_ref.at[1, z_down, t], first.at[1, t]).astype(merged.dtype)
+        link(5, t).start()
+
+    def sum_over_z(t):
+        for kind in (2, 3, 4, 5):
+            arrived(kind, t)
+        half[t] = added(part_ref.at[l, z, t], second.at[0, t, l], second.at[1, t, l]).astype(half.dtype)
+        link(6, t).start()
+
+    def sum_over_y(t):
+        o = 1 - l
+        arrived(6, t)
+        total[t] = added(
+            part_ref.at[o, z, t], second.at[0, t, o], second.at[1, t, o], pair_in.at[t]
+        ).astype(total.dtype)
+        link(7, t).start()
+        link(8, t).start()
+
+    def spread(t):
+        arrived(7, t)
+        arrived(8, t)
+        link(9, t).start()
+        link(10, t).start()
+
+    def forward(t):
+        arrived(9, t)
+        link(11, t).start()
+        arrived(10, t)
+        link(12, t).start()
+
+    def multiply(t):
+        arrived(11, t)
+        arrived(12, t)
+        panel = whole[t].reshape(weight_ref.shape[1], tile)
+        part = pl.ds(pl.multiple_of(t * tile, tile), tile)
+        product = jnp.dot(weight_ref[...], panel, preferred_element_type=jnp.float32)
+        gf_ref[part, :] = product.T.astype(gf_ref.dtype)
+        gw_ref[...] += jnp.dot(panel, feat_ref[part, :], preferred_element_type=jnp.float32)
+
+    stages = (send_shares, merge, sum_over_z, sum_over_y, spread, forward, multiply)
+
+    @pl.loop(0, chunks + len(stages) - 1)
+    def _(step):
+        for late, stage in enumerate(stages):
+            t = step - late
+
+            @pl.when((t >= 0) & (t < chunks))
+            def _(stage=stage, t=t):
+                stage(t)
+
+    @pl.loop(0, chunks)
+    def _(t):
+        for kind in range(13):
+            link(kind, t).wait_send()
+
+
+def flow(part, weight, features):
+    _, _, chunks, width, tile = part.shape
+    nodes, whole = features.shape[0], weight.shape[1]
+    piece = (width, tile)
+    sixteen = jnp.bfloat16
+    return pl.pallas_call(
+        flow_kernel,
+        out_shape=(
+            jax.ShapeDtypeStruct((nodes, width), sixteen),
+            jax.ShapeDtypeStruct((whole, width), jnp.float32),
+        ),
+        in_specs=[VMEM] * 3,
+        out_specs=(VMEM, VMEM),
+        scratch_shapes=[
+            pltpu.VMEM((2, chunks, *piece), sixteen),
+            pltpu.VMEM((2, chunks, 2, *piece), sixteen),
+            pltpu.VMEM((2, chunks, *piece), sixteen),
+            pltpu.VMEM((chunks, *piece), sixteen),
+            pltpu.VMEM((chunks, *piece), sixteen),
+            pltpu.VMEM((chunks, *piece), sixteen),
+            pltpu.VMEM((chunks, RING, 2, *piece), sixteen),
+            pltpu.SemaphoreType.DMA((13, chunks)),
+            pltpu.SemaphoreType.DMA((13, chunks)),
+        ],
+        compiler_params=pltpu.CompilerParams(
+            collective_id=1, has_side_effects=True, vmem_limit_bytes=40 << 20
+        ),
+        cost_estimate=pl.CostEstimate(
+            flops=4 * nodes * width * whole, bytes_accessed=16 << 20, transcendentals=0
+        ),
+        name="flow",
+    )(part, weight, features)
+
+
+def weight_kernel(part_ref, out_ref, mate_in, mine, row_in, sems):
+    row, col, fib = position()
+    rows = out_ref.shape[0] // 16
+    span = 8 * rows
+    mate = (row, 1 - col, fib)
+    peers = [(lax.rem(row + d, 8), col, fib) for d in range(1, 8)]
+    greet([mate, *peers])
+
+    def copy(kind, d, source, target, peer):
+        return pltpu.make_async_remote_copy(
+            source, target, sems.at[0, kind, d], sems.at[1, kind, d], device_id=peer, device_id_type=MESH
+        )
+
+    def at(ref, start, size):
+        return ref.at[pl.ds(pl.multiple_of(start, rows), size)]
+
+    swap = copy(0, 0, at(part_ref, (1 - col) * span, span), mate_in, mate)
+    swap.start()
+    swap.wait()
+    mine[...] = part_ref[pl.ds(pl.multiple_of(col * span, span), span), :] + mate_in[...]
+    sends = []
+    for d in range(1, 8):
+        to = lax.rem(row + d, 8)
+        sends.append(copy(1, d, at(mine, to * rows, rows), row_in.at[d], peers[d - 1]))
+        sends[-1].start()
+    own = mine[pl.ds(pl.multiple_of(row * rows, rows), rows), :]
+    for s, d in zip(sends, range(1, 8)):
+        s.wait_recv()
+        own += row_in[d]
+    here = col * span + row * rows
+    out_ref[pl.ds(pl.multiple_of(here, rows), rows), :] = own
+    gives = []
+    for d in range(1, 8):
+        piece = at(out_ref, here, rows)
+        gives.append(copy(2, d, piece, piece, peers[d - 1]))
+        gives[-1].start()
+    for d in range(1, 8):
+        slot = at(out_ref, col * span + lax.rem(row + 8 - d, 8) * rows, rows)
+        copy(2, d, slot, slot, peers[d - 1]).wait_recv()
+    final = at(out_ref, col * span, span)
+    last = copy(0, 1, final, final, mate)
+    last.start()
+    for s in (*sends, *gives):
+        s.wait_send()
+    last.wait_send()
+    slot = at(out_ref, (1 - col) * span, span)
+    copy(0, 1, slot, slot, mate).wait_recv()
+
+
+def weight_sum(part):
+    depth, width = part.shape
+    return pl.pallas_call(
+        weight_kernel,
+        out_shape=jax.ShapeDtypeStruct(part.shape, part.dtype),
+        in_specs=[VMEM],
+        out_specs=VMEM,
+        scratch_shapes=[
+            pltpu.VMEM((depth // 2, width), part.dtype),
+            pltpu.VMEM((depth // 2, width), part.dtype),
+            pltpu.VMEM((8, depth // 16, width), part.dtype),
+            pltpu.SemaphoreType.DMA((2, 3, 8)),
+        ],
+        compiler_params=pltpu.CompilerParams(
+            collective_id=2, has_side_effects=True, vmem_limit_bytes=16 << 20
+        ),
+        cost_estimate=pl.CostEstimate(flops=1 << 20, bytes_accessed=2 << 20, transcendentals=0),
+        name="weight_sum",
+    )(part)
+
+
 def on_device(features, pre_activation, out_grad, weight, tiles, rows, cols, counts):
     nodes, width = features.shape
     tile = tiles.shape[-1]
-    fib = lax.axis_size("fib")
     own_tiles = nodes // tile
-    pre = pre_activation.astype(jnp.float32)
-    sigmoid = jax.nn.sigmoid(pre)
-    grad = (out_grad.astype(jnp.float32) * sigmoid * (1.0 + pre * (1.0 - sigmoid))).astype(
-        jnp.bfloat16
-    )
-    grad = grad.reshape(own_tiles, tile, width).transpose(0, 2, 1)
-    grad = lax.all_gather(grad, "col", axis=0, tiled=True)
-    partial_t = tile_products(
-        rows, cols, counts, grad, tiles[0, 0], own_tiles * lax.axis_size("row")
-    )
-    summed = lax.psum_scatter(partial_t, "row", scatter_dimension=0, tiled=True)
-    whole = lax.all_gather(summed, "fib", axis=0)
-    left = weight.reshape(width, fib, width)
-    grad_features = jnp.einsum("ifo,fton->tni", left, whole, preferred_element_type=jnp.float32)
-    grad_features = grad_features.astype(jnp.bfloat16).reshape(nodes, width)
-    part = jnp.einsum(
-        "fton,tni->foi",
-        whole,
-        features.reshape(own_tiles, tile, width),
-        preferred_element_type=jnp.float32,
-    )
-    part = part.reshape(fib * width, width)
-    piece = lax.psum_scatter(part, ("row", "col"), scatter_dimension=0, tiled=True)
-    grad_weight = lax.all_gather(piece, ("row", "col"), axis=0, tiled=True).T
+    grad = local_grads(pre_activation, out_grad, tile)
+    part = tile_products(rows, cols, counts, grad, tiles[0, 0], 8 * own_tiles)
+    part = part.reshape(2, RING, own_tiles, width, tile)
+    mixed = weight.reshape(width, 2, RING, width).transpose(0, 2, 1, 3).reshape(width, -1)
+    grad_features, share = flow(part, mixed, features)
+    total = weight_sum(share)
+    grad_weight = total.reshape(RING, 2, width, width).transpose(3, 1, 0, 2).reshape(width, -1)
     return grad_features, grad_weight
 
 

time: 254 us -> 104 us (0.41)
  waiting for transfers between devices: 192 us -> 0 us
  Pallas kernels: 5.12 us -> 91.8 us
  blocking collectives: 22 us -> 0 us
  between operations: 14.5 us -> 1.38 us
  matrix products: 6.41 us -> 0 us
    reduce_scatter x2 -> x0, waiting for transfers between devices: 105 us -> none  [the longest x1 54 us: on_device(): summed = lax.psum_scatter(partial_t, 'row', scatter_dimension=0, tiled=True)]
    pallas_call x0 -> x3, Pallas kernels: none -> 88.3 us  [the longest x1 66.6 us: flow(): pl.pallas_call(flow_kernel, out_shape=(jax.ShapeDtypeStruct((nodes, width...]
    all_gather x2 -> x0, waiting for transfers between devices: 86.9 us -> none  [the longest x1 72 us: on_device(): whole = lax.all_gather(summed, 'fib', axis=0)]
    all_gather x1 -> x0, blocking collectives: 22 us -> none  [on_device(): grad_weight = lax.all_gather(piece, ('row', 'col'), axis=0, tiled=True).T]
    dot_general x2 -> x0, matrix products: 6.41 us -> none  [the longest x1 4.29 us: on_device(): jnp.einsum('ifo,fton->tni', left, whole, preferred_element_type=jnp.float32)]
    dot_general x1 -> x0, local copies, waits for them, and re-layouts: 4.75 us -> none  [on_device(): jnp.einsum('fton,tni->foi', whole, features.reshape(own_tiles, tile, widt...]
    unnamed x14 -> x17, local copies, waits for them, and re-layouts: 5.53 us -> 8.29 us
  transfers between devices with their start and end apart: 4 -> 0, of which waited for: 4 -> 0; matrix products, arithmetic and copies ran while one was open for 2% -> 0% of each run, Pallas kernels for 0% -> 0%
where the time goes in v2:
time: 104 us; the launch traced here: 103 us
  Pallas kernels  91.8 us (88%)
  local copies, waits for them, and re-layouts  10.1 us (10%)
  between operations  1.38 us (1%)
    pallas_call x1, Pallas kernels, flow(): pl.pallas_call(flow_kernel, out_shape=(jax.ShapeDtypeStruct((nodes, width...  66.6 us
    pallas_call x1, Pallas kernels, weight_sum(): pl.pallas_call(weight_kernel, out_shape=jax.ShapeDtypeStruct(part.shape,...  18.2 us
    unnamed x17, local copies, waits for them, and re-layouts  8.29 us
    pallas_call x1, Pallas kernels, tile_products(): pl.pallas_call(tile_kernel, out_shape=jax.ShapeDtypeStruct((out_tiles, wi...  3.53 us
    pallas_call x1, Pallas kernels, local_grads(): pl.pallas_call(grad_kernel, out_shape=jax.ShapeDtypeStruct((2 * own_tiles...  3.44 us

profile of v2, /device:TPU:1, one launch (start us, length us, event | category | flops | bytes accessed | tf_op | source)
XLA Modules:
  0.0 103.3 jit_solution(11609915227250382698)
XLA Ops:
  0.6 0.0 copy-start.3
  0.6 1.0 copy-done.3
  1.7 0.0 copy-start.4
  1.7 1.0 %copy-done.4 = bf16[2048,128]{1,0:T(8,128)(2,1)S(1)} copy-done((bf16[2048,128]{1,0:T(8,128)(2,1)S(1)}, bf16[2048,128]{1,0:T(8,128)(2,1)}, u32[]{:S(2)}) %copy-start.4) | copy-done | bytes 524312
  2.7 0.0 copy-start.7
  2.7 3.4 %local_grads.1.grad_ref = bf16[16,128,256]{2,1,0:T(8,128)(2,1)S(1)} custom-call(bf16[2048,128]{1,0:T(8,128)(2,1)S(1)} %copy-done.3, bf16[2048,128]{1,0:T(8,128)(2,1)S(1)} %copy-done.4), custom_call_target="tpu_custom_call" | custom-call | flops 2621440 | bytes 2097152 | tf_op jit(solution)/shard_map/local_grads/pallas_call | solution.py:65
  6.8 0.0 copy-start.5
  6.8 0.6 copy-done.5
  7.5 0.7 copy-done.6
  8.1 3.5 %tile_products.1 = bf16[64,128,256]{2,1,0:T(8,128)(2,1)S(1)} custom-call(s32[1,1,128]{2,1,0:T(1,128)S(1)} %copy-done.5, s32[1,1,128]{2,1,0:T(1,128)S(1)} %copy-done.6, s32[1,1]{1,0:T(1,128)S(6)} %copy.15.count_ref, bf16[16,128,256]{2,1,0:T(8,128)(2,1)S(1)} %local_grads.1.grad_ref, bf16[128,256,256]{2,1,0:T(8,128)(2,1)} %bitcast.10), custom_call_target="tpu_custom_call" | custom-call | flops 2147483648 | bytes 16777216 | tf_op jit(solution)/shard_map/tile_products/pallas_call | solution.py:121
  11.7 0.0 copy-start
  11.7 1.9 %copy-done = bf16[64,128,256]{2,1,0:T(8,128)(2,1)} copy-done((bf16[64,128,256]{2,1,0:T(8,128)(2,1)}, bf16[64,128,256]{2,1,0:T(8,128)(2,1)S(1)}, u32[]{:S(2)}) %copy-start) | copy-done | bytes 4194328
  13.6 0.0 copy-done.7
  13.6 0.2 reshape.20
  13.8 0.2 copy.13
  14.0 0.2 reshape.21.weight_ref
  14.2 0.0 copy-done.2
  14.2 0.0 copy-start.1
  14.2 2.2 %copy-done.1 = bf16[64,128,256]{2,1,0:T(8,128)(2,1)S(1)} copy-done((bf16[64,128,256]{2,1,0:T(8,128)(2,1)S(1)}, bf16[64,128,256]{2,1,0:T(8,128)(2,1)}, u32[]{:S(2)}) %copy-start.1) | copy-done | bytes 4194328
  16.4 66.6 %flow.1 = (bf16[2048,128]{1,0:T(8,128)(2,1)S(1)}, f32[1024,128]{1,0:T(8,128)S(1)}) custom-call(bf16[2,4,8,128,256]{4,3,2,1,0:T(8,128)(2,1)S(1)} %bitcast.8, bf16[128,1024]{1,0:T(8,128)(2,1)S(1)} %reshape.21.weight_ref, bf16[2048,128]{1,0:T(8,128)(2,1)S(1)} %copy-done.2), custom_call_target="tpu_custom_call" | custom-call | flops 1073741824 | bytes 16777216 | tf_op jit(solution)/shard_map/flow/pallas_call | solution.py:288
  83.0 18.2 %weight_sum.1 = f32[1024,128]{1,0:T(8,128)S(1)} custom-call(f32[1024,128]{1,0:T(8,128)S(1)} %get-tuple-element.5.part_ref), custom_call_target="tpu_custom_call" | custom-call | flops 1048576 | bytes 2097152 | tf_op jit(solution)/shard_map/weight_sum/pallas_call | solution.py:368
  101.2 0.3 copy.11
  101.5 1.0 reshape.23
  102.5 0.8 copy.16
  (2 shorter events, 0.0 us)
Async XLA Ops:
  0.6 1.0 %copy-start.3 = (bf16[2048,128]{1,0:T(8,128)(2,1)S(1)}, bf16[2048,128]{1,0:T(8,128)(2,1)}, u32[]{:S(2)}) copy-start(bf16[2048,128]{1,0:T(8,128)(2,1)} %pre_ref.1) | copy-start | bytes 1572868
  1.7 1.0 %copy-start.4 = (bf16[2048,128]{1,0:T(8,128)(2,1)S(1)}, bf16[2048,128]{1,0:T(8,128)(2,1)}, u32[]{:S(2)}) copy-start(bf16[2048,128]{1,0:T(8,128)(2,1)} %out_grad_ref.1) | copy-start | bytes 1572868
  2.7 10.9 %copy-start.7 = (bf16[128,1024]{1,0:T(8,128)(2,1)S(1)}, bf16[128,1024]{1,0:T(8,128)(2,1)}, u32[]{:S(2)}) copy-start(bf16[128,1024]{1,0:T(8,128)(2,1)} %param.11) | copy-start | bytes 786436
  2.7 11.5 %copy-start.2 = (bf16[2048,128]{1,0:T(8,128)(2,1)S(1)}, bf16[2048,128]{1,0:T(8,128)(2,1)}, u32[]{:S(2)}) copy-start(bf16[2048,128]{1,0:T(8,128)(2,1)} %feat_ref.1) | copy-start | bytes 1572868
  6.8 0.7 copy-start.5
  7.5 0.7 copy-start.6
  11.7 1.9 %copy-start = (bf16[64,128,256]{2,1,0:T(8,128)(2,1)}, bf16[64,128,256]{2,1,0:T(8,128)(2,1)S(1)}, u32[]{:S(2)}) copy-start(bf16[64,128,256]{2,1,0:T(8,128)(2,1)S(1)} %tile_products.1) | copy-start | bytes 12582916
  14.2 2.2 %copy-start.1 = (bf16[64,128,256]{2,1,0:T(8,128)(2,1)S(1)}, bf16[64,128,256]{2,1,0:T(8,128)(2,1)}, u32[]{:S(2)}) copy-start(bf16[64,128,256]{2,1,0:T(8,128)(2,1)} %copy-done) | copy-start | bytes 12582916

commit v3 on v2

v3 whole, which is shorter than its diff:
```python
import functools

import jax
import jax.numpy as jnp
from jax import lax
from jax.experimental import pallas as pl
from jax.experimental.pallas import tpu as pltpu
from jax.sharding import PartitionSpec as P

GROUP = 8
RING = 4
LAGS = (0, 1, 2, 3, 4, 5, 6)
MESH = pl.DeviceIdType.MESH
VMEM = pl.BlockSpec(memory_space=pltpu.VMEM)
ANY = pl.BlockSpec(memory_space=pl.ANY)
CHUNK = 128


def greet(peers):
    barrier = pltpu.get_barrier_semaphore()
    for peer in peers:
        pl.semaphore_signal(barrier, inc=1, device_id=peer, device_id_type=MESH)
    pl.semaphore_wait(barrier, len(peers))


def position():
    return lax.axis_index("row"), lax.axis_index("col"), lax.axis_index("fib")


def grad_kernel(
    pre_hbm, out_grad_hbm, grad_ref, pre_ref, out_grad_ref, load_sems, send_sems, recv_sems
):
    row, col, fib = position()
    own_tiles = grad_ref.shape[0] // 2
    tile = grad_ref.shape[2]
    partner = (row, 1 - col, fib)

    def loads(t):
        part = pl.ds(pl.multiple_of(t * tile, tile), tile)
        return (
            pltpu.make_async_copy(pre_hbm.at[part], pre_ref.at[part], load_sems.at[0, t]),
            pltpu.make_async_copy(out_grad_hbm.at[part], out_grad_ref.at[part], load_sems.at[1, t]),
        )

    @pl.loop(0, own_tiles)
    def _(t):
        for load in loads(t):
            load.start()

    greet([partner])

    def copy(t, owner):
        slot = grad_ref.at[owner * own_tiles + t]
        return pltpu.make_async_remote_copy(
            slot, slot, send_sems.at[t], recv_sems.at[t], device_id=partner, device_id_type=MESH
        )

    @pl.loop(0, own_tiles)
    def _(t):
        for load in loads(t):
            load.wait()
        part = pl.ds(pl.multiple_of(t * tile, tile), tile)
        pre = pre_ref[part, :].astype(jnp.float32)
        sigmoid = jax.nn.sigmoid(pre)
        grad = out_grad_ref[part, :].astype(jnp.float32) * sigmoid * (1.0 + pre * (1.0 - sigmoid))
        grad_ref[col * own_tiles + t] = grad.T.astype(grad_ref.dtype)
        copy(t, col).start()

    @pl.loop(0, own_tiles)
    def _(t):
        copy(t, col).wait_send()
        copy(t, 1 - col).wait_recv()


def local_grads(pre, out_grad, tile):
    nodes, width = pre.shape
    own_tiles = nodes // tile
    return pl.pallas_call(
        grad_kernel,
        out_shape=jax.ShapeDtypeStruct((2 * own_tiles, width, tile), jnp.bfloat16),
        in_specs=[ANY, ANY],
        out_specs=VMEM,
        scratch_shapes=[
            pltpu.VMEM(pre.shape, pre.dtype),
            pltpu.VMEM(pre.shape, pre.dtype),
            pltpu.SemaphoreType.DMA((2, own_tiles)),
            pltpu.SemaphoreType.DMA((own_tiles,)),
            pltpu.SemaphoreType.DMA((own_tiles,)),
        ],
        compiler_params=pltpu.CompilerParams(
            collective_id=0, has_side_effects=True, vmem_limit_bytes=8 << 20
        ),
        cost_estimate=pl.CostEstimate(
            flops=10 * nodes * width, bytes_accessed=8 * nodes * width, transcendentals=nodes * width
        ),
        name="local_grads",
    )(pre, out_grad)


def tile_kernel(
    rows_hbm, cols_hbm, count_hbm, grad_ref, tiles_ref, out_ref,
    held, total, rows_ref, cols_ref, count_ref, sems, index_sems,
):
    slots, tile, _ = tiles_ref.shape
    cuts = tile // CHUNK
    out_tiles = out_ref.shape[0] // cuts
    row_tiles = grad_ref.shape[0]
    def copy(g):
        part = pl.ds(g * GROUP, GROUP)
        return pltpu.make_async_copy(tiles_ref.at[part], held.at[part], sems.at[g])

    indices = [
        pltpu.make_async_copy(source, target, index_sems.at[i])
        for i, (source, target) in enumerate(
            ((count_hbm, count_ref), (rows_hbm, rows_ref), (cols_hbm, cols_ref))
        )
    ]
    for load in indices:
        load.start()
    copy(0).start()
    indices[0].wait()
    count = jnp.clip(count_ref[0, 0], 1, slots)
    used = (count + GROUP - 1) // GROUP

    @pl.loop(1, used)
    def _(g):
        copy(g).start()

    @pl.loop(0, out_tiles + 1)
    def _(t):
        total[t] = jnp.zeros(total.shape[1:], total.dtype)

    for load in indices[1:]:
        load.wait()

    @pl.loop(0, used)
    def _(g):
        copy(g).wait()
        for j in range(GROUP):
            slot = g * GROUP + j
            row = jnp.clip(rows_ref[0, 0, slot], 0, row_tiles - 1)
            col = jnp.clip(cols_ref[0, 0, slot], 0, out_tiles - 1)
            target = jnp.where(slot < count, col, out_tiles)
            total[target] += jnp.dot(
                grad_ref[row], held[slot], preferred_element_type=jnp.float32
            )

    @pl.loop(0, out_tiles)
    def _(t):
        for cut in range(cuts):
            out_ref[t * cuts + cut] = total[t, :, cut * CHUNK : (cut + 1) * CHUNK].astype(out_ref.dtype)


def tile_products(rows, cols, count, grad, tiles, out_tiles):
    slots, tile, _ = tiles.shape
    width = grad.shape[1]
    return pl.pallas_call(
        tile_kernel,
        out_shape=jax.ShapeDtypeStruct((out_tiles * tile // CHUNK, width, CHUNK), jnp.bfloat16),
        in_specs=[ANY, ANY, ANY, VMEM, ANY],
        out_specs=VMEM,
        scratch_shapes=[
            pltpu.VMEM((slots, tile, tile), jnp.bfloat16),
            pltpu.VMEM((out_tiles + 1, width, tile), jnp.float32),
            pltpu.SMEM(rows.shape, rows.dtype),
            pltpu.SMEM(cols.shape, cols.dtype),
            pltpu.SMEM(count.shape, count.dtype),
            pltpu.SemaphoreType.DMA((slots // GROUP,)),
            pltpu.SemaphoreType.DMA((3,)),
        ],
        compiler_params=pltpu.CompilerParams(vmem_limit_bytes=28 << 20),
        cost_estimate=pl.CostEstimate(
            flops=2 * slots * width * tile * tile,
            bytes_accessed=2 * slots * tile * tile,
            transcendentals=0,
        ),
        name="tile_products",
    )(rows, cols, count, grad, tiles)


def flow_kernel(
    part_all, weight_hbm, feat_hbm, gf_ref, gw_out,
    first, second, merged, half, pair_in, total, whole, weight_raw, weight_ref, feat_ref, gw_ref, gw_send, gw_in,
    load_sems, send_sems, recv_sems, gw_sems,
):
    width = part_all.shape[1]
    chunks, nodes_t = whole.shape[0], part_all.shape[2]
    loads = [
        pltpu.make_async_copy(weight_hbm, weight_raw, load_sems.at[0]),
        pltpu.make_async_copy(feat_hbm, feat_ref, load_sems.at[1]),
    ]
    for load in loads:
        load.start()
    row, col, fib = position()
    l, z = row // RING, lax.rem(row, RING)
    h, x = fib // RING, lax.rem(fib, RING)
    z_up, z_down, z_far = (lax.rem(z + d, RING) for d in (1, RING - 1, 2))
    x_up, x_down, x_far = (lax.rem(x + d, RING) for d in (1, RING - 1, 2))
    to_z_up, to_z_down = (l * RING + z_up, col, fib), (l * RING + z_down, col, fib)
    to_x_up, to_x_down = (row, col, h * RING + x_up), (row, col, h * RING + x_down)
    to_pair = ((1 - l) * RING + z, col, fib)
    to_cross = ((1 - l) * RING + z, col, (1 - h) * RING + x)
    peers = [
        (lax.rem(row + d // 2, 8), lax.rem(col + d, 2), fib) for d in range(1, 16)
    ]
    greet([to_x_up, to_x_down, to_cross, *peers])

    def part_at(to_l, to_z, t):
        return part_all.at[(to_l * RING + to_z) * chunks + t]

    def copy(kind, t, source, target, peer):
        return pltpu.make_async_remote_copy(
            source,
            target,
            send_sems.at[kind, t],
            recv_sems.at[kind, t],
            device_id=peer,
            device_id_type=MESH,
        )

    def link(kind, t):
        if kind == 0:
            return copy(0, t, part_at(0, z_far, t), first.at[0, t], to_z_up)
        if kind == 1:
            return copy(1, t, part_at(1, z_far, t), first.at[1, t], to_z_down)
        if kind == 2:
            return copy(2, t, part_at(1, z_up, t), second.at[0, t, 1], to_z_up)
        if kind == 3:
            return copy(3, t, part_at(0, z_down, t), second.at[1, t, 0], to_z_down)
        if kind == 4:
            return copy(4, t, merged.at[0, t], second.at[0, t, 0], to_z_up)
        if kind == 5:
            return copy(5, t, merged.at[1, t], second.at[1, t, 1], to_z_down)
        if kind == 6:
            return copy(6, t, half.at[t], pair_in.at[t], to_pair)
        if kind == 7:
            return copy(7, t, total.at[t], whole.at[t, x, h], to_pair)
        if kind == 8:
            return copy(8, t, total.at[t], whole.at[t, x, h], to_cross)
        if kind == 9:
            return copy(9, t, whole.at[t, x], whole.at[t, x], to_x_up)
        if kind == 10:
            return copy(10, t, whole.at[t, x], whole.at[t, x], to_x_down)
        if kind == 11:
            return copy(11, t, whole.at[t, x_down, 0], whole.at[t, x_down, 0], to_x_up)
        return copy(12, t, whole.at[t, x_up, 1], whole.at[t, x_up, 1], to_x_down)

    def arrived(kind, t):
        if kind == 7:
            slot = whole.at[t, x, h]
        elif kind == 8:
            slot = whole.at[t, x, 1 - h]
        elif kind == 9:
            slot = whole.at[t, x_down]
        elif kind == 10:
            slot = whole.at[t, x_up]
        elif kind == 11:
            slot = whole.at[t, x_far, 0]
        elif kind == 12:
            slot = whole.at[t, x_far, 1]
        else:
            link(kind, t).wait_recv()
            return
        copy(kind, t, slot, slot, to_pair).wait_recv()

    def added(*refs):
        terms = [r[...].astype(jnp.float32) for r in refs]
        return functools.reduce(lambda a, b: a + b, terms)

    gw_ref[...] = jnp.zeros_like(gw_ref)

    def settle_loads():
        for load in loads:
            load.wait()
        for k in range(2 * RING):
            source = (k % 2) * RING + k // 2
            weight_ref[:, k * width : (k + 1) * width] = weight_raw[:, source * width : (source + 1) * width]

    def send_shares(t):
        for kind in range(4):
            link(kind, t).start()

    def merge(t):
        arrived(0, t)
        merged[0, t] = added(part_at(0, z_up, t), first.at[0, t]).astype(merged.dtype)
        link(4, t).start()
        arrived(1, t)
        merged[1, t] = added(part_at(1, z_down, t), first.at[1, t]).astype(merged.dtype)
        link(5, t).start()

    def sum_over_z(t):
        for kind in (2, 3, 4, 5):
            arrived(kind, t)
        half[t] = added(part_at(l, z, t), second.at[0, t, l], second.at[1, t, l]).astype(half.dtype)
        link(6, t).start()

    def sum_over_y(t):
        o = 1 - l
        arrived(6, t)
        total[t] = added(
            part_at(o, z, t), second.at[0, t, o], second.at[1, t, o], pair_in.at[t]
        ).astype(total.dtype)
        link(7, t).start()
        link(8, t).start()

    def spread(t):
        arrived(7, t)
        arrived(8, t)
        link(9, t).start()
        link(10, t).start()

    def forward(t):
        arrived(9, t)
        link(11, t).start()
        arrived(10, t)
        link(12, t).start()

    def multiply(t):
        arrived(11, t)
        arrived(12, t)

        @pl.when(lax.rem(t, 2) == 1)
        def _():
            depth = weight_ref.shape[1]
            panel = jnp.concatenate(
                [whole[t - 1].reshape(depth, nodes_t), whole[t].reshape(depth, nodes_t)], axis=1
            )
            part = pl.ds(pl.multiple_of((t - 1) * nodes_t, 2 * nodes_t), 2 * nodes_t)
            product = jnp.dot(weight_ref[...], panel, preferred_element_type=jnp.float32)
            gf_ref[part, :] = product.T.astype(gf_ref.dtype)
            gw_ref[...] += jnp.dot(panel, feat_ref[part, :], preferred_element_type=jnp.float32)

    stages = (send_shares, merge, sum_over_z, sum_over_y, spread, forward, multiply)

    settle_loads()

    @pl.loop(0, chunks + LAGS[-1])
    def _(step):
        for late, stage in zip(LAGS, stages):
            t = step - late

            @pl.when((t >= 0) & (t < chunks))
            def _(stage=stage, t=t):
                stage(t)

    rows = gw_ref.shape[0] // 16

    def place(of_row, of_col):
        return of_row * 2 + of_col

    def piece(ref, of):
        return ref.at[pl.ds(pl.multiple_of(of * rows, rows), rows)]

    def gw_copy(phase, d, source, target):
        return pltpu.make_async_remote_copy(
            source, target, gw_sems.at[phase, 0, d], gw_sems.at[phase, 1, d], device_id=peers[d - 1], device_id_type=MESH
        )

    here = place(row, col)
    gw_send[...] = gw_ref[...].astype(gw_send.dtype)
    gives = []
    for d, peer in enumerate(peers, 1):
        gives.append(gw_copy(0, d, piece(gw_send, place(peer[0], peer[1])), gw_in.at[d]))
        gives[-1].start()
    own = gw_ref[pl.ds(pl.multiple_of(here * rows, rows), rows), :]
    for d in range(1, 16):
        gives[d - 1].wait_recv()
        own += gw_in[d].astype(jnp.float32)
    gw_out[pl.ds(pl.multiple_of(here * rows, rows), rows), :] = own.astype(gw_out.dtype)
    for d in range(1, 16):
        gives.append(gw_copy(1, d, piece(gw_out, here), piece(gw_out, here)))
        gives[-1].start()

    @pl.loop(0, chunks)
    def _(t):
        for kind in range(13):
            link(kind, t).wait_send()

    for d in range(1, 16):
        slot = piece(gw_out, place(lax.rem(row + 8 - (d // 2), 8), lax.rem(col + d, 2)))
        gw_copy(1, d, slot, slot).wait_recv()
    for give in gives:
        give.wait_send()


def flow(part, weight, features):
    _, width, cut = part.shape
    nodes, whole = features.shape[0], weight.shape[1]
    chunks = nodes // cut
    piece = (width, cut)
    sixteen = jnp.bfloat16
    return pl.pallas_call(
        flow_kernel,
        out_shape=(
            jax.ShapeDtypeStruct((nodes, width), sixteen),
            jax.ShapeDtypeStruct((whole, width), sixteen),
        ),
        in_specs=[VMEM, ANY, ANY],
        out_specs=(VMEM, VMEM),
        scratch_shapes=[
            pltpu.VMEM((2, chunks, *piece), sixteen),
            pltpu.VMEM((2, chunks, 2, *piece), sixteen),
            pltpu.VMEM((2, chunks, *piece), sixteen),
            pltpu.VMEM((chunks, *piece), sixteen),
            pltpu.VMEM((chunks, *piece), sixteen),
            pltpu.VMEM((chunks, *piece), sixteen),
            pltpu.VMEM((chunks, RING, 2, *piece), sixteen),
            pltpu.VMEM(weight.shape, sixteen),
            pltpu.VMEM(weight.shape, sixteen),
            pltpu.VMEM(features.shape, sixteen),
            pltpu.VMEM((whole, width), jnp.float32),
            pltpu.VMEM((whole, width), sixteen),
            pltpu.VMEM((16, whole // 16, width), sixteen),
            pltpu.SemaphoreType.DMA((2,)),
            pltpu.SemaphoreType.DMA((13, chunks)),
            pltpu.SemaphoreType.DMA((13, chunks)),
            pltpu.SemaphoreType.DMA((2, 2, 16)),
        ],
        compiler_params=pltpu.CompilerParams(
            collective_id=1, has_side_effects=True, vmem_limit_bytes=20 << 20
        ),
        cost_estimate=pl.CostEstimate(
            flops=4 * nodes * width * whole, bytes_accessed=16 << 20, transcendentals=0
        ),
        name="flow",
    )(part, weight, features)


def finish_kernel(gf_ref, gw_ref, gf_hbm, gw_hbm, gw_turned, sems):
    width = gw_turned.shape[0]
    write_gf = pltpu.make_async_copy(gf_ref, gf_hbm, sems.at[0])
    write_gf.start()
    for k in range(2 * RING):
        target = (k % 2) * RING + k // 2
        block = gw_ref[k * width : (k + 1) * width, :].astype(jnp.float32)
        gw_turned[:, target * width : (target + 1) * width] = block.T
    write_gw = pltpu.make_async_copy(gw_turned, gw_hbm, sems.at[1])
    write_gw.start()
    write_gf.wait()
    write_gw.wait()


def finish(gf, gw):
    turned = gw.shape[::-1]
    return pl.pallas_call(
        finish_kernel,
        out_shape=(
            jax.ShapeDtypeStruct(gf.shape, gf.dtype),
            jax.ShapeDtypeStruct(turned, jnp.float32),
        ),
        in_specs=[VMEM, VMEM],
        out_specs=(ANY, ANY),
        scratch_shapes=[pltpu.VMEM(turned, jnp.float32), pltpu.SemaphoreType.DMA((2,))],
        compiler_params=pltpu.CompilerParams(vmem_limit_bytes=4 << 20),
        cost_estimate=pl.CostEstimate(flops=0, bytes_accessed=1 << 20, transcendentals=0),
        name="finish",
    )(gf, gw)


def on_device(features, pre_activation, out_grad, weight, tiles, rows, cols, counts):
    tile = tiles.shape[-1]
    grad = local_grads(pre_activation, out_grad, tile)
    part = tile_products(rows, cols, counts, grad, tiles[0, 0], 8 * (features.shape[0] // tile))
    return finish(*flow(part, weight, features))


def solution(mesh):
    in_specs = (
        P(("row", "col"), "fib"),
        P(("row", "col"), "fib"),
        P(("row", "col"), "fib"),
        P("fib", None),
        P("row", "col", None, None, None),
        P("row", "col", None),
        P("row", "col", None),
        P("row", "col"),
    )
    out_specs = (P(("row", "col"), "fib"), P("fib", None))
    return jax.shard_map(
        on_device, mesh=mesh, in_specs=in_specs, out_specs=out_specs, check_vma=False
    )
```

time: 104 us -> 114 us (1.096)
  Pallas kernels: 91.8 us -> 104 us
    pallas_call x1, Pallas kernels: 66.6 us -> 93 us  [flow(): pl.pallas_call(flow_kernel, out_shape=(jax.ShapeDtypeStruct((nodes, width...]
    pallas_call x2, Pallas kernels: 21.8 us -> 5.68 us  [the longest x1 4.7 us: tile_products(): pl.pallas_call(tile_kernel, out_shape=jax.ShapeDtypeStruct((out_tiles * t...]
    reshape x4 -> x0, local copies, waits for them, and re-layouts: 1.55 us -> none  [the longest x1 1 us: on_device(): total.reshape(RING, 2, width, width).transpose(3, 1, 0, 2)]
    pallas_call x1, Pallas kernels: 3.44 us -> 4.97 us  [local_grads(): pl.pallas_call(grad_kernel, out_shape=jax.ShapeDtypeStruct((2 * own_tiles...]
    unnamed x17 -> x14, local copies, waits for them, and re-layouts: 8.29 us -> 9.16 us
where the time goes in v3:
time: 114 us
  Pallas kernels  104 us (91%)
  local copies, waits for them, and re-layouts  9.16 us (8%)
  between operations  1.4 us (1%)
    pallas_call x1, Pallas kernels, flow(): pl.pallas_call(flow_kernel, out_shape=(jax.ShapeDtypeStruct((nodes, width...  93 us
    unnamed x14, local copies, waits for them, and re-layouts  9.16 us
    pallas_call x1, Pallas kernels, local_grads(): pl.pallas_call(grad_kernel, out_shape=jax.ShapeDtypeStruct((2 * own_tiles...  4.97 us
    pallas_call x1, Pallas kernels, tile_products(): pl.pallas_call(tile_kernel, out_shape=jax.ShapeDtypeStruct((out_tiles * t...  4.7 us

profile of v3, /device:TPU:1, one launch (start us, length us, event | category | flops | bytes accessed | tf_op | source)
XLA Modules:
  0.0 114.2 jit_solution(491437396580725686)
XLA Ops:
  0.6 0.0 copy-start.1
  1.3 0.0 copy-start.2
  1.4 1.0 copy-done.2
  2.4 0.0 copy-start.3
  2.4 1.0 copy-done.3
  3.4 0.0 copy-start.4
  3.4 5.0 %local_grads.1.grad_ref = bf16[16,128,256]{2,1,0:T(8,128)(2,1)S(1)} custom-call(bf16[2048,128]{1,0:T(8,128)(2,1)S(1)} %copy-done.2, bf16[2048,128]{1,0:T(8,128)(2,1)S(1)} %copy-done.3), custom_call_target="tpu_custom_call" | custom-call | flops 2621440 | bytes 2097152 | tf_op jit(solution)/shard_map/local_grads/pallas_call | solution.py:78
  8.4 0.0 copy-start
  8.4 5.8 %copy-done = bf16[1,1,128,256,256]{4,3,2,1,0:T(8,128)(2,1)S(1)} copy-done((bf16[1,1,128,256,256]{4,3,2,1,0:T(8,128)(2,1)S(1)}, bf16[1,1,128,256,256]{4,3,2,1,0:T(8,128)(2,1)}, u32[]{:S(2)}) %copy-start) | copy-done | bytes 16777240
  14.2 0.0 copy-start.5
  14.2 0.7 copy-done.5
  14.8 0.0 copy-start.6
  14.8 0.7 copy-done.6
  15.5 4.7 %tile_products.1.part_all = bf16[128,128,128]{2,1,0:T(8,128)(2,1)S(1)} custom-call(s32[1,1,128]{2,1,0:T(1,128)S(1)} %copy-done.5, s32[1,1,128]{2,1,0:T(1,128)S(1)} %copy-done.6, s32[1,1]{1,0:T(1,128)S(6)} %copy.10.count_hbm, bf16[16,128,256]{2,1,0:T(8,128)(2,1)S(1)} %local_grads.1.grad_ref, bf16[128,256,256]{2,1,0:T(8,128)(2,1)S(1)} %bitcast.1), custom_call_target="tpu_custom_call" | custom-call | flops 2147483648 | bytes 16777216 | tf_op jit(solution)/shard_map/tile_products/pallas_call | solution.py:157
  20.2 0.0 copy-done.1
  20.2 0.0 copy-done.4
  20.2 93.0 %flow.1 = (bf16[2048,128]{1,0:T(8,128)(2,1)S(1)}, bf16[1024,128]{1,0:T(8,128)(2,1)S(1)}) custom-call(bf16[128,128,128]{2,1,0:T(8,128)(2,1)S(1)} %tile_products.1.part_all, bf16[128,1024]{1,0:T(8,128)(2,1)S(1)} %copy-done.4, bf16[2048,128]{1,0:T(8,128)(2,1)S(1)} %copy-done.1), custom_call_target="tpu_custom_call" | custom-call | flops 1073741824 | bytes 16777216 | tf_op jit(solution)/shard_map/flow/pallas_call | solution.py:392
  113.3 1.0 finish.1
Async XLA Ops:
  0.6 19.6 %copy-start.1 = (bf16[2048,128]{1,0:T(8,128)(2,1)S(1)}, bf16[2048,128]{1,0:T(8,128)(2,1)}, u32[]{:S(2)}) copy-start(bf16[2048,128]{1,0:T(8,128)(2,1)} %feat_hbm.1) | copy-start | bytes 1572868
  1.3 1.0 copy-start.2
  2.4 1.0 copy-start.3
  3.4 16.8 %copy-start.4 = (bf16[128,1024]{1,0:T(8,128)(2,1)S(1)}, bf16[128,1024]{1,0:T(8,128)(2,1)}, u32[]{:S(2)}) copy-start(bf16[128,1024]{1,0:T(8,128)(2,1)} %weight_hbm.1) | copy-start | bytes 786436
  8.4 5.8 %copy-start = (bf16[1,1,128,256,256]{4,3,2,1,0:T(8,128)(2,1)S(1)}, bf16[1,1,128,256,256]{4,3,2,1,0:T(8,128)(2,1)}, u32[]{:S(2)}) copy-start(bf16[1,1,128,256,256]{4,3,2,1,0:T(8,128)(2,1)} %param.12) | copy-start | bytes 50331652
  14.2 0.7 copy-start.5
  14.8 0.7 copy-start.6

commit v4 on v3

--- a/solution.py
+++ b/solution.py
@@ -9,11 +9,12 @@
 
 GROUP = 8
 RING = 4
-LAGS = (0, 1, 2, 3, 4, 5, 6)
+LAGS = (0, 2, 4, 6, 8, 10)
 MESH = pl.DeviceIdType.MESH
 VMEM = pl.BlockSpec(memory_space=pltpu.VMEM)
-ANY = pl.BlockSpec(memory_space=pl.ANY)
+HBM = pl.BlockSpec(memory_space=pltpu.HBM)
 CHUNK = 128
+DIRECT = 2
 
 
 def greet(peers):
@@ -78,7 +79,7 @@
     return pl.pallas_call(
         grad_kernel,
         out_shape=jax.ShapeDtypeStruct((2 * own_tiles, width, tile), jnp.bfloat16),
-        in_specs=[ANY, ANY],
+        in_specs=[HBM, HBM],
         out_specs=VMEM,
         scratch_shapes=[
             pltpu.VMEM(pre.shape, pre.dtype),
@@ -98,8 +99,8 @@
 
 
 def tile_kernel(
-    rows_hbm, cols_hbm, count_hbm, grad_ref, tiles_ref, out_ref,
-    held, total, rows_ref, cols_ref, count_ref, sems, index_sems,
+    rows_hbm, cols_hbm, count_ref, grad_ref, tiles_ref, out_ref,
+    held, total, rows_ref, cols_ref, sems, index_sems,
 ):
     slots, tile, _ = tiles_ref.shape
     cuts = tile // CHUNK
@@ -112,17 +113,15 @@
     indices = [
         pltpu.make_async_copy(source, target, index_sems.at[i])
         for i, (source, target) in enumerate(
-            ((count_hbm, count_ref), (rows_hbm, rows_ref), (cols_hbm, cols_ref))
+            ((rows_hbm, rows_ref), (cols_hbm, cols_ref))
         )
     ]
     for load in indices:
         load.start()
-    copy(0).start()
-    indices[0].wait()
     count = jnp.clip(count_ref[0, 0], 1, slots)
     used = (count + GROUP - 1) // GROUP
 
-    @pl.loop(1, used)
+    @pl.loop(0, used)
     def _(g):
         copy(g).start()
 
@@ -130,7 +129,7 @@
     def _(t):
         total[t] = jnp.zeros(total.shape[1:], total.dtype)
 
-    for load in indices[1:]:
+    for load in indices:
         load.wait()
 
     @pl.loop(0, used)
@@ -157,16 +156,15 @@
     return pl.pallas_call(
         tile_kernel,
         out_shape=jax.ShapeDtypeStruct((out_tiles * tile // CHUNK, width, CHUNK), jnp.bfloat16),
-        in_specs=[ANY, ANY, ANY, VMEM, ANY],
+        in_specs=[HBM, HBM, pl.BlockSpec(memory_space=pltpu.SMEM), VMEM, HBM],
         out_specs=VMEM,
         scratch_shapes=[
             pltpu.VMEM((slots, tile, tile), jnp.bfloat16),
             pltpu.VMEM((out_tiles + 1, width, tile), jnp.float32),
             pltpu.SMEM(rows.shape, rows.dtype),
             pltpu.SMEM(cols.shape, cols.dtype),
-            pltpu.SMEM(count.shape, count.dtype),
             pltpu.SemaphoreType.DMA((slots // GROUP,)),
-            pltpu.SemaphoreType.DMA((3,)),
+            pltpu.SemaphoreType.DMA((2,)),
         ],
         compiler_params=pltpu.CompilerParams(vmem_limit_bytes=28 << 20),
         cost_estimate=pl.CostEstimate(
@@ -180,7 +178,8 @@
 
 def flow_kernel(
     part_all, weight_hbm, feat_hbm, gf_ref, gw_out,
-    first, second, merged, half, pair_in, total, whole, weight_raw, weight_ref, feat_ref, gw_ref, gw_send, gw_in,
+    first, second, merged, half, y_in, whole, weight_raw, weight_ref, feat_ref, gw_ref, gw_send, mate_in,
+    half_send, gw_in,
     load_sems, send_sems, recv_sems, gw_sems,
 ):
     width = part_all.shape[1]
@@ -198,12 +197,15 @@
     x_up, x_down, x_far = (lax.rem(x + d, RING) for d in (1, RING - 1, 2))
     to_z_up, to_z_down = (l * RING + z_up, col, fib), (l * RING + z_down, col, fib)
     to_x_up, to_x_down = (row, col, h * RING + x_up), (row, col, h * RING + x_down)
+    to_x_far = (row, col, h * RING + x_far)
     to_pair = ((1 - l) * RING + z, col, fib)
     to_cross = ((1 - l) * RING + z, col, (1 - h) * RING + x)
-    peers = [
-        (lax.rem(row + d // 2, 8), lax.rem(col + d, 2), fib) for d in range(1, 16)
-    ]
-    greet([to_x_up, to_x_down, to_cross, *peers])
+    to_far = (row, col, (1 - h) * RING + x)
+    mate = (row, 1 - col, fib)
+    peers = [(lax.rem(row + d, 8), col, fib) for d in range(1, 8)]
+    greet([to_x_up, to_x_down, to_x_far, to_cross, to_far, mate, *peers])
+
+    forwarded = chunks - DIRECT
 
     def part_at(to_l, to_z, t):
         return part_all.at[(to_l * RING + to_z) * chunks + t]
@@ -232,11 +234,11 @@
         if kind == 5:
             return copy(5, t, merged.at[1, t], second.at[1, t, 1], to_z_down)
         if kind == 6:
-            return copy(6, t, half.at[t], pair_in.at[t], to_pair)
+            return copy(6, t, half.at[t, 1 - l], y_in.at[0, t], to_pair)
         if kind == 7:
-            return copy(7, t, total.at[t], whole.at[t, x, h], to_pair)
+            return copy(7, t, half.at[t, 1 - l], y_in.at[1, t], to_cross)
         if kind == 8:
-            return copy(8, t, total.at[t], whole.at[t, x, h], to_cross)
+            return copy(8, t, half.at[t, l], y_in.at[2, t], to_far)
         if kind == 9:
             return copy(9, t, whole.at[t, x], whole.at[t, x], to_x_up)
         if kind == 10:
@@ -246,11 +248,7 @@
         return copy(12, t, whole.at[t, x_up, 1], whole.at[t, x_up, 1], to_x_down)
 
     def arrived(kind, t):
-        if kind == 7:
-            slot = whole.at[t, x, h]
-        elif kind == 8:
-            slot = whole.at[t, x, 1 - h]
-        elif kind == 9:
+        if kind == 9:
             slot = whole.at[t, x_down]
         elif kind == 10:
             slot = whole.at[t, x_up]
@@ -291,29 +289,38 @@
     def sum_over_z(t):
         for kind in (2, 3, 4, 5):
             arrived(kind, t)
-        half[t] = added(part_at(l, z, t), second.at[0, t, l], second.at[1, t, l]).astype(half.dtype)
-        link(6, t).start()
+        for to_l in range(2):
+            half[t, to_l] = added(
+                part_at(to_l, z, t), second.at[0, t, to_l], second.at[1, t, to_l]
+            ).astype(half.dtype)
+        for kind in (6, 7, 8):
+            link(kind, t).start()
 
     def sum_over_y(t):
-        o = 1 - l
-        arrived(6, t)
-        total[t] = added(
-            part_at(o, z, t), second.at[0, t, o], second.at[1, t, o], pair_in.at[t]
-        ).astype(total.dtype)
-        link(7, t).start()
-        link(8, t).start()
-
-    def spread(t):
-        arrived(7, t)
-        arrived(8, t)
+        for kind in (6, 7, 8):
+            arrived(kind, t)
+        whole[t, x, h] = added(half.at[t, l], y_in.at[0, t]).astype(whole.dtype)
+        whole[t, x, 1 - h] = added(y_in.at[1, t], y_in.at[2, t]).astype(whole.dtype)
         link(9, t).start()
         link(10, t).start()
 
+        @pl.when(t >= forwarded)
+        def _():
+            for side in range(2):
+                block = whole.at[t, x, side]
+                copy(11 + side, t, block, block, to_x_far).start()
+
     def forward(t):
-        arrived(9, t)
-        link(11, t).start()
-        arrived(10, t)
-        link(12, t).start()
+        for kind in (9, 10):
+            arrived(kind, t)
+
+            @pl.when(t < forwarded)
+            def _(kind=kind):
+                link(kind + 2, t).start()
+
+        @pl.when(t >= forwarded)
+        def _():
+            multiply(t)
 
     def multiply(t):
         arrived(11, t)
@@ -330,45 +337,49 @@
             gf_ref[part, :] = product.T.astype(gf_ref.dtype)
             gw_ref[...] += jnp.dot(panel, feat_ref[part, :], preferred_element_type=jnp.float32)
 
-    stages = (send_shares, merge, sum_over_z, sum_over_y, spread, forward, multiply)
+    stages = (send_shares, merge, sum_over_z, sum_over_y, forward, multiply)
 
     settle_loads()
 
-    @pl.loop(0, chunks + LAGS[-1])
+    @pl.loop(0, chunks + LAGS[-2])
     def _(step):
         for late, stage in zip(LAGS, stages):
             t = step - late
 
-            @pl.when((t >= 0) & (t < chunks))
+            @pl.when((t >= 0) & (t < (forwarded if stage is multiply else chunks)))
             def _(stage=stage, t=t):
                 stage(t)
 
-    rows = gw_ref.shape[0] // 16
-
-    def place(of_row, of_col):
-        return of_row * 2 + of_col
-
-    def piece(ref, of):
-        return ref.at[pl.ds(pl.multiple_of(of * rows, rows), rows)]
-
-    def gw_copy(phase, d, source, target):
+    span = gw_ref.shape[0] // 2
+    rows = span // 8
+
+    def piece(ref, of_row, size=rows):
+        return ref.at[pl.ds(pl.multiple_of(of_row, size), size)]
+
+    def gw_copy(phase, d, source, target, peer):
         return pltpu.make_async_remote_copy(
-            source, target, gw_sems.at[phase, 0, d], gw_sems.at[phase, 1, d], device_id=peers[d - 1], device_id_type=MESH
+            source, target, gw_sems.at[phase, 0, d], gw_sems.at[phase, 1, d], device_id=peer, device_id_type=MESH
         )
 
-    here = place(row, col)
     gw_send[...] = gw_ref[...].astype(gw_send.dtype)
-    gives = []
-    for d, peer in enumerate(peers, 1):
-        gives.append(gw_copy(0, d, piece(gw_send, place(peer[0], peer[1])), gw_in.at[d]))
+    gives = [gw_copy(0, 0, piece(gw_send, (1 - col) * span, span), mate_in, mate)]
+    gives[0].start()
+    gives[0].wait_recv()
+    mine = gw_ref[pl.ds(pl.multiple_of(col * span, span), span), :] + mate_in[...].astype(jnp.float32)
+    gw_ref[0:span, :] = mine
+    half_send[...] = mine.astype(half_send.dtype)
+    for d in range(1, 8):
+        to = lax.rem(row + d, 8)
+        gives.append(gw_copy(1, d, piece(half_send, to * rows), gw_in.at[d], peers[d - 1]))
         gives[-1].start()
-    own = gw_ref[pl.ds(pl.multiple_of(here * rows, rows), rows), :]
-    for d in range(1, 16):
-        gives[d - 1].wait_recv()
+    own = gw_ref[pl.ds(pl.multiple_of(row * rows, rows), rows), :]
+    for d in range(1, 8):
+        gives[d].wait_recv()
         own += gw_in[d].astype(jnp.float32)
-    gw_out[pl.ds(pl.multiple_of(here * rows, rows), rows), :] = own.astype(gw_out.dtype)
-    for d in range(1, 16):
-        gives.append(gw_copy(1, d, piece(gw_out, here), piece(gw_out, here)))
+    here = col * span + row * rows
+    gw_out[pl.ds(pl.multiple_of(here, rows), rows), :] = own.astype(gw_out.dtype)
+    for d in range(1, 8):
+        gives.append(gw_copy(2, d, piece(gw_out, here), piece(gw_out, here), peers[d - 1]))
         gives[-1].start()
 
     @pl.loop(0, chunks)
@@ -376,9 +387,14 @@
         for kind in range(13):
             link(kind, t).wait_send()
 
-    for d in range(1, 16):
-        slot = piece(gw_out, place(lax.rem(row + 8 - (d // 2), 8), lax.rem(col + d, 2)))
-        gw_copy(1, d, slot, slot).wait_recv()
+    for d in range(1, 8):
+        slot = piece(gw_out, col * span + lax.rem(row + 8 - d, 8) * rows)
+        gw_copy(2, d, slot, slot, peers[d - 1]).wait_recv()
+    final = piece(gw_out, col * span, span)
+    gives.append(gw_copy(0, 1, final, final, mate))
+    gives[-1].start()
+    slot = piece(gw_out, (1 - col) * span, span)
+    gw_copy(0, 1, slot, slot, mate).wait_recv()
     for give in gives:
         give.wait_send()
 
@@ -395,26 +411,27 @@
             jax.ShapeDtypeStruct((nodes, width), sixteen),
             jax.ShapeDtypeStruct((whole, width), sixteen),
         ),
-        in_specs=[VMEM, ANY, ANY],
+        in_specs=[VMEM, HBM, HBM],
         out_specs=(VMEM, VMEM),
         scratch_shapes=[
             pltpu.VMEM((2, chunks, *piece), sixteen),
             pltpu.VMEM((2, chunks, 2, *piece), sixteen),
             pltpu.VMEM((2, chunks, *piece), sixteen),
-            pltpu.VMEM((chunks, *piece), sixteen),
-            pltpu.VMEM((chunks, *piece), sixteen),
-            pltpu.VMEM((chunks, *piece), sixteen),
+            pltpu.VMEM((chunks, 2, *piece), sixteen),
+            pltpu.VMEM((3, chunks, *piece), sixteen),
             pltpu.VMEM((chunks, RING, 2, *piece), sixteen),
             pltpu.VMEM(weight.shape, sixteen),
             pltpu.VMEM(weight.shape, sixteen),
             pltpu.VMEM(features.shape, sixteen),
             pltpu.VMEM((whole, width), jnp.float32),
             pltpu.VMEM((whole, width), sixteen),
-            pltpu.VMEM((16, whole // 16, width), sixteen),
+            pltpu.VMEM((whole // 2, width), sixteen),
+            pltpu.VMEM((whole // 2, width), sixteen),
+            pltpu.VMEM((8, whole // 16, width), sixteen),
             pltpu.SemaphoreType.DMA((2,)),
             pltpu.SemaphoreType.DMA((13, chunks)),
             pltpu.SemaphoreType.DMA((13, chunks)),
-            pltpu.SemaphoreType.DMA((2, 2, 16)),
+            pltpu.SemaphoreType.DMA((3, 2, 8)),
         ],
         compiler_params=pltpu.CompilerParams(
             collective_id=1, has_side_effects=True, vmem_limit_bytes=20 << 20
@@ -449,7 +466,7 @@
             jax.ShapeDtypeStruct(turned, jnp.float32),
         ),
         in_specs=[VMEM, VMEM],
-        out_specs=(ANY, ANY),
+        out_specs=(HBM, HBM),
         scratch_shapes=[pltpu.VMEM(turned, jnp.float32), pltpu.SemaphoreType.DMA((2,))],
         compiler_params=pltpu.CompilerParams(vmem_limit_bytes=4 << 20),
         cost_estimate=pl.CostEstimate(flops=0, bytes_accessed=1 << 20, transcendentals=0),
@@ -459,8 +476,12 @@
 
 def on_device(features, pre_activation, out_grad, weight, tiles, rows, cols, counts):
     tile = tiles.shape[-1]
+    features, pre_activation, out_grad, weight, tiles, rows, cols = (
+        pltpu.with_memory_space_constraint(a, pltpu.HBM)
+        for a in (features, pre_activation, out_grad, weight, tiles[0, 0], rows, cols)
+    )
     grad = local_grads(pre_activation, out_grad, tile)
-    part = tile_products(rows, cols, counts, grad, tiles[0, 0], 8 * (features.shape[0] // tile))
+    part = tile_products(rows, cols, counts, grad, tiles, 8 * (features.shape[0] // tile))
     return finish(*flow(part, weight, features))
 
 

time: 114 us -> 84.2 us (0.74)
  Pallas kernels: 104 us -> 82.8 us
  local copies, waits for them, and re-layouts: 9.16 us -> 0 us
    pallas_call x1, Pallas kernels: 93 us -> 72.8 us  [flow(): pl.pallas_call(flow_kernel, out_shape=(jax.ShapeDtypeStruct((nodes, width...]
    unnamed x14 -> x0, local copies, waits for them, and re-layouts: 9.16 us -> none
where the time goes in v4:
time: 84.2 us; the launch traced here: 84.1 us
  Pallas kernels  82.8 us (98%)
  between operations  1.3 us (2%)
    pallas_call x1, Pallas kernels, flow(): pl.pallas_call(flow_kernel, out_shape=(jax.ShapeDtypeStruct((nodes, width...  72.8 us
    pallas_call x1, Pallas kernels, tile_products(): pl.pallas_call(tile_kernel, out_shape=jax.ShapeDtypeStruct((out_tiles * t...  4.6 us
    pallas_call x1, Pallas kernels, local_grads(): pl.pallas_call(grad_kernel, out_shape=jax.ShapeDtypeStruct((2 * own_tiles...  4.38 us

profile of v4, /device:TPU:1, one launch (start us, length us, event | category | flops | bytes accessed | tf_op | source)
XLA Modules:
  0.0 84.1 jit_solution(14658402880863816385)
XLA Ops:
  1.3 4.4 %local_grads.1.grad_ref = bf16[16,128,256]{2,1,0:T(8,128)(2,1)S(1)} custom-call(bf16[2048,128]{1,0:T(8,128)(2,1)} %pre_hbm.1, bf16[2048,128]{1,0:T(8,128)(2,1)} %out_grad_hbm.1), custom_call_target="tpu_custom_call" | custom-call | flops 2621440 | bytes 2097152 | tf_op jit(solution)/shard_map/local_grads/pallas_call | solution.py:79
  5.7 4.6 %tile_products.1.part_all = bf16[128,128,128]{2,1,0:T(8,128)(2,1)S(1)} custom-call(s32[1,1,128]{2,1,0:T(1,128)} %rows_hbm.1, s32[1,1,128]{2,1,0:T(1,128)} %cols_hbm.1, s32[1,1]{1,0:T(1,128)S(6)} %copy.10.count_ref, bf16[16,128,256]{2,1,0:T(8,128)(2,1)S(1)} %local_grads.1.grad_ref, bf16[128,256,256]{2,1,0:T(8,128)(2,1)} %bitcast.1), custom_call_target="tpu_custom_call" | custom-call | flops 2147483648 | bytes 16777216 | tf_op jit(solution)/shard_map/tile_products/pallas_call | solution.py:156
  10.3 72.8 %flow.1 = (bf16[2048,128]{1,0:T(8,128)(2,1)S(1)}, bf16[1024,128]{1,0:T(8,128)(2,1)S(1)}) custom-call(bf16[128,128,128]{2,1,0:T(8,128)(2,1)S(1)} %tile_products.1.part_all, bf16[128,1024]{1,0:T(8,128)(2,1)} %weight_hbm.1, bf16[2048,128]{1,0:T(8,128)(2,1)} %feat_hbm.1), custom_call_target="tpu_custom_call" | custom-call | flops 1073741824 | bytes 16777216 | tf_op jit(solution)/shard_map/flow/pallas_call | solution.py:408
  83.1 1.0 %finish.1 = (bf16[2048,128]{1,0:T(8,128)(2,1)}, f32[128,1024]{1,0:T(8,128)}) custom-call(bf16[2048,128]{1,0:T(8,128)(2,1)S(1)} %get-tuple-element.4.gf_ref, bf16[1024,128]{1,0:T(8,128)(2,1)S(1)} %get-tuple-element.5.gw_ref), custom_call_target="tpu_custom_call" | custom-call | bytes 1048576 | tf_op jit(solution)/shard_map/finish/pallas_call | solution.py:462

commit v5 on v4

--- a/solution.py
+++ b/solution.py
@@ -9,12 +9,11 @@
 
 GROUP = 8
 RING = 4
-LAGS = (0, 2, 4, 6, 8, 10)
+LAGS = (0, 2, 4, 6)
 MESH = pl.DeviceIdType.MESH
 VMEM = pl.BlockSpec(memory_space=pltpu.VMEM)
 HBM = pl.BlockSpec(memory_space=pltpu.HBM)
 CHUNK = 128
-DIRECT = 2
 
 
 def greet(peers):
@@ -178,46 +177,45 @@
 
 def flow_kernel(
     part_all, weight_hbm, feat_hbm, gf_ref, gw_out,
-    first, second, merged, half, y_in, whole, weight_raw, weight_ref, feat_ref, gw_ref, gw_send, mate_in,
-    half_send, gw_in,
-    load_sems, send_sems, recv_sems, gw_sems,
+    first, second, merged, half, y_in, whole, weight_raw, weight_send, weight_in, feat,
+    gf_own, gf_send, gf_in, gw_ref, gw_send, mate_in, row_send, row_in, x_send,
+    load_sems, send_sems, recv_sems, x_sems, gw_sems,
 ):
-    width = part_all.shape[1]
-    chunks, nodes_t = whole.shape[0], part_all.shape[2]
-    loads = [
-        pltpu.make_async_copy(weight_hbm, weight_raw, load_sems.at[0]),
-        pltpu.make_async_copy(feat_hbm, feat_ref, load_sems.at[1]),
-    ]
-    for load in loads:
-        load.start()
     row, col, fib = position()
     l, z = row // RING, lax.rem(row, RING)
     h, x = fib // RING, lax.rem(fib, RING)
+    chunks, width, nodes_t = whole.shape[1:]
+    pairs, span_t = chunks // 2, 2 * nodes_t
     z_up, z_down, z_far = (lax.rem(z + d, RING) for d in (1, RING - 1, 2))
-    x_up, x_down, x_far = (lax.rem(x + d, RING) for d in (1, RING - 1, 2))
     to_z_up, to_z_down = (l * RING + z_up, col, fib), (l * RING + z_down, col, fib)
-    to_x_up, to_x_down = (row, col, h * RING + x_up), (row, col, h * RING + x_down)
-    to_x_far = (row, col, h * RING + x_far)
+    to_x = [(row, col, h * RING + lax.rem(x + d, RING)) for d in range(RING)]
     to_pair = ((1 - l) * RING + z, col, fib)
     to_cross = ((1 - l) * RING + z, col, (1 - h) * RING + x)
     to_far = (row, col, (1 - h) * RING + x)
     mate = (row, 1 - col, fib)
     peers = [(lax.rem(row + d, 8), col, fib) for d in range(1, 8)]
-    greet([to_x_up, to_x_down, to_x_far, to_cross, to_far, mate, *peers])
-
-    forwarded = chunks - DIRECT
+
+    def nodes_of(p):
+        return pl.ds(pl.multiple_of(p * span_t, span_t), span_t)
+
+    load_weight = [
+        pltpu.make_async_copy(
+            weight_hbm.at[:, k * width : (k + 1) * width], weight_raw.at[k], load_sems.at[1 + k]
+        )
+        for k in range(2 * RING)
+    ]
+    load_feat = pltpu.make_async_copy(feat_hbm, feat.at[0], load_sems.at[0])
+    for load in load_weight:
+        load.start()
+    load_feat.start()
+    greet([*to_x[1:], to_cross, to_far, mate, *peers])
 
     def part_at(to_l, to_z, t):
         return part_all.at[(to_l * RING + to_z) * chunks + t]
 
     def copy(kind, t, source, target, peer):
         return pltpu.make_async_remote_copy(
-            source,
-            target,
-            send_sems.at[kind, t],
-            recv_sems.at[kind, t],
-            device_id=peer,
-            device_id_type=MESH,
+            source, target, send_sems.at[kind, t], recv_sems.at[kind, t], device_id=peer, device_id_type=MESH
         )
 
     def link(kind, t):
@@ -237,58 +235,61 @@
             return copy(6, t, half.at[t, 1 - l], y_in.at[0, t], to_pair)
         if kind == 7:
             return copy(7, t, half.at[t, 1 - l], y_in.at[1, t], to_cross)
-        if kind == 8:
-            return copy(8, t, half.at[t, l], y_in.at[2, t], to_far)
-        if kind == 9:
-            return copy(9, t, whole.at[t, x], whole.at[t, x], to_x_up)
-        if kind == 10:
-            return copy(10, t, whole.at[t, x], whole.at[t, x], to_x_down)
-        if kind == 11:
-            return copy(11, t, whole.at[t, x_down, 0], whole.at[t, x_down, 0], to_x_up)
-        return copy(12, t, whole.at[t, x_up, 1], whole.at[t, x_up, 1], to_x_down)
-
-    def arrived(kind, t):
-        if kind == 9:
-            slot = whole.at[t, x_down]
-        elif kind == 10:
-            slot = whole.at[t, x_up]
-        elif kind == 11:
-            slot = whole.at[t, x_far, 0]
-        elif kind == 12:
-            slot = whole.at[t, x_far, 1]
-        else:
-            link(kind, t).wait_recv()
-            return
-        copy(kind, t, slot, slot, to_pair).wait_recv()
+        return copy(8, t, half.at[t, l], y_in.at[2, t], to_far)
+
+    def along_x(kind, d, p, source, target):
+        return pltpu.make_async_remote_copy(
+            source, target, x_sems.at[0, kind, d, p], x_sems.at[1, kind, d, p], device_id=to_x[d], device_id_type=MESH
+        )
+
+    def feat_copy(d, p):
+        return along_x(0, d, p, feat.at[0, nodes_of(p)], feat.at[RING - d, nodes_of(p)])
+
+    def gf_copy(d, p):
+        return along_x(1, d, p, gf_send.at[d - 1, p], gf_in.at[d - 1, p])
+
+    def weight_copy(d):
+        return along_x(2, d, 0, weight_send.at[d - 1], weight_in.at[RING - d])
 
     def added(*refs):
         terms = [r[...].astype(jnp.float32) for r in refs]
         return functools.reduce(lambda a, b: a + b, terms)
 
-    gw_ref[...] = jnp.zeros_like(gw_ref)
-
-    def settle_loads():
-        for load in loads:
-            load.wait()
-        for k in range(2 * RING):
-            source = (k % 2) * RING + k // 2
-            weight_ref[:, k * width : (k + 1) * width] = weight_raw[:, source * width : (source + 1) * width]
-
     def send_shares(t):
         for kind in range(4):
             link(kind, t).start()
 
+        @pl.when(t == 0)
+        def _():
+            for load in load_weight:
+                load.wait()
+            for d in range(RING):
+                at = lax.rem(x + d, RING)
+                block = jnp.concatenate([weight_raw[at], weight_raw[RING + at]], axis=1)
+                if d == 0:
+                    weight_in[0] = block
+                else:
+                    weight_send[d - 1] = block
+                    weight_copy(d).start()
+            gw_ref[...] = jnp.zeros_like(gw_ref)
+            load_feat.wait()
+
+        @pl.when(t < pairs)
+        def _():
+            for d in range(1, RING):
+                feat_copy(d, t).start()
+
     def merge(t):
-        arrived(0, t)
+        link(0, t).wait_recv()
         merged[0, t] = added(part_at(0, z_up, t), first.at[0, t]).astype(merged.dtype)
         link(4, t).start()
-        arrived(1, t)
+        link(1, t).wait_recv()
         merged[1, t] = added(part_at(1, z_down, t), first.at[1, t]).astype(merged.dtype)
         link(5, t).start()
 
     def sum_over_z(t):
         for kind in (2, 3, 4, 5):
-            arrived(kind, t)
+            link(kind, t).wait_recv()
         for to_l in range(2):
             half[t, to_l] = added(
                 part_at(to_l, z, t), second.at[0, t, to_l], second.at[1, t, to_l]
@@ -298,102 +299,120 @@
 
     def sum_over_y(t):
         for kind in (6, 7, 8):
-            arrived(kind, t)
-        whole[t, x, h] = added(half.at[t, l], y_in.at[0, t]).astype(whole.dtype)
-        whole[t, x, 1 - h] = added(y_in.at[1, t], y_in.at[2, t]).astype(whole.dtype)
-        link(9, t).start()
-        link(10, t).start()
-
-        @pl.when(t >= forwarded)
-        def _():
-            for side in range(2):
-                block = whole.at[t, x, side]
-                copy(11 + side, t, block, block, to_x_far).start()
-
-    def forward(t):
-        for kind in (9, 10):
-            arrived(kind, t)
-
-            @pl.when(t < forwarded)
-            def _(kind=kind):
-                link(kind + 2, t).start()
-
-        @pl.when(t >= forwarded)
-        def _():
-            multiply(t)
-
-    def multiply(t):
-        arrived(11, t)
-        arrived(12, t)
+            link(kind, t).wait_recv()
+        whole[h, t] = added(half.at[t, l], y_in.at[0, t]).astype(whole.dtype)
+        whole[1 - h, t] = added(y_in.at[1, t], y_in.at[2, t]).astype(whole.dtype)
 
         @pl.when(lax.rem(t, 2) == 1)
         def _():
-            depth = weight_ref.shape[1]
-            panel = jnp.concatenate(
-                [whole[t - 1].reshape(depth, nodes_t), whole[t].reshape(depth, nodes_t)], axis=1
-            )
-            part = pl.ds(pl.multiple_of((t - 1) * nodes_t, 2 * nodes_t), 2 * nodes_t)
-            product = jnp.dot(weight_ref[...], panel, preferred_element_type=jnp.float32)
-            gf_ref[part, :] = product.T.astype(gf_ref.dtype)
-            gw_ref[...] += jnp.dot(panel, feat_ref[part, :], preferred_element_type=jnp.float32)
-
-    stages = (send_shares, merge, sum_over_z, sum_over_y, forward, multiply)
-
-    settle_loads()
-
-    @pl.loop(0, chunks + LAGS[-2])
+            multiply(lax.div(t, 2))
+
+    def multiply(p):
+        @pl.when(p == 0)
+        def _():
+            for d in range(1, RING):
+                weight_copy(d).wait_recv()
+
+        panel = jnp.concatenate(
+            [whole[:, 2 * p].reshape(2 * width, nodes_t), whole[:, 2 * p + 1].reshape(2 * width, nodes_t)], axis=1
+        )
+        for d in range(1, RING):
+            feat_copy(d, p).wait_recv()
+        beside = jnp.concatenate([feat[d, nodes_of(p), :] for d in range(RING)], axis=1)
+        gw_ref[...] += jnp.dot(panel, beside, preferred_element_type=jnp.float32)
+        for d in (2, 1, 3, 0):
+            block = jnp.dot(weight_in[d], panel, preferred_element_type=jnp.float32)
+            if d == 0:
+                gf_own[p] = block
+            else:
+                gf_send[d - 1, p] = block.astype(gf_send.dtype)
+                gf_copy(d, p).start()
+
+    def collect(p):
+        for d in range(1, RING):
+            gf_copy(d, p).wait_recv()
+        block = gf_own[p] + added(*[gf_in.at[d - 1, p] for d in range(1, RING)])
+        gf_ref[nodes_of(p), :] = block.T.astype(gf_ref.dtype)
+
+    stages = (send_shares, merge, sum_over_z, sum_over_y)
+
+    @pl.loop(0, chunks + LAGS[-1])
     def _(step):
         for late, stage in zip(LAGS, stages):
             t = step - late
 
-            @pl.when((t >= 0) & (t < (forwarded if stage is multiply else chunks)))
+            @pl.when((t >= 0) & (t < chunks))
             def _(stage=stage, t=t):
                 stage(t)
 
-    span = gw_ref.shape[0] // 2
-    rows = span // 8
-
-    def piece(ref, of_row, size=rows):
-        return ref.at[pl.ds(pl.multiple_of(of_row, size), size)]
+    rows = width // 8
 
     def gw_copy(phase, d, source, target, peer):
         return pltpu.make_async_remote_copy(
             source, target, gw_sems.at[phase, 0, d], gw_sems.at[phase, 1, d], device_id=peer, device_id_type=MESH
         )
 
-    gw_send[...] = gw_ref[...].astype(gw_send.dtype)
-    gives = [gw_copy(0, 0, piece(gw_send, (1 - col) * span, span), mate_in, mate)]
+    def piece(ref, of, size=rows):
+        return ref.at[pl.ds(pl.multiple_of(of * size, size), size)]
+
+    gw_send[...] = gw_ref[pl.ds(pl.multiple_of((1 - col) * width, width), width), :].astype(gw_send.dtype)
+    gives = [gw_copy(0, 0, gw_send, mate_in, mate)]
     gives[0].start()
     gives[0].wait_recv()
-    mine = gw_ref[pl.ds(pl.multiple_of(col * span, span), span), :] + mate_in[...].astype(jnp.float32)
-    gw_ref[0:span, :] = mine
-    half_send[...] = mine.astype(half_send.dtype)
+    mine = gw_ref[pl.ds(pl.multiple_of(col * width, width), width), :] + mate_in[...].astype(jnp.float32)
+    gw_ref[0:width, :] = mine
+    row_send[...] = mine.astype(row_send.dtype)
     for d in range(1, 8):
-        to = lax.rem(row + d, 8)
-        gives.append(gw_copy(1, d, piece(half_send, to * rows), gw_in.at[d], peers[d - 1]))
+        gives.append(gw_copy(1, d, piece(row_send, lax.rem(row + d, 8)), row_in.at[d], peers[d - 1]))
         gives[-1].start()
+
+    @pl.loop(0, pairs // 2)
+    def _(p):
+        collect(p)
+
     own = gw_ref[pl.ds(pl.multiple_of(row * rows, rows), rows), :]
     for d in range(1, 8):
         gives[d].wait_recv()
-        own += gw_in[d].astype(jnp.float32)
-    here = col * span + row * rows
-    gw_out[pl.ds(pl.multiple_of(here, rows), rows), :] = own.astype(gw_out.dtype)
+        own += row_in[d].astype(jnp.float32)
+    for d in range(RING):
+        block = own[:, d * width : (d + 1) * width].astype(gw_out.dtype)
+        if d == 0:
+            gw_out[col, row, x] = block
+        else:
+            x_send[d] = block
+            gives.append(gw_copy(2, d, x_send.at[d], gw_out.at[col, row, x], to_x[d]))
+            gives[-1].start()
+
+    @pl.loop(pairs // 2, pairs)
+    def _(p):
+        collect(p)
+
+    for d in range(1, RING):
+        slot = gw_out.at[col, row, lax.rem(x + RING - d, RING)]
+        gw_copy(2, d, slot, slot, to_x[d]).wait_recv()
     for d in range(1, 8):
-        gives.append(gw_copy(2, d, piece(gw_out, here), piece(gw_out, here), peers[d - 1]))
+        gives.append(gw_copy(3, d, gw_out.at[col, row], gw_out.at[col, row], peers[d - 1]))
         gives[-1].start()
 
     @pl.loop(0, chunks)
     def _(t):
-        for kind in range(13):
+        for kind in range(9):
             link(kind, t).wait_send()
 
+    @pl.loop(0, pairs)
+    def _(p):
+        for d in range(1, RING):
+            feat_copy(d, p).wait_send()
+            gf_copy(d, p).wait_send()
+
+    for d in range(1, RING):
+        weight_copy(d).wait_send()
     for d in range(1, 8):
-        slot = piece(gw_out, col * span + lax.rem(row + 8 - d, 8) * rows)
-        gw_copy(2, d, slot, slot, peers[d - 1]).wait_recv()
-    final = piece(gw_out, col * span, span)
-    gives.append(gw_copy(0, 1, final, final, mate))
+        slot = gw_out.at[col, lax.rem(row + 8 - d, 8)]
+        gw_copy(3, d, slot, slot, peers[d - 1]).wait_recv()
+    gives.append(gw_copy(0, 1, gw_out.at[col], gw_out.at[col], mate))
     gives[-1].start()
-    slot = piece(gw_out, (1 - col) * span, span)
+    slot = gw_out.at[1 - col]
     gw_copy(0, 1, slot, slot, mate).wait_recv()
     for give in gives:
         give.wait_send()
@@ -401,15 +420,18 @@
 
 def flow(part, weight, features):
     _, width, cut = part.shape
-    nodes, whole = features.shape[0], weight.shape[1]
+    nodes = features.shape[0]
     chunks = nodes // cut
+    pairs = chunks // 2
     piece = (width, cut)
+    block = (width, 2 * cut)
     sixteen = jnp.bfloat16
+    rows = width // 8
     return pl.pallas_call(
         flow_kernel,
         out_shape=(
             jax.ShapeDtypeStruct((nodes, width), sixteen),
-            jax.ShapeDtypeStruct((whole, width), sixteen),
+            jax.ShapeDtypeStruct((2, 8, RING, rows, width), sixteen),
         ),
         in_specs=[VMEM, HBM, HBM],
         out_specs=(VMEM, VMEM),
@@ -419,25 +441,31 @@
             pltpu.VMEM((2, chunks, *piece), sixteen),
             pltpu.VMEM((chunks, 2, *piece), sixteen),
             pltpu.VMEM((3, chunks, *piece), sixteen),
-            pltpu.VMEM((chunks, RING, 2, *piece), sixteen),
-            pltpu.VMEM(weight.shape, sixteen),
-            pltpu.VMEM(weight.shape, sixteen),
-            pltpu.VMEM(features.shape, sixteen),
-            pltpu.VMEM((whole, width), jnp.float32),
-            pltpu.VMEM((whole, width), sixteen),
-            pltpu.VMEM((whole // 2, width), sixteen),
-            pltpu.VMEM((whole // 2, width), sixteen),
-            pltpu.VMEM((8, whole // 16, width), sixteen),
-            pltpu.SemaphoreType.DMA((2,)),
-            pltpu.SemaphoreType.DMA((13, chunks)),
-            pltpu.SemaphoreType.DMA((13, chunks)),
-            pltpu.SemaphoreType.DMA((3, 2, 8)),
+            pltpu.VMEM((2, chunks, *piece), sixteen),
+            pltpu.VMEM((2 * RING, width, width), sixteen),
+            pltpu.VMEM((RING - 1, width, 2 * width), sixteen),
+            pltpu.VMEM((RING, width, 2 * width), sixteen),
+            pltpu.VMEM((RING, nodes, width), sixteen),
+            pltpu.VMEM((pairs, *block), jnp.float32),
+            pltpu.VMEM((RING - 1, pairs, *block), sixteen),
+            pltpu.VMEM((RING - 1, pairs, *block), sixteen),
+            pltpu.VMEM((2 * width, RING * width), jnp.float32),
+            pltpu.VMEM((width, RING * width), sixteen),
+            pltpu.VMEM((width, RING * width), sixteen),
+            pltpu.VMEM((width, RING * width), sixteen),
+            pltpu.VMEM((8, rows, RING * width), sixteen),
+            pltpu.VMEM((RING, rows, width), sixteen),
+            pltpu.SemaphoreType.DMA((1 + 2 * RING,)),
+            pltpu.SemaphoreType.DMA((9, chunks)),
+            pltpu.SemaphoreType.DMA((9, chunks)),
+            pltpu.SemaphoreType.DMA((2, 3, RING, pairs)),
+            pltpu.SemaphoreType.DMA((4, 2, 8)),
         ],
         compiler_params=pltpu.CompilerParams(
-            collective_id=1, has_side_effects=True, vmem_limit_bytes=20 << 20
+            collective_id=1, has_side_effects=True, vmem_limit_bytes=24 << 20
         ),
         cost_estimate=pl.CostEstimate(
-            flops=4 * nodes * width * whole, bytes_accessed=16 << 20, transcendentals=0
+            flops=32 * nodes * width * width, bytes_accessed=16 << 20, transcendentals=0
         ),
         name="flow",
     )(part, weight, features)
@@ -447,10 +475,11 @@
     width = gw_turned.shape[0]
     write_gf = pltpu.make_async_copy(gf_ref, gf_hbm, sems.at[0])
     write_gf.start()
-    for k in range(2 * RING):
-        target = (k % 2) * RING + k // 2
-        block = gw_ref[k * width : (k + 1) * width, :].astype(jnp.float32)
-        gw_turned[:, target * width : (target + 1) * width] = block.T
+    for side in range(2):
+        for x in range(RING):
+            target = side * RING + x
+            block = gw_ref[side, :, x].reshape(width, width).astype(jnp.float32)
+            gw_turned[:, target * width : (target + 1) * width] = block.T
     write_gw = pltpu.make_async_copy(gw_turned, gw_hbm, sems.at[1])
     write_gw.start()
     write_gf.wait()
@@ -458,7 +487,8 @@
 
 
 def finish(gf, gw):
-    turned = gw.shape[::-1]
+    width = gf.shape[1]
+    turned = (width, 2 * RING * width)
     return pl.pallas_call(
         finish_kernel,
         out_shape=(

time: 84.2 us -> 79.7 us (0.947)
  Pallas kernels: 82.8 us -> 78.2 us
    pallas_call x1, Pallas kernels: 72.8 us -> 68.9 us  [flow(): pl.pallas_call(flow_kernel, out_shape=(jax.ShapeDtypeStruct((nodes, width...]
where the time goes in v5:
time: 79.7 us; the launch traced here: 79.5 us
  Pallas kernels  78.2 us (98%)
  between operations  1.3 us (2%)
    pallas_call x1, Pallas kernels, flow(): pl.pallas_call(flow_kernel, out_shape=(jax.ShapeDtypeStruct((nodes, width...  68.9 us
    pallas_call x1, Pallas kernels, local_grads(): pl.pallas_call(grad_kernel, out_shape=jax.ShapeDtypeStruct((2 * own_tiles...  4.38 us
    pallas_call x1, Pallas kernels, tile_products(): pl.pallas_call(tile_kernel, out_shape=jax.ShapeDtypeStruct((out_tiles * t...  3.96 us

profile of v5, /device:TPU:1, one launch (start us, length us, event | category | flops | bytes accessed | tf_op | source)
XLA Modules:
  0.0 79.5 jit_solution(10599129038182485066)
XLA Ops:
  1.3 4.4 %local_grads.1.grad_ref = bf16[16,128,256]{2,1,0:T(8,128)(2,1)S(1)} custom-call(bf16[2048,128]{1,0:T(8,128)(2,1)} %pre_hbm.1, bf16[2048,128]{1,0:T(8,128)(2,1)} %out_grad_hbm.1), custom_call_target="tpu_custom_call" | custom-call | flops 2621440 | bytes 2097152 | tf_op jit(solution)/shard_map/local_grads/pallas_call | solution.py:78
  5.7 4.0 %tile_products.1.part_all = bf16[128,128,128]{2,1,0:T(8,128)(2,1)S(1)} custom-call(s32[1,1,128]{2,1,0:T(1,128)} %rows_hbm.1, s32[1,1,128]{2,1,0:T(1,128)} %cols_hbm.1, s32[1,1]{1,0:T(1,128)S(6)} %copy.10.count_ref, bf16[16,128,256]{2,1,0:T(8,128)(2,1)S(1)} %local_grads.1.grad_ref, bf16[128,256,256]{2,1,0:T(8,128)(2,1)} %bitcast.1), custom_call_target="tpu_custom_call" | custom-call | flops 2147483648 | bytes 16777216 | tf_op jit(solution)/shard_map/tile_products/pallas_call | solution.py:155
  9.6 68.9 %flow.1 = (bf16[2048,128]{1,0:T(8,128)(2,1)S(1)}, bf16[2,8,4,16,128]{4,3,2,1,0:T(8,128)(2,1)S(1)}) custom-call(bf16[128,128,128]{2,1,0:T(8,128)(2,1)S(1)} %tile_products.1.part_all, bf16[128,1024]{1,0:T(8,128)(2,1)} %weight_hbm.1, bf16[2048,128]{1,0:T(8,128)(2,1)} %feat_hbm.1), custom_call_target="tpu_custom_call" | custom-call | flops 1073741824 | bytes 16777216 | tf_op jit(solution)/shard_map/flow/pallas_call | solution.py:430
  78.6 1.0 %finish.1 = (bf16[2048,128]{1,0:T(8,128)(2,1)}, f32[128,1024]{1,0:T(8,128)}) custom-call(bf16[2048,128]{1,0:T(8,128)(2,1)S(1)} %get-tuple-element.4.gf_ref, bf16[2,8,4,16,128]{4,3,2,1,0:T(8,128)(2,1)S(1)} %get-tuple-element.5.gw_ref), custom_call_target="tpu_custom_call" | custom-call | bytes 1048576 | tf_op jit(solution)/shard_map/finish/pallas_call | solution.py:492

commit v6 on v5

--- a/solution.py
+++ b/solution.py
@@ -8,12 +8,14 @@
 from jax.sharding import PartitionSpec as P
 
 GROUP = 8
+EARLY = 64
 RING = 4
 LAGS = (0, 2, 4, 6)
 MESH = pl.DeviceIdType.MESH
 VMEM = pl.BlockSpec(memory_space=pltpu.VMEM)
 HBM = pl.BlockSpec(memory_space=pltpu.HBM)
 CHUNK = 128
+LATE = 4
 
 
 def greet(peers):
@@ -28,7 +30,8 @@
 
 
 def grad_kernel(
-    pre_hbm, out_grad_hbm, grad_ref, pre_ref, out_grad_ref, load_sems, send_sems, recv_sems
+    pre_hbm, out_grad_hbm, tiles_hbm, grad_ref, early_ref,
+    pre_ref, out_grad_ref, load_sems, tile_sems, send_sems, recv_sems,
 ):
     row, col, fib = position()
     own_tiles = grad_ref.shape[0] // 2
@@ -46,6 +49,14 @@
     def _(t):
         for load in loads(t):
             load.start()
+
+    def early(g):
+        group = pl.ds(g * GROUP, GROUP)
+        return pltpu.make_async_copy(tiles_hbm.at[group], early_ref.at[group], tile_sems.at[g])
+
+    @pl.loop(0, EARLY // GROUP)
+    def _(g):
+        early(g).start()
 
     greet([partner])
 
@@ -71,34 +82,43 @@
         copy(t, col).wait_send()
         copy(t, 1 - col).wait_recv()
 
-
-def local_grads(pre, out_grad, tile):
+    @pl.loop(0, EARLY // GROUP)
+    def _(g):
+        early(g).wait()
+
+
+def local_grads(pre, out_grad, tiles):
     nodes, width = pre.shape
+    tile = tiles.shape[1]
     own_tiles = nodes // tile
     return pl.pallas_call(
         grad_kernel,
-        out_shape=jax.ShapeDtypeStruct((2 * own_tiles, width, tile), jnp.bfloat16),
-        in_specs=[HBM, HBM],
-        out_specs=VMEM,
+        out_shape=(
+            jax.ShapeDtypeStruct((2 * own_tiles, width, tile), jnp.bfloat16),
+            jax.ShapeDtypeStruct((EARLY, tile, tile), tiles.dtype),
+        ),
+        in_specs=[HBM, HBM, HBM],
+        out_specs=(VMEM, VMEM),
         scratch_shapes=[
             pltpu.VMEM(pre.shape, pre.dtype),
             pltpu.VMEM(pre.shape, pre.dtype),
             pltpu.SemaphoreType.DMA((2, own_tiles)),
+            pltpu.SemaphoreType.DMA((EARLY // GROUP,)),
             pltpu.SemaphoreType.DMA((own_tiles,)),
             pltpu.SemaphoreType.DMA((own_tiles,)),
         ],
         compiler_params=pltpu.CompilerParams(
-            collective_id=0, has_side_effects=True, vmem_limit_bytes=8 << 20
+            collective_id=0, has_side_effects=True, vmem_limit_bytes=16 << 20
         ),
         cost_estimate=pl.CostEstimate(
             flops=10 * nodes * width, bytes_accessed=8 * nodes * width, transcendentals=nodes * width
         ),
         name="local_grads",
-    )(pre, out_grad)
+    )(pre, out_grad, tiles)
 
 
 def tile_kernel(
-    rows_hbm, cols_hbm, count_ref, grad_ref, tiles_ref, out_ref,
+    rows_hbm, cols_hbm, count_ref, grad_ref, early_ref, tiles_ref, out_ref,
     held, total, rows_ref, cols_ref, sems, index_sems,
 ):
     slots, tile, _ = tiles_ref.shape
@@ -106,8 +126,10 @@
     out_tiles = out_ref.shape[0] // cuts
     row_tiles = grad_ref.shape[0]
     def copy(g):
-        part = pl.ds(g * GROUP, GROUP)
-        return pltpu.make_async_copy(tiles_ref.at[part], held.at[part], sems.at[g])
+        source = tiles_ref.at[pl.ds(g * GROUP, GROUP)]
+        return pltpu.make_async_copy(
+            source, held.at[pl.ds(g * GROUP - EARLY, GROUP)], sems.at[g - EARLY // GROUP]
+        )
 
     indices = [
         pltpu.make_async_copy(source, target, index_sems.at[i])
@@ -120,7 +142,7 @@
     count = jnp.clip(count_ref[0, 0], 1, slots)
     used = (count + GROUP - 1) // GROUP
 
-    @pl.loop(0, used)
+    @pl.loop(EARLY // GROUP, used)
     def _(g):
         copy(g).start()
 
@@ -131,17 +153,22 @@
     for load in indices:
         load.wait()
 
-    @pl.loop(0, used)
-    def _(g):
-        copy(g).wait()
+    def add_group(g, tile_at):
         for j in range(GROUP):
             slot = g * GROUP + j
             row = jnp.clip(rows_ref[0, 0, slot], 0, row_tiles - 1)
             col = jnp.clip(cols_ref[0, 0, slot], 0, out_tiles - 1)
             target = jnp.where(slot < count, col, out_tiles)
-            total[target] += jnp.dot(
-                grad_ref[row], held[slot], preferred_element_type=jnp.float32
-            )
+            total[target] += jnp.dot(grad_ref[row], tile_at(slot), preferred_element_type=jnp.float32)
+
+    @pl.loop(0, jnp.minimum(used, EARLY // GROUP))
+    def _(g):
+        add_group(g, lambda slot: early_ref[slot])
+
+    @pl.loop(EARLY // GROUP, used)
+    def _(g):
+        copy(g).wait()
+        add_group(g, lambda slot: held[slot - EARLY])
 
     @pl.loop(0, out_tiles)
     def _(t):
@@ -149,20 +176,20 @@
             out_ref[t * cuts + cut] = total[t, :, cut * CHUNK : (cut + 1) * CHUNK].astype(out_ref.dtype)
 
 
-def tile_products(rows, cols, count, grad, tiles, out_tiles):
+def tile_products(rows, cols, count, grad, early, tiles, out_tiles):
     slots, tile, _ = tiles.shape
     width = grad.shape[1]
     return pl.pallas_call(
         tile_kernel,
         out_shape=jax.ShapeDtypeStruct((out_tiles * tile // CHUNK, width, CHUNK), jnp.bfloat16),
-        in_specs=[HBM, HBM, pl.BlockSpec(memory_space=pltpu.SMEM), VMEM, HBM],
+        in_specs=[HBM, HBM, pl.BlockSpec(memory_space=pltpu.SMEM), VMEM, VMEM, HBM],
         out_specs=VMEM,
         scratch_shapes=[
-            pltpu.VMEM((slots, tile, tile), jnp.bfloat16),
+            pltpu.VMEM((slots - EARLY, tile, tile), jnp.bfloat16),
             pltpu.VMEM((out_tiles + 1, width, tile), jnp.float32),
             pltpu.SMEM(rows.shape, rows.dtype),
             pltpu.SMEM(cols.shape, cols.dtype),
-            pltpu.SemaphoreType.DMA((slots // GROUP,)),
+            pltpu.SemaphoreType.DMA(((slots - EARLY) // GROUP,)),
             pltpu.SemaphoreType.DMA((2,)),
         ],
         compiler_params=pltpu.CompilerParams(vmem_limit_bytes=28 << 20),
@@ -172,20 +199,22 @@
             transcendentals=0,
         ),
         name="tile_products",
-    )(rows, cols, count, grad, tiles)
+    )(rows, cols, count, grad, early, tiles)
 
 
 def flow_kernel(
     part_all, weight_hbm, feat_hbm, gf_ref, gw_out,
-    first, second, merged, half, y_in, whole, weight_raw, weight_send, weight_in, feat,
+    first, second, merged, half, y_in, late_in, late, whole, weight_raw, weight_send, weight_in, feat,
     gf_own, gf_send, gf_in, gw_ref, gw_send, mate_in, row_send, row_in, x_send,
-    load_sems, send_sems, recv_sems, x_sems, gw_sems,
+    load_sems, send_sems, recv_sems, x_sems, late_sems, gw_sems,
 ):
     row, col, fib = position()
     l, z = row // RING, lax.rem(row, RING)
     h, x = fib // RING, lax.rem(fib, RING)
     chunks, width, nodes_t = whole.shape[1:]
     pairs, span_t = chunks // 2, 2 * nodes_t
+    split = chunks - LATE
+    units = split + LATE // 2
     z_up, z_down, z_far = (lax.rem(z + d, RING) for d in (1, RING - 1, 2))
     to_z_up, to_z_down = (l * RING + z_up, col, fib), (l * RING + z_down, col, fib)
     to_x = [(row, col, h * RING + lax.rem(x + d, RING)) for d in range(RING)]
@@ -218,15 +247,27 @@
             source, target, send_sems.at[kind, t], recv_sems.at[kind, t], device_id=peer, device_id_type=MESH
         )
 
-    def link(kind, t):
+    def late_copy(to_z):
+        source = part_all.at[pl.ds(((1 - l) * RING + to_z) * chunks + split, LATE)]
+        return pltpu.make_async_remote_copy(
+            source, late_in.at[to_z], late_sems.at[0, to_z], late_sems.at[1, to_z], device_id=to_pair, device_id_type=MESH
+        )
+
+    def early_share(i, to_z, t):
+        return part_at(i, to_z, t)
+
+    def late_share(i, to_z, t):
+        return late.at[to_z, t - split, i]
+
+    def link(kind, t, share=early_share):
         if kind == 0:
-            return copy(0, t, part_at(0, z_far, t), first.at[0, t], to_z_up)
+            return copy(0, t, share(0, z_far, t), first.at[0, t], to_z_up)
         if kind == 1:
-            return copy(1, t, part_at(1, z_far, t), first.at[1, t], to_z_down)
+            return copy(1, t, share(1, z_far, t), first.at[1, t], to_z_down)
         if kind == 2:
-            return copy(2, t, part_at(1, z_up, t), second.at[0, t, 1], to_z_up)
+            return copy(2, t, share(1, z_up, t), second.at[0, t, 1], to_z_up)
         if kind == 3:
-            return copy(3, t, part_at(0, z_down, t), second.at[1, t, 0], to_z_down)
+            return copy(3, t, share(0, z_down, t), second.at[1, t, 0], to_z_down)
         if kind == 4:
             return copy(4, t, merged.at[0, t], second.at[0, t, 0], to_z_up)
         if kind == 5:
@@ -235,6 +276,9 @@
             return copy(6, t, half.at[t, 1 - l], y_in.at[0, t], to_pair)
         if kind == 7:
             return copy(7, t, half.at[t, 1 - l], y_in.at[1, t], to_cross)
+        if share is late_share:
+            both = whole.at[h, pl.ds(2 * t - split, 2)]
+            return copy(8, t, both, both, to_far)
         return copy(8, t, half.at[t, l], y_in.at[2, t], to_far)
 
     def along_x(kind, d, p, source, target):
@@ -256,11 +300,31 @@
         return functools.reduce(lambda a, b: a + b, terms)
 
     def send_shares(t):
-        for kind in range(4):
-            link(kind, t).start()
+        @pl.when(t < split)
+        def _():
+            for kind in range(4):
+                link(kind, t).start()
+
+        @pl.when(t == split)
+        def _():
+            for to_z in range(RING):
+                late_copy(to_z).wait_recv()
+
+        @pl.when(t >= split)
+        def _():
+            for to_z in (z_far, z_up, z_down, z):
+                for i in range(2):
+                    n = 2 * (t - split) + i
+                    late[to_z, t - split, i] = added(
+                        part_at(l, to_z, split + n), late_in.at[to_z, n]
+                    ).astype(late.dtype)
+            for kind in range(4):
+                link(kind, t, late_share).start()
 
         @pl.when(t == 0)
         def _():
+            for to_z in range(RING):
+                late_copy(to_z).start()
             for load in load_weight:
                 load.wait()
             for d in range(RING):
@@ -280,32 +344,53 @@
                 feat_copy(d, t).start()
 
     def merge(t):
-        link(0, t).wait_recv()
-        merged[0, t] = added(part_at(0, z_up, t), first.at[0, t]).astype(merged.dtype)
-        link(4, t).start()
-        link(1, t).wait_recv()
-        merged[1, t] = added(part_at(1, z_down, t), first.at[1, t]).astype(merged.dtype)
-        link(5, t).start()
+        def run(share):
+            link(0, t, share).wait_recv()
+            merged[0, t] = added(share(0, z_up, t), first.at[0, t]).astype(merged.dtype)
+            link(4, t, share).start()
+            link(1, t, share).wait_recv()
+            merged[1, t] = added(share(1, z_down, t), first.at[1, t]).astype(merged.dtype)
+            link(5, t, share).start()
+
+        pl.when(t < split)(lambda: run(early_share))
+        pl.when(t >= split)(lambda: run(late_share))
 
     def sum_over_z(t):
         for kind in (2, 3, 4, 5):
             link(kind, t).wait_recv()
-        for to_l in range(2):
-            half[t, to_l] = added(
-                part_at(to_l, z, t), second.at[0, t, to_l], second.at[1, t, to_l]
-            ).astype(half.dtype)
-        for kind in (6, 7, 8):
-            link(kind, t).start()
+
+        @pl.when(t < split)
+        def _():
+            for i in range(2):
+                half[t, i] = added(part_at(i, z, t), second.at[0, t, i], second.at[1, t, i]).astype(
+                    half.dtype
+                )
+            for kind in (6, 7, 8):
+                link(kind, t).start()
+
+        @pl.when(t >= split)
+        def _():
+            for i in range(2):
+                whole[h, 2 * t - split + i] = added(
+                    late.at[z, t - split, i], second.at[0, t, i], second.at[1, t, i]
+                ).astype(whole.dtype)
+            link(8, t, late_share).start()
 
     def sum_over_y(t):
-        for kind in (6, 7, 8):
-            link(kind, t).wait_recv()
-        whole[h, t] = added(half.at[t, l], y_in.at[0, t]).astype(whole.dtype)
-        whole[1 - h, t] = added(y_in.at[1, t], y_in.at[2, t]).astype(whole.dtype)
-
-        @pl.when(lax.rem(t, 2) == 1)
-        def _():
-            multiply(lax.div(t, 2))
+        @pl.when(t < split)
+        def _():
+            for kind in (6, 7, 8):
+                link(kind, t).wait_recv()
+            whole[h, t] = added(half.at[t, l], y_in.at[0, t]).astype(whole.dtype)
+            whole[1 - h, t] = added(y_in.at[1, t], y_in.at[2, t]).astype(whole.dtype)
+
+        @pl.when(t >= split)
+        def _():
+            link(8, t, late_share).wait_recv()
+
+        @pl.when((lax.rem(t, 2) == 1) | (t >= split))
+        def _():
+            multiply(jnp.where(t < split, lax.div(t, 2), t - split // 2))
 
     def multiply(p):
         @pl.when(p == 0)
@@ -336,12 +421,12 @@
 
     stages = (send_shares, merge, sum_over_z, sum_over_y)
 
-    @pl.loop(0, chunks + LAGS[-1])
+    @pl.loop(0, units + LAGS[-1])
     def _(step):
         for late, stage in zip(LAGS, stages):
             t = step - late
 
-            @pl.when((t >= 0) & (t < chunks))
+            @pl.when((t >= 0) & (t < units))
             def _(stage=stage, t=t):
                 stage(t)
 
@@ -383,10 +468,6 @@
             gives.append(gw_copy(2, d, x_send.at[d], gw_out.at[col, row, x], to_x[d]))
             gives[-1].start()
 
-    @pl.loop(pairs // 2, pairs)
-    def _(p):
-        collect(p)
-
     for d in range(1, RING):
         slot = gw_out.at[col, row, lax.rem(x + RING - d, RING)]
         gw_copy(2, d, slot, slot, to_x[d]).wait_recv()
@@ -394,10 +475,22 @@
         gives.append(gw_copy(3, d, gw_out.at[col, row], gw_out.at[col, row], peers[d - 1]))
         gives[-1].start()
 
-    @pl.loop(0, chunks)
+    @pl.loop(pairs // 2, pairs)
+    def _(p):
+        collect(p)
+
+    @pl.loop(0, split)
     def _(t):
         for kind in range(9):
             link(kind, t).wait_send()
+
+    @pl.loop(split, units)
+    def _(t):
+        for kind in (0, 1, 2, 3, 4, 5, 8):
+            link(kind, t, late_share).wait_send()
+
+    for to_z in range(RING):
+        late_copy(to_z).wait_send()
 
     @pl.loop(0, pairs)
     def _(p):
@@ -441,6 +534,8 @@
             pltpu.VMEM((2, chunks, *piece), sixteen),
             pltpu.VMEM((chunks, 2, *piece), sixteen),
             pltpu.VMEM((3, chunks, *piece), sixteen),
+            pltpu.VMEM((RING, LATE, *piece), sixteen),
+            pltpu.VMEM((RING, LATE // 2, 2, *piece), sixteen),
             pltpu.VMEM((2, chunks, *piece), sixteen),
             pltpu.VMEM((2 * RING, width, width), sixteen),
             pltpu.VMEM((RING - 1, width, 2 * width), sixteen),
@@ -459,6 +554,7 @@
             pltpu.SemaphoreType.DMA((9, chunks)),
             pltpu.SemaphoreType.DMA((9, chunks)),
             pltpu.SemaphoreType.DMA((2, 3, RING, pairs)),
+            pltpu.SemaphoreType.DMA((2, RING)),
             pltpu.SemaphoreType.DMA((4, 2, 8)),
         ],
         compiler_params=pltpu.CompilerParams(
@@ -505,13 +601,13 @@
 
 
 def on_device(features, pre_activation, out_grad, weight, tiles, rows, cols, counts):
-    tile = tiles.shape[-1]
     features, pre_activation, out_grad, weight, tiles, rows, cols = (
         pltpu.with_memory_space_constraint(a, pltpu.HBM)
         for a in (features, pre_activation, out_grad, weight, tiles[0, 0], rows, cols)
     )
-    grad = local_grads(pre_activation, out_grad, tile)
-    part = tile_products(rows, cols, counts, grad, tiles, 8 * (features.shape[0] // tile))
+    grad, early = local_grads(pre_activation, out_grad, tiles)
+    out_tiles = 8 * (features.shape[0] // tiles.shape[1])
+    part = tile_products(rows, cols, counts, grad, early, tiles, out_tiles)
     return finish(*flow(part, weight, features))
 
 

time: 79.7 us -> 79.2 us (level)
  no operation moved by 1% of the time
where the time goes in v6:
time: 79.2 us; the launch traced here: 79.1 us
  Pallas kernels  77.8 us (98%)
  between operations  1.3 us (2%)
    pallas_call x1, Pallas kernels, flow(): pl.pallas_call(flow_kernel, out_shape=(jax.ShapeDtypeStruct((nodes, width...  68.7 us
    pallas_call x1, Pallas kernels, local_grads(): pl.pallas_call(grad_kernel, out_shape=(jax.ShapeDtypeStruct((2 * own_tile...  4.46 us
    pallas_call x1, Pallas kernels, tile_products(): pl.pallas_call(tile_kernel, out_shape=jax.ShapeDtypeStruct((out_tiles * t...  3.65 us

profile of v6, /device:TPU:1, one launch (start us, length us, event | category | flops | bytes accessed | tf_op | source)
XLA Modules:
  0.0 79.1 jit_solution(3091823256843010652)
XLA Ops:
  1.3 4.5 %local_grads.1 = (bf16[16,128,256]{2,1,0:T(8,128)(2,1)S(1)}, bf16[64,256,256]{2,1,0:T(8,128)(2,1)S(1)}) custom-call(bf16[2048,128]{1,0:T(8,128)(2,1)} %pre_hbm.1, bf16[2048,128]{1,0:T(8,128)(2,1)} %out_grad_hbm.1, bf16[128,256,256]{2,1,0:T(8,128)(2,1)} %bitcast.1), custom_call_target="tpu_custom_call" | custom-call | flops 2621440 | bytes 2097152 | tf_op jit(solution)/shard_map/local_grads/pallas_call | solution.py:94
  5.7 3.6 %tile_products.1.part_all = bf16[128,128,128]{2,1,0:T(8,128)(2,1)S(1)} custom-call(s32[1,1,128]{2,1,0:T(1,128)} %rows_hbm.1, s32[1,1,128]{2,1,0:T(1,128)} %cols_hbm.1, s32[1,1]{1,0:T(1,128)S(6)} %copy.10.count_ref, bf16[16,128,256]{2,1,0:T(8,128)(2,1)S(1)} %get-tuple-element.6.grad_ref, bf16[64,256,256]{2,1,0:T(8,128)(2,1)S(1)} %get-tuple-element.7.early_ref, ...), custom_call_target="tpu_custom_call" | custom-call | flops 2147483648 | bytes 16777216 | tf_op jit(solution)/shard_map/tile_products/pallas_call | solution.py:182
  9.4 68.7 %flow.1 = (bf16[2048,128]{1,0:T(8,128)(2,1)S(1)}, bf16[2,8,4,16,128]{4,3,2,1,0:T(8,128)(2,1)S(1)}) custom-call(bf16[128,128,128]{2,1,0:T(8,128)(2,1)S(1)} %tile_products.1.part_all, bf16[128,1024]{1,0:T(8,128)(2,1)} %weight_hbm.1, bf16[2048,128]{1,0:T(8,128)(2,1)} %feat_hbm.1), custom_call_target="tpu_custom_call" | custom-call | flops 1073741824 | bytes 16777216 | tf_op jit(solution)/shard_map/flow/pallas_call | solution.py:523
  78.1 1.0 %finish.1 = (bf16[2048,128]{1,0:T(8,128)(2,1)}, f32[128,1024]{1,0:T(8,128)}) custom-call(bf16[2048,128]{1,0:T(8,128)(2,1)S(1)} %get-tuple-element.8.gf_ref, bf16[2,8,4,16,128]{4,3,2,1,0:T(8,128)(2,1)S(1)} %get-tuple-element.9.gw_ref), custom_call_target="tpu_custom_call" | custom-call | bytes 1048576 | tf_op jit(solution)/shard_map/finish/pallas_call | solution.py:588

commit v7 on v6

--- a/solution.py
+++ b/solution.py
@@ -8,9 +8,9 @@
 from jax.sharding import PartitionSpec as P
 
 GROUP = 8
-EARLY = 64
+EARLY = 24
 RING = 4
-LAGS = (0, 2, 4, 6)
+LAGS = (0, 2, 5, 8, 4)
 MESH = pl.DeviceIdType.MESH
 VMEM = pl.BlockSpec(memory_space=pltpu.VMEM)
 HBM = pl.BlockSpec(memory_space=pltpu.HBM)
@@ -146,7 +146,7 @@
     def _(g):
         copy(g).start()
 
-    @pl.loop(0, out_tiles + 1)
+    @pl.loop(0, out_tiles + 1, unroll=5)
     def _(t):
         total[t] = jnp.zeros(total.shape[1:], total.dtype)
 
@@ -170,7 +170,7 @@
         copy(g).wait()
         add_group(g, lambda slot: held[slot - EARLY])
 
-    @pl.loop(0, out_tiles)
+    @pl.loop(0, out_tiles, unroll=4)
     def _(t):
         for cut in range(cuts):
             out_ref[t * cuts + cut] = total[t, :, cut * CHUNK : (cut + 1) * CHUNK].astype(out_ref.dtype)
@@ -281,10 +281,20 @@
             return copy(8, t, both, both, to_far)
         return copy(8, t, half.at[t, l], y_in.at[2, t], to_far)
 
-    def along_x(kind, d, p, source, target):
+    def along_x(kind, d, p, source, target, peer=None):
         return pltpu.make_async_remote_copy(
-            source, target, x_sems.at[0, kind, d, p], x_sems.at[1, kind, d, p], device_id=to_x[d], device_id_type=MESH
-        )
+            source,
+            target,
+            x_sems.at[0, kind, d, p],
+            x_sems.at[1, kind, d, p],
+            device_id=to_x[d] if peer is None else peer,
+            device_id_type=MESH,
+        )
+
+    def feat_pass(up, p):
+        part = pl.ds(pl.multiple_of(p * span_t + (0 if up else nodes_t), nodes_t), nodes_t)
+        source = feat.at[RING - 1 if up else 1, part]
+        return along_x(0, 2 if up else 0, p, source, feat.at[2, part], to_x[1 if up else RING - 1])
 
     def feat_copy(d, p):
         return along_x(0, d, p, feat.at[0, nodes_of(p)], feat.at[RING - d, nodes_of(p)])
@@ -340,8 +350,16 @@
 
         @pl.when(t < pairs)
         def _():
-            for d in range(1, RING):
+            for d in (1, RING - 1):
                 feat_copy(d, t).start()
+
+    def pass_on(t):
+        @pl.when(t < pairs)
+        def _():
+            feat_copy(1, t).wait_recv()
+            feat_pass(True, t).start()
+            feat_copy(RING - 1, t).wait_recv()
+            feat_pass(False, t).start()
 
     def merge(t):
         def run(share):
@@ -401,8 +419,8 @@
         panel = jnp.concatenate(
             [whole[:, 2 * p].reshape(2 * width, nodes_t), whole[:, 2 * p + 1].reshape(2 * width, nodes_t)], axis=1
         )
-        for d in range(1, RING):
-            feat_copy(d, p).wait_recv()
+        for up in (True, False):
+            feat_pass(up, p).wait_recv()
         beside = jnp.concatenate([feat[d, nodes_of(p), :] for d in range(RING)], axis=1)
         gw_ref[...] += jnp.dot(panel, beside, preferred_element_type=jnp.float32)
         for d in (2, 1, 3, 0):
@@ -419,9 +437,9 @@
         block = gf_own[p] + added(*[gf_in.at[d - 1, p] for d in range(1, RING)])
         gf_ref[nodes_of(p), :] = block.T.astype(gf_ref.dtype)
 
-    stages = (send_shares, merge, sum_over_z, sum_over_y)
-
-    @pl.loop(0, units + LAGS[-1])
+    stages = (send_shares, merge, sum_over_z, sum_over_y, pass_on)
+
+    @pl.loop(0, units + max(LAGS))
     def _(step):
         for late, stage in zip(LAGS, stages):
             t = step - late
@@ -454,6 +472,19 @@
     @pl.loop(0, pairs // 2)
     def _(p):
         collect(p)
+
+    @pl.loop(0, split)
+    def _(t):
+        for kind in range(9):
+            link(kind, t).wait_send()
+
+    @pl.loop(split, units)
+    def _(t):
+        for kind in (0, 1, 2, 3, 4, 5, 8):
+            link(kind, t, late_share).wait_send()
+
+    for to_z in range(RING):
+        late_copy(to_z).wait_send()
 
     own = gw_ref[pl.ds(pl.multiple_of(row * rows, rows), rows), :]
     for d in range(1, 8):
@@ -479,23 +510,13 @@
     def _(p):
         collect(p)
 
-    @pl.loop(0, split)
-    def _(t):
-        for kind in range(9):
-            link(kind, t).wait_send()
-
-    @pl.loop(split, units)
-    def _(t):
-        for kind in (0, 1, 2, 3, 4, 5, 8):
-            link(kind, t, late_share).wait_send()
-
-    for to_z in range(RING):
-        late_copy(to_z).wait_send()
-
     @pl.loop(0, pairs)
     def _(p):
+        for up in (True, False):
+            feat_pass(up, p).wait_send()
+        for d in (1, RING - 1):
+            feat_copy(d, p).wait_send()
         for d in range(1, RING):
-            feat_copy(d, p).wait_send()
             gf_copy(d, p).wait_send()
 
     for d in range(1, RING):

time: 79.2 us -> 75.5 us (0.953)
  Pallas kernels: 77.8 us -> 74.1 us
    pallas_call x1, Pallas kernels: 68.7 us -> 64.9 us  [flow(): pl.pallas_call(flow_kernel, out_shape=(jax.ShapeDtypeStruct((nodes, width...]
where the time goes in v7:
time: 75.5 us; the launch traced here: 75.4 us
  Pallas kernels  74.1 us (98%)
  between operations  1.3 us (2%)
    pallas_call x1, Pallas kernels, flow(): pl.pallas_call(flow_kernel, out_shape=(jax.ShapeDtypeStruct((nodes, width...  64.9 us
    pallas_call x1, Pallas kernels, local_grads(): pl.pallas_call(grad_kernel, out_shape=(jax.ShapeDtypeStruct((2 * own_tile...  4.41 us
    pallas_call x1, Pallas kernels, tile_products(): pl.pallas_call(tile_kernel, out_shape=jax.ShapeDtypeStruct((out_tiles * t...  3.85 us

profile of v7, /device:TPU:1, one launch (start us, length us, event | category | flops | bytes accessed | tf_op | source)
XLA Modules:
  0.0 75.4 jit_solution(14434979438270008673)
XLA Ops:
  1.3 4.4 %local_grads.1 = (bf16[16,128,256]{2,1,0:T(8,128)(2,1)S(1)}, bf16[24,256,256]{2,1,0:T(8,128)(2,1)S(1)}) custom-call(bf16[2048,128]{1,0:T(8,128)(2,1)} %pre_hbm.1, bf16[2048,128]{1,0:T(8,128)(2,1)} %out_grad_hbm.1, bf16[128,256,256]{2,1,0:T(8,128)(2,1)} %bitcast.1), custom_call_target="tpu_custom_call" | custom-call | flops 2621440 | bytes 2097152 | tf_op jit(solution)/shard_map/local_grads/pallas_call | solution.py:94
  5.7 3.8 %tile_products.1.part_all = bf16[128,128,128]{2,1,0:T(8,128)(2,1)S(1)} custom-call(s32[1,1,128]{2,1,0:T(1,128)} %rows_hbm.1, s32[1,1,128]{2,1,0:T(1,128)} %cols_hbm.1, s32[1,1]{1,0:T(1,128)S(6)} %copy.10.count_ref, bf16[16,128,256]{2,1,0:T(8,128)(2,1)S(1)} %get-tuple-element.6.grad_ref, bf16[24,256,256]{2,1,0:T(8,128)(2,1)S(1)} %get-tuple-element.7.early_ref, ...), custom_call_target="tpu_custom_call" | custom-call | flops 2147483648 | bytes 16777216 | tf_op jit(solution)/shard_map/tile_products/pallas_call | solution.py:182
  9.6 64.9 %flow.1 = (bf16[2048,128]{1,0:T(8,128)(2,1)S(1)}, bf16[2,8,4,16,128]{4,3,2,1,0:T(8,128)(2,1)S(1)}) custom-call(bf16[128,128,128]{2,1,0:T(8,128)(2,1)S(1)} %tile_products.1.part_all, bf16[128,1024]{1,0:T(8,128)(2,1)} %weight_hbm.1, bf16[2048,128]{1,0:T(8,128)(2,1)} %feat_hbm.1), custom_call_target="tpu_custom_call" | custom-call | flops 1073741824 | bytes 16777216 | tf_op jit(solution)/shard_map/flow/pallas_call | solution.py:544
  74.4 1.0 %finish.1 = (bf16[2048,128]{1,0:T(8,128)(2,1)}, f32[128,1024]{1,0:T(8,128)}) custom-call(bf16[2048,128]{1,0:T(8,128)(2,1)S(1)} %get-tuple-element.8.gf_ref, bf16[2,8,4,16,128]{4,3,2,1,0:T(8,128)(2,1)S(1)} %get-tuple-element.9.gw_ref), custom_call_target="tpu_custom_call" | custom-call | bytes 1048576 | tf_op jit(solution)/shard_map/finish/pallas_call | solution.py:609

commit v8 on v7

--- a/solution.py
+++ b/solution.py
@@ -7,8 +7,8 @@
 from jax.experimental.pallas import tpu as pltpu
 from jax.sharding import PartitionSpec as P
 
-GROUP = 8
-EARLY = 24
+GROUP = 16
+EARLY = 48
 RING = 4
 LAGS = (0, 2, 5, 8, 4)
 MESH = pl.DeviceIdType.MESH
@@ -408,21 +408,31 @@
 
         @pl.when((lax.rem(t, 2) == 1) | (t >= split))
         def _():
-            multiply(jnp.where(t < split, lax.div(t, 2), t - split // 2))
-
-    def multiply(p):
-        @pl.when(p == 0)
-        def _():
-            for d in range(1, RING):
-                weight_copy(d).wait_recv()
-
-        panel = jnp.concatenate(
-            [whole[:, 2 * p].reshape(2 * width, nodes_t), whole[:, 2 * p + 1].reshape(2 * width, nodes_t)], axis=1
-        )
+            p = jnp.where(t < split, lax.div(t, 2), t - split // 2)
+            multiply_features(p)
+
+            @pl.when(p < pairs - 1)
+            def _():
+                multiply_weight(p)
+
+    def panel_of(p):
+        return jnp.concatenate(
+            [whole[:, 2 * p + i].reshape(2 * width, nodes_t) for i in range(2)], axis=1
+        )
+
+    def multiply_features(p):
         for up in (True, False):
             feat_pass(up, p).wait_recv()
         beside = jnp.concatenate([feat[d, nodes_of(p), :] for d in range(RING)], axis=1)
-        gw_ref[...] += jnp.dot(panel, beside, preferred_element_type=jnp.float32)
+        gw_ref[...] += jnp.dot(panel_of(p), beside, preferred_element_type=jnp.float32)
+
+    def multiply_weight(p):
+        @pl.when(p == 0)
+        def _():
+            for d in range(1, RING):
+                weight_copy(d).wait_recv()
+
+        panel = panel_of(p)
         for d in (2, 1, 3, 0):
             block = jnp.dot(weight_in[d], panel, preferred_element_type=jnp.float32)
             if d == 0:
@@ -461,6 +471,7 @@
     gw_send[...] = gw_ref[pl.ds(pl.multiple_of((1 - col) * width, width), width), :].astype(gw_send.dtype)
     gives = [gw_copy(0, 0, gw_send, mate_in, mate)]
     gives[0].start()
+    multiply_weight(pairs - 1)
     gives[0].wait_recv()
     mine = gw_ref[pl.ds(pl.multiple_of(col * width, width), width), :] + mate_in[...].astype(jnp.float32)
     gw_ref[0:width, :] = mine

time: 75.5 us -> 75.1 us (level)
    pallas_call x1, Pallas kernels: 3.85 us -> 2.2 us  [tile_products(): pl.pallas_call(tile_kernel, out_shape=jax.ShapeDtypeStruct((out_tiles * t...]
    pallas_call x1, Pallas kernels: 64.9 us -> 66.1 us  [flow(): pl.pallas_call(flow_kernel, out_shape=(jax.ShapeDtypeStruct((nodes, width...]
where the time goes in v8:
time: 75.1 us; the launch traced here: 75 us
  Pallas kernels  73.7 us (98%)
  between operations  1.3 us (2%)
    pallas_call x1, Pallas kernels, flow(): pl.pallas_call(flow_kernel, out_shape=(jax.ShapeDtypeStruct((nodes, width...  66.1 us
    pallas_call x1, Pallas kernels, local_grads(): pl.pallas_call(grad_kernel, out_shape=(jax.ShapeDtypeStruct((2 * own_tile...  4.41 us
    pallas_call x1, Pallas kernels, tile_products(): pl.pallas_call(tile_kernel, out_shape=jax.ShapeDtypeStruct((out_tiles * t...  2.2 us

profile of v8, /device:TPU:1, one launch (start us, length us, event | category | flops | bytes accessed | tf_op | source)
XLA Modules:
  0.0 75.0 jit_solution(11956341522546374359)
XLA Ops:
  1.3 4.4 %local_grads.1 = (bf16[16,128,256]{2,1,0:T(8,128)(2,1)S(1)}, bf16[48,256,256]{2,1,0:T(8,128)(2,1)S(1)}) custom-call(bf16[2048,128]{1,0:T(8,128)(2,1)} %pre_hbm.1, bf16[2048,128]{1,0:T(8,128)(2,1)} %out_grad_hbm.1, bf16[128,256,256]{2,1,0:T(8,128)(2,1)} %bitcast.1), custom_call_target="tpu_custom_call" | custom-call | flops 2621440 | bytes 2097152 | tf_op jit(solution)/shard_map/local_grads/pallas_call | solution.py:94
  5.7 2.2 %tile_products.1.part_all = bf16[128,128,128]{2,1,0:T(8,128)(2,1)S(1)} custom-call(s32[1,1,128]{2,1,0:T(1,128)} %rows_hbm.1, s32[1,1,128]{2,1,0:T(1,128)} %cols_hbm.1, s32[1,1]{1,0:T(1,128)S(6)} %copy.10.count_ref, bf16[16,128,256]{2,1,0:T(8,128)(2,1)S(1)} %get-tuple-element.6.grad_ref, bf16[48,256,256]{2,1,0:T(8,128)(2,1)S(1)} %get-tuple-element.7.early_ref, ...), custom_call_target="tpu_custom_call" | custom-call | flops 2147483648 | bytes 16777216 | tf_op jit(solution)/shard_map/tile_products/pallas_call | solution.py:182
  7.9 66.1 %flow.1 = (bf16[2048,128]{1,0:T(8,128)(2,1)S(1)}, bf16[2,8,4,16,128]{4,3,2,1,0:T(8,128)(2,1)S(1)}) custom-call(bf16[128,128,128]{2,1,0:T(8,128)(2,1)S(1)} %tile_products.1.part_all, bf16[128,1024]{1,0:T(8,128)(2,1)} %weight_hbm.1, bf16[2048,128]{1,0:T(8,128)(2,1)} %feat_hbm.1), custom_call_target="tpu_custom_call" | custom-call | flops 1073741824 | bytes 16777216 | tf_op jit(solution)/shard_map/flow/pallas_call | solution.py:555
  74.0 1.0 %finish.1 = (bf16[2048,128]{1,0:T(8,128)(2,1)}, f32[128,1024]{1,0:T(8,128)}) custom-call(bf16[2048,128]{1,0:T(8,128)(2,1)S(1)} %get-tuple-element.8.gf_ref, bf16[2,8,4,16,128]{4,3,2,1,0:T(8,128)(2,1)S(1)} %get-tuple-element.9.gw_ref), custom_call_target="tpu_custom_call" | custom-call | bytes 1048576 | tf_op jit(solution)/shard_map/finish/pallas_call | solution.py:620

commit v9 on v8

--- a/solution.py
+++ b/solution.py
@@ -30,7 +30,7 @@
 
 
 def grad_kernel(
-    pre_hbm, out_grad_hbm, tiles_hbm, grad_ref, early_ref,
+    pre_hbm, out_grad_hbm, tiles_hbm, grad_ref, early_ref, sums_ref,
     pre_ref, out_grad_ref, load_sems, tile_sems, send_sems, recv_sems,
 ):
     row, col, fib = position()
@@ -77,6 +77,10 @@
         grad_ref[col * own_tiles + t] = grad.T.astype(grad_ref.dtype)
         copy(t, col).start()
 
+    @pl.loop(0, sums_ref.shape[0], unroll=5)
+    def _(t):
+        sums_ref[t] = jnp.zeros(sums_ref.shape[1:], sums_ref.dtype)
+
     @pl.loop(0, own_tiles)
     def _(t):
         copy(t, col).wait_send()
@@ -87,7 +91,7 @@
         early(g).wait()
 
 
-def local_grads(pre, out_grad, tiles):
+def local_grads(pre, out_grad, tiles, out_tiles):
     nodes, width = pre.shape
     tile = tiles.shape[1]
     own_tiles = nodes // tile
@@ -96,9 +100,10 @@
         out_shape=(
             jax.ShapeDtypeStruct((2 * own_tiles, width, tile), jnp.bfloat16),
             jax.ShapeDtypeStruct((EARLY, tile, tile), tiles.dtype),
+            jax.ShapeDtypeStruct((out_tiles + 1, width, tile), jnp.float32),
         ),
         in_specs=[HBM, HBM, HBM],
-        out_specs=(VMEM, VMEM),
+        out_specs=(VMEM, VMEM, VMEM),
         scratch_shapes=[
             pltpu.VMEM(pre.shape, pre.dtype),
             pltpu.VMEM(pre.shape, pre.dtype),
@@ -118,8 +123,8 @@
 
 
 def tile_kernel(
-    rows_hbm, cols_hbm, count_ref, grad_ref, early_ref, tiles_ref, out_ref,
-    held, total, rows_ref, cols_ref, sems, index_sems,
+    rows_hbm, cols_hbm, count_ref, grad_ref, early_ref, sums_ref, tiles_ref, out_ref, total,
+    held, rows_ref, cols_ref, sems, index_sems,
 ):
     slots, tile, _ = tiles_ref.shape
     cuts = tile // CHUNK
@@ -146,10 +151,6 @@
     def _(g):
         copy(g).start()
 
-    @pl.loop(0, out_tiles + 1, unroll=5)
-    def _(t):
-        total[t] = jnp.zeros(total.shape[1:], total.dtype)
-
     for load in indices:
         load.wait()
 
@@ -176,17 +177,20 @@
             out_ref[t * cuts + cut] = total[t, :, cut * CHUNK : (cut + 1) * CHUNK].astype(out_ref.dtype)
 
 
-def tile_products(rows, cols, count, grad, early, tiles, out_tiles):
+def tile_products(rows, cols, count, grad, early, sums, tiles, out_tiles):
     slots, tile, _ = tiles.shape
     width = grad.shape[1]
     return pl.pallas_call(
         tile_kernel,
-        out_shape=jax.ShapeDtypeStruct((out_tiles * tile // CHUNK, width, CHUNK), jnp.bfloat16),
-        in_specs=[HBM, HBM, pl.BlockSpec(memory_space=pltpu.SMEM), VMEM, VMEM, HBM],
-        out_specs=VMEM,
+        out_shape=(
+            jax.ShapeDtypeStruct((out_tiles * tile // CHUNK, width, CHUNK), jnp.bfloat16),
+            jax.ShapeDtypeStruct(sums.shape, sums.dtype),
+        ),
+        input_output_aliases={5: 1},
+        in_specs=[HBM, HBM, pl.BlockSpec(memory_space=pltpu.SMEM), VMEM, VMEM, VMEM, HBM],
+        out_specs=(VMEM, VMEM),
         scratch_shapes=[
             pltpu.VMEM((slots - EARLY, tile, tile), jnp.bfloat16),
-            pltpu.VMEM((out_tiles + 1, width, tile), jnp.float32),
             pltpu.SMEM(rows.shape, rows.dtype),
             pltpu.SMEM(cols.shape, cols.dtype),
             pltpu.SemaphoreType.DMA(((slots - EARLY) // GROUP,)),
@@ -199,7 +203,7 @@
             transcendentals=0,
         ),
         name="tile_products",
-    )(rows, cols, count, grad, early, tiles)
+    )(rows, cols, count, grad, early, sums, tiles)[0]
 
 
 def flow_kernel(
@@ -401,6 +405,8 @@
                 link(kind, t).wait_recv()
             whole[h, t] = added(half.at[t, l], y_in.at[0, t]).astype(whole.dtype)
             whole[1 - h, t] = added(y_in.at[1, t], y_in.at[2, t]).astype(whole.dtype)
+            for kind in range(9):
+                link(kind, t).wait_send()
 
         @pl.when(t >= split)
         def _():
@@ -484,18 +490,13 @@
     def _(p):
         collect(p)
 
-    @pl.loop(0, split)
-    def _(t):
-        for kind in range(9):
-            link(kind, t).wait_send()
+    for to_z in range(RING):
+        late_copy(to_z).wait_send()
 
     @pl.loop(split, units)
     def _(t):
         for kind in (0, 1, 2, 3, 4, 5, 8):
             link(kind, t, late_share).wait_send()
-
-    for to_z in range(RING):
-        late_copy(to_z).wait_send()
 
     own = gw_ref[pl.ds(pl.multiple_of(row * rows, rows), rows), :]
     for d in range(1, 8):
@@ -532,13 +533,19 @@
 
     for d in range(1, RING):
         weight_copy(d).wait_send()
+    def hand_on(d, of_col):
+        slot = gw_out.at[of_col, lax.rem(row + 8 - d, 8)]
+        return gw_copy(4, d, slot, slot, mate)
+
+    gives.append(hand_on(0, col))
+    gives[-1].start()
     for d in range(1, 8):
         slot = gw_out.at[col, lax.rem(row + 8 - d, 8)]
         gw_copy(3, d, slot, slot, peers[d - 1]).wait_recv()
-    gives.append(gw_copy(0, 1, gw_out.at[col], gw_out.at[col], mate))
-    gives[-1].start()
-    slot = gw_out.at[1 - col]
-    gw_copy(0, 1, slot, slot, mate).wait_recv()
+        gives.append(hand_on(d, col))
+        gives[-1].start()
+    for d in range(8):
+        hand_on(d, 1 - col).wait_recv()
     for give in gives:
         give.wait_send()
 
@@ -587,7 +594,7 @@
             pltpu.SemaphoreType.DMA((9, chunks)),
             pltpu.SemaphoreType.DMA((2, 3, RING, pairs)),
             pltpu.SemaphoreType.DMA((2, RING)),
-            pltpu.SemaphoreType.DMA((4, 2, 8)),
+            pltpu.SemaphoreType.DMA((5, 2, 8)),
         ],
         compiler_params=pltpu.CompilerParams(
             collective_id=1, has_side_effects=True, vmem_limit_bytes=24 << 20
@@ -637,9 +644,9 @@
         pltpu.with_memory_space_constraint(a, pltpu.HBM)
         for a in (features, pre_activation, out_grad, weight, tiles[0, 0], rows, cols)
     )
-    grad, early = local_grads(pre_activation, out_grad, tiles)
     out_tiles = 8 * (features.shape[0] // tiles.shape[1])
-    part = tile_products(rows, cols, counts, grad, early, tiles, out_tiles)
+    grad, early, sums = local_grads(pre_activation, out_grad, tiles, out_tiles)
+    part = tile_products(rows, cols, counts, grad, early, sums, tiles, out_tiles)
     return finish(*flow(part, weight, features))
 
 

time: 75.1 us -> 76 us (1.012)
  Pallas kernels: 73.7 us -> 74.5 us
    pallas_call x1, Pallas kernels: 2.2 us -> 3.18 us  [tile_products(): pl.pallas_call(tile_kernel, out_shape=(jax.ShapeDtypeStruct((out_tiles *...]
where the time goes in v9:
time: 76 us; the launch traced here: 75.8 us
  Pallas kernels  74.5 us (98%)
  between operations  1.3 us (2%)
    pallas_call x1, Pallas kernels, flow(): pl.pallas_call(flow_kernel, out_shape=(jax.ShapeDtypeStruct((nodes, width...  66 us
    pallas_call x1, Pallas kernels, local_grads(): pl.pallas_call(grad_kernel, out_shape=(jax.ShapeDtypeStruct((2 * own_tile...  4.41 us
    pallas_call x1, Pallas kernels, tile_products(): pl.pallas_call(tile_kernel, out_shape=(jax.ShapeDtypeStruct((out_tiles *...  3.18 us

profile of v9, /device:TPU:1, one launch (start us, length us, event | category | flops | bytes accessed | tf_op | source)
XLA Modules:
  0.0 75.8 jit_solution(8177688884647522065)
XLA Ops:
  1.3 4.4 %local_grads.1 = (bf16[16,128,256]{2,1,0:T(8,128)(2,1)S(1)}, bf16[48,256,256]{2,1,0:T(8,128)(2,1)S(1)}, f32[65,128,256]{2,1,0:T(8,128)S(1)}) custom-call(bf16[2048,128]{1,0:T(8,128)(2,1)} %pre_hbm.1, bf16[2048,128]{1,0:T(8,128)(2,1)} %out_grad_hbm.1, bf16[128,256,256]{2,1,0:T(8,128)(2,1)} %bitcast.1), custom_call_target="tpu_custom_call" | custom-call | flops 2621440 | bytes 2097152 | tf_op jit(solution)/shard_map/local_grads/pallas_call | solution.py:98
  5.7 3.2 %tile_products.1 = (bf16[128,128,128]{2,1,0:T(8,128)(2,1)S(1)}, f32[65,128,256]{2,1,0:T(8,128)S(1)}) custom-call(s32[1,1,128]{2,1,0:T(1,128)} %rows_hbm.1, s32[1,1,128]{2,1,0:T(1,128)} %cols_hbm.1, s32[1,1]{1,0:T(1,128)S(6)} %copy.12.count_ref, bf16[16,128,256]{2,1,0:T(8,128)(2,1)S(1)} %get-tuple-element.8.grad_ref, ...), custom_call_target="tpu_custom_call", output_to_operand_aliasing={{1}: (5, {})} | custom-call | flops 2147483648 | bytes 16777216 | tf_op jit(solution)/shard_map/tile_products/pallas_call | solution.py:183
  8.9 66.0 %flow.1 = (bf16[2048,128]{1,0:T(8,128)(2,1)S(1)}, bf16[2,8,4,16,128]{4,3,2,1,0:T(8,128)(2,1)S(1)}) custom-call(bf16[128,128,128]{2,1,0:T(8,128)(2,1)S(1)} %get-tuple-element.11.part_all, bf16[128,1024]{1,0:T(8,128)(2,1)} %weight_hbm.1, bf16[2048,128]{1,0:T(8,128)(2,1)} %feat_hbm.1), custom_call_target="tpu_custom_call" | custom-call | flops 1073741824 | bytes 16777216 | tf_op jit(solution)/shard_map/flow/pallas_call | solution.py:562
  74.9 1.0 %finish.1 = (bf16[2048,128]{1,0:T(8,128)(2,1)}, f32[128,1024]{1,0:T(8,128)}) custom-call(bf16[2048,128]{1,0:T(8,128)(2,1)S(1)} %get-tuple-element.12.gf_ref, bf16[2,8,4,16,128]{4,3,2,1,0:T(8,128)(2,1)S(1)} %get-tuple-element.13.gw_ref), custom_call_target="tpu_custom_call" | custom-call | bytes 1048576 | tf_op jit(solution)/shard_map/finish/pallas_call | solution.py:627

commit v10 on v9

--- a/solution.py
+++ b/solution.py
@@ -14,6 +14,7 @@
 MESH = pl.DeviceIdType.MESH
 VMEM = pl.BlockSpec(memory_space=pltpu.VMEM)
 HBM = pl.BlockSpec(memory_space=pltpu.HBM)
+SMEM = pl.BlockSpec(memory_space=pltpu.SMEM)
 CHUNK = 128
 LATE = 4
 
@@ -30,8 +31,9 @@
 
 
 def grad_kernel(
-    pre_hbm, out_grad_hbm, tiles_hbm, grad_ref, early_ref, sums_ref,
-    pre_ref, out_grad_ref, load_sems, tile_sems, send_sems, recv_sems,
+    pre_hbm, out_grad_hbm, tiles_hbm, rows_hbm, cols_hbm,
+    grad_ref, early_ref, sums_ref, rows_ref, cols_ref,
+    pre_ref, out_grad_ref, load_sems, tile_sems, index_sems, send_sems, recv_sems,
 ):
     row, col, fib = position()
     own_tiles = grad_ref.shape[0] // 2
@@ -58,6 +60,12 @@
     def _(g):
         early(g).start()
 
+    indices = [
+        pltpu.make_async_copy(source, target, index_sems.at[i])
+        for i, (source, target) in enumerate(((rows_hbm, rows_ref), (cols_hbm, cols_ref)))
+    ]
+    for load in indices:
+        load.start()
     greet([partner])
 
     def copy(t, owner):
@@ -90,8 +98,11 @@
     def _(g):
         early(g).wait()
 
-
-def local_grads(pre, out_grad, tiles, out_tiles):
+    for load in indices:
+        load.wait()
+
+
+def local_grads(pre, out_grad, tiles, rows, cols, out_tiles):
     nodes, width = pre.shape
     tile = tiles.shape[1]
     own_tiles = nodes // tile
@@ -101,14 +112,17 @@
             jax.ShapeDtypeStruct((2 * own_tiles, width, tile), jnp.bfloat16),
             jax.ShapeDtypeStruct((EARLY, tile, tile), tiles.dtype),
             jax.ShapeDtypeStruct((out_tiles + 1, width, tile), jnp.float32),
-        ),
-        in_specs=[HBM, HBM, HBM],
-        out_specs=(VMEM, VMEM, VMEM),
+            jax.ShapeDtypeStruct(rows.shape, rows.dtype),
+            jax.ShapeDtypeStruct(cols.shape, cols.dtype),
+        ),
+        in_specs=[HBM] * 5,
+        out_specs=(VMEM, VMEM, VMEM, SMEM, SMEM),
         scratch_shapes=[
             pltpu.VMEM(pre.shape, pre.dtype),
             pltpu.VMEM(pre.shape, pre.dtype),
             pltpu.SemaphoreType.DMA((2, own_tiles)),
             pltpu.SemaphoreType.DMA((EARLY // GROUP,)),
+            pltpu.SemaphoreType.DMA((2,)),
             pltpu.SemaphoreType.DMA((own_tiles,)),
             pltpu.SemaphoreType.DMA((own_tiles,)),
         ],
@@ -119,12 +133,12 @@
             flops=10 * nodes * width, bytes_accessed=8 * nodes * width, transcendentals=nodes * width
         ),
         name="local_grads",
-    )(pre, out_grad, tiles)
+    )(pre, out_grad, tiles, rows, cols)
 
 
 def tile_kernel(
-    rows_hbm, cols_hbm, count_ref, grad_ref, early_ref, sums_ref, tiles_ref, out_ref, total,
-    held, rows_ref, cols_ref, sems, index_sems,
+    rows_ref, cols_ref, count_ref, grad_ref, early_ref, sums_ref, tiles_ref, out_ref, total,
+    held, sems,
 ):
     slots, tile, _ = tiles_ref.shape
     cuts = tile // CHUNK
@@ -136,23 +150,12 @@
             source, held.at[pl.ds(g * GROUP - EARLY, GROUP)], sems.at[g - EARLY // GROUP]
         )
 
-    indices = [
-        pltpu.make_async_copy(source, target, index_sems.at[i])
-        for i, (source, target) in enumerate(
-            ((rows_hbm, rows_ref), (cols_hbm, cols_ref))
-        )
-    ]
-    for load in indices:
-        load.start()
     count = jnp.clip(count_ref[0, 0], 1, slots)
     used = (count + GROUP - 1) // GROUP
 
     @pl.loop(EARLY // GROUP, used)
     def _(g):
         copy(g).start()
-
-    for load in indices:
-        load.wait()
 
     def add_group(g, tile_at):
         for j in range(GROUP):
@@ -187,14 +190,11 @@
             jax.ShapeDtypeStruct(sums.shape, sums.dtype),
         ),
         input_output_aliases={5: 1},
-        in_specs=[HBM, HBM, pl.BlockSpec(memory_space=pltpu.SMEM), VMEM, VMEM, VMEM, HBM],
+        in_specs=[SMEM, SMEM, SMEM, VMEM, VMEM, VMEM, HBM],
         out_specs=(VMEM, VMEM),
         scratch_shapes=[
             pltpu.VMEM((slots - EARLY, tile, tile), jnp.bfloat16),
-            pltpu.SMEM(rows.shape, rows.dtype),
-            pltpu.SMEM(cols.shape, cols.dtype),
             pltpu.SemaphoreType.DMA(((slots - EARLY) // GROUP,)),
-            pltpu.SemaphoreType.DMA((2,)),
         ],
         compiler_params=pltpu.CompilerParams(vmem_limit_bytes=28 << 20),
         cost_estimate=pl.CostEstimate(
@@ -645,7 +645,9 @@
         for a in (features, pre_activation, out_grad, weight, tiles[0, 0], rows, cols)
     )
     out_tiles = 8 * (features.shape[0] // tiles.shape[1])
-    grad, early, sums = local_grads(pre_activation, out_grad, tiles, out_tiles)
+    grad, early, sums, rows, cols = local_grads(
+        pre_activation, out_grad, tiles, rows, cols, out_tiles
+    )
     part = tile_products(rows, cols, counts, grad, early, sums, tiles, out_tiles)
     return finish(*flow(part, weight, features))
 

time: 76 us -> 78.3 us (1.030)
  Pallas kernels: 74.5 us -> 76.8 us
    pallas_call x1, Pallas kernels: 66 us -> 68.7 us  [flow(): pl.pallas_call(flow_kernel, out_shape=(jax.ShapeDtypeStruct((nodes, width...]
    pallas_call x1, Pallas kernels: 3.18 us -> 2.13 us  [tile_products(): pl.pallas_call(tile_kernel, out_shape=(jax.ShapeDtypeStruct((out_tiles *...]
where the time goes in v10:
time: 78.3 us; the launch traced here: 78.2 us
  Pallas kernels  76.8 us (98%)
  between operations  1.3 us (2%)
    pallas_call x1, Pallas kernels, flow(): pl.pallas_call(flow_kernel, out_shape=(jax.ShapeDtypeStruct((nodes, width...  68.7 us
    pallas_call x1, Pallas kernels, local_grads(): pl.pallas_call(grad_kernel, out_shape=(jax.ShapeDtypeStruct((2 * own_tile...  5.05 us
    pallas_call x1, Pallas kernels, tile_products(): pl.pallas_call(tile_kernel, out_shape=(jax.ShapeDtypeStruct((out_tiles *...  2.13 us

profile of v10, /device:TPU:1, one launch (start us, length us, event | category | flops | bytes accessed | tf_op | source)
XLA Modules:
  0.0 78.2 jit_solution(11226144518636138504)
XLA Ops:
  1.3 5.0 %local_grads.1 = (bf16[16,128,256]{2,1,0:T(8,128)(2,1)S(1)}, bf16[48,256,256]{2,1,0:T(8,128)(2,1)S(1)}, f32[65,128,256]{2,1,0:T(8,128)S(1)}, s32[1,1,128]{2,1,0:T(1,128)S(1)}, s32[1,1,128]{2,1,0:T(1,128)S(1)}) custom-call(bf16[2048,128]{1,0:T(8,128)(2,1)} %pre_hbm.1, bf16[2048,128]{1,0:T(8,128)(2,1)} %out_grad_hbm.1, bf16[128,256,256]{2,1,0:T(8,128)(2,1)} %bitcast.1, ...), custom_call_target="tpu_custom_call" | custom-call | flops 2621440 | bytes 2097152 | tf_op jit(solution)/shard_map/local_grads/pallas_call | solution.py:109
  6.3 2.1 %tile_products.1 = (bf16[128,128,128]{2,1,0:T(8,128)(2,1)S(1)}, f32[65,128,256]{2,1,0:T(8,128)S(1)}) custom-call(s32[1,1,128]{2,1,0:T(1,128)S(1)} %get-tuple-element.10.rows_ref, s32[1,1,128]{2,1,0:T(1,128)S(1)} %get-tuple-element.11.cols_ref, s32[1,1]{1,0:T(1,128)S(6)} %copy.12.count_ref, ...), custom_call_target="tpu_custom_call", output_to_operand_aliasing={{1}: (5, {})} | custom-call | flops 2147483648 | bytes 16777216 | tf_op jit(solution)/shard_map/tile_products/pallas_call | solution.py:186
  8.5 68.7 %flow.1 = (bf16[2048,128]{1,0:T(8,128)(2,1)S(1)}, bf16[2,8,4,16,128]{4,3,2,1,0:T(8,128)(2,1)S(1)}) custom-call(bf16[128,128,128]{2,1,0:T(8,128)(2,1)S(1)} %get-tuple-element.15.part_all, bf16[128,1024]{1,0:T(8,128)(2,1)} %weight_hbm.1, bf16[2048,128]{1,0:T(8,128)(2,1)} %feat_hbm.1), custom_call_target="tpu_custom_call" | custom-call | flops 1073741824 | bytes 16777216 | tf_op jit(solution)/shard_map/flow/pallas_call | solution.py:562
  77.2 1.0 %finish.1 = (bf16[2048,128]{1,0:T(8,128)(2,1)}, f32[128,1024]{1,0:T(8,128)}) custom-call(bf16[2048,128]{1,0:T(8,128)(2,1)S(1)} %get-tuple-element.16.gf_ref, bf16[2,8,4,16,128]{4,3,2,1,0:T(8,128)(2,1)S(1)} %get-tuple-element.17.gw_ref), custom_call_target="tpu_custom_call" | custom-call | bytes 1048576 | tf_op jit(solution)/shard_map/finish/pallas_call | solution.py:627

commit v11 on v10

--- a/solution.py
+++ b/solution.py
@@ -116,7 +116,7 @@
             jax.ShapeDtypeStruct(cols.shape, cols.dtype),
         ),
         in_specs=[HBM] * 5,
-        out_specs=(VMEM, VMEM, VMEM, SMEM, SMEM),
+        out_specs=(VMEM,) * 5,
         scratch_shapes=[
             pltpu.VMEM(pre.shape, pre.dtype),
             pltpu.VMEM(pre.shape, pre.dtype),

time: 78.3 us -> 76.5 us (0.977); the launches traced: 78.2 us -> 77.5 us
    pallas_call x1, Pallas kernels: 68.7 us -> 67.6 us  [flow(): pl.pallas_call(flow_kernel, out_shape=(jax.ShapeDtypeStruct((nodes, width...]
    pallas_call x1, Pallas kernels: 2.13 us -> 3.15 us  [tile_products(): pl.pallas_call(tile_kernel, out_shape=(jax.ShapeDtypeStruct((out_tiles *...]
where the time goes in v11:
time: 76.5 us; the launch traced here: 77.5 us
  Pallas kernels  76.2 us (100%)
  between operations  1.3 us (2%)
    pallas_call x1, Pallas kernels, flow(): pl.pallas_call(flow_kernel, out_shape=(jax.ShapeDtypeStruct((nodes, width...  67.6 us
    pallas_call x1, Pallas kernels, local_grads(): pl.pallas_call(grad_kernel, out_shape=(jax.ShapeDtypeStruct((2 * own_tile...  4.43 us
    pallas_call x1, Pallas kernels, tile_products(): pl.pallas_call(tile_kernel, out_shape=(jax.ShapeDtypeStruct((out_tiles *...  3.15 us

profile of v11, /device:TPU:1, one launch (start us, length us, event | category | flops | bytes accessed | tf_op | source)
XLA Modules:
  0.0 77.5 jit_solution(16486108125221558858)
XLA Ops:
  1.3 4.4 %local_grads.1 = (bf16[16,128,256]{2,1,0:T(8,128)(2,1)S(1)}, bf16[48,256,256]{2,1,0:T(8,128)(2,1)S(1)}, f32[65,128,256]{2,1,0:T(8,128)S(1)}, s32[1,1,128]{2,1,0:T(1,128)S(1)}, s32[1,1,128]{2,1,0:T(1,128)S(1)}) custom-call(bf16[2048,128]{1,0:T(8,128)(2,1)} %pre_hbm.1, bf16[2048,128]{1,0:T(8,128)(2,1)} %out_grad_hbm.1, bf16[128,256,256]{2,1,0:T(8,128)(2,1)} %bitcast.1, ...), custom_call_target="tpu_custom_call" | custom-call | flops 2621440 | bytes 2097152 | tf_op jit(solution)/shard_map/local_grads/pallas_call | solution.py:109
  5.7 3.2 %tile_products.1 = (bf16[128,128,128]{2,1,0:T(8,128)(2,1)S(1)}, f32[65,128,256]{2,1,0:T(8,128)S(1)}) custom-call(s32[1,1,128]{2,1,0:T(1,128)S(1)} %get-tuple-element.10.rows_ref, s32[1,1,128]{2,1,0:T(1,128)S(1)} %get-tuple-element.11.cols_ref, s32[1,1]{1,0:T(1,128)S(6)} %copy.12.count_ref, ...), custom_call_target="tpu_custom_call", output_to_operand_aliasing={{1}: (5, {})} | custom-call | flops 2147483648 | bytes 16777216 | tf_op jit(solution)/shard_map/tile_products/pallas_call | solution.py:186
  8.9 67.6 %flow.1 = (bf16[2048,128]{1,0:T(8,128)(2,1)S(1)}, bf16[2,8,4,16,128]{4,3,2,1,0:T(8,128)(2,1)S(1)}) custom-call(bf16[128,128,128]{2,1,0:T(8,128)(2,1)S(1)} %get-tuple-element.15.part_all, bf16[128,1024]{1,0:T(8,128)(2,1)} %weight_hbm.1, bf16[2048,128]{1,0:T(8,128)(2,1)} %feat_hbm.1), custom_call_target="tpu_custom_call" | custom-call | flops 1073741824 | bytes 16777216 | tf_op jit(solution)/shard_map/flow/pallas_call | solution.py:562
  76.5 1.0 %finish.1 = (bf16[2048,128]{1,0:T(8,128)(2,1)}, f32[128,1024]{1,0:T(8,128)}) custom-call(bf16[2048,128]{1,0:T(8,128)(2,1)S(1)} %get-tuple-element.16.gf_ref, bf16[2,8,4,16,128]{4,3,2,1,0:T(8,128)(2,1)S(1)} %get-tuple-element.17.gw_ref), custom_call_target="tpu_custom_call" | custom-call | bytes 1048576 | tf_op jit(solution)/shard_map/finish/pallas_call | solution.py:627

commit v12 on v11

--- a/solution.py
+++ b/solution.py
@@ -8,7 +8,7 @@
 from jax.sharding import PartitionSpec as P
 
 GROUP = 16
-EARLY = 48
+EARLY = 32
 RING = 4
 LAGS = (0, 2, 5, 8, 4)
 MESH = pl.DeviceIdType.MESH

time: 76.5 us -> 75.7 us (0.990); the launches traced: 77.5 us -> 75.5 us
  Pallas kernels: 76.2 us -> 74.2 us
    pallas_call x1, Pallas kernels: 67.6 us -> 65 us  [flow(): pl.pallas_call(flow_kernel, out_shape=(jax.ShapeDtypeStruct((nodes, width...]
where the time goes in v12:
time: 75.7 us; the launch traced here: 75.5 us
  Pallas kernels  74.2 us (98%)
  between operations  1.3 us (2%)
    pallas_call x1, Pallas kernels, flow(): pl.pallas_call(flow_kernel, out_shape=(jax.ShapeDtypeStruct((nodes, width...  65 us
    pallas_call x1, Pallas kernels, local_grads(): pl.pallas_call(grad_kernel, out_shape=(jax.ShapeDtypeStruct((2 * own_tile...  4.42 us
    pallas_call x1, Pallas kernels, tile_products(): pl.pallas_call(tile_kernel, out_shape=(jax.ShapeDtypeStruct((out_tiles *...  3.79 us

profile of v12, /device:TPU:1, one launch (start us, length us, event | category | flops | bytes accessed | tf_op | source)
XLA Modules:
  0.0 75.5 jit_solution(15871332871425075667)
XLA Ops:
  1.3 4.4 %local_grads.1 = (bf16[16,128,256]{2,1,0:T(8,128)(2,1)S(1)}, bf16[32,256,256]{2,1,0:T(8,128)(2,1)S(1)}, f32[65,128,256]{2,1,0:T(8,128)S(1)}, s32[1,1,128]{2,1,0:T(1,128)S(1)}, s32[1,1,128]{2,1,0:T(1,128)S(1)}) custom-call(bf16[2048,128]{1,0:T(8,128)(2,1)} %pre_hbm.1, bf16[2048,128]{1,0:T(8,128)(2,1)} %out_grad_hbm.1, bf16[128,256,256]{2,1,0:T(8,128)(2,1)} %bitcast.1, ...), custom_call_target="tpu_custom_call" | custom-call | flops 2621440 | bytes 2097152 | tf_op jit(solution)/shard_map/local_grads/pallas_call | solution.py:109
  5.7 3.8 %tile_products.1 = (bf16[128,128,128]{2,1,0:T(8,128)(2,1)S(1)}, f32[65,128,256]{2,1,0:T(8,128)S(1)}) custom-call(s32[1,1,128]{2,1,0:T(1,128)S(1)} %get-tuple-element.10.rows_ref, s32[1,1,128]{2,1,0:T(1,128)S(1)} %get-tuple-element.11.cols_ref, s32[1,1]{1,0:T(1,128)S(6)} %copy.12.count_ref, ...), custom_call_target="tpu_custom_call", output_to_operand_aliasing={{1}: (5, {})} | custom-call | flops 2147483648 | bytes 16777216 | tf_op jit(solution)/shard_map/tile_products/pallas_call | solution.py:186
  9.5 65.0 %flow.1 = (bf16[2048,128]{1,0:T(8,128)(2,1)S(1)}, bf16[2,8,4,16,128]{4,3,2,1,0:T(8,128)(2,1)S(1)}) custom-call(bf16[128,128,128]{2,1,0:T(8,128)(2,1)S(1)} %get-tuple-element.15.part_all, bf16[128,1024]{1,0:T(8,128)(2,1)} %weight_hbm.1, bf16[2048,128]{1,0:T(8,128)(2,1)} %feat_hbm.1), custom_call_target="tpu_custom_call" | custom-call | flops 1073741824 | bytes 16777216 | tf_op jit(solution)/shard_map/flow/pallas_call | solution.py:562
  74.5 1.0 %finish.1 = (bf16[2048,128]{1,0:T(8,128)(2,1)}, f32[128,1024]{1,0:T(8,128)}) custom-call(bf16[2048,128]{1,0:T(8,128)(2,1)S(1)} %get-tuple-element.16.gf_ref, bf16[2,8,4,16,128]{4,3,2,1,0:T(8,128)(2,1)S(1)} %get-tuple-element.17.gw_ref), custom_call_target="tpu_custom_call" | custom-call | bytes 1048576 | tf_op jit(solution)/shard_map/finish/pallas_call | solution.py:627

commit v13 on v12

--- a/solution.py
+++ b/solution.py
@@ -7,8 +7,8 @@
 from jax.experimental.pallas import tpu as pltpu
 from jax.sharding import PartitionSpec as P
 
-GROUP = 16
-EARLY = 32
+GROUP = 32
+EARLY = 64
 RING = 4
 LAGS = (0, 2, 5, 8, 4)
 MESH = pl.DeviceIdType.MESH

time: 75.7 us -> 76.7 us (1.013)
  Pallas kernels: 74.2 us -> 75.7 us
    pallas_call x1, Pallas kernels: 65 us -> 67.3 us  [flow(): pl.pallas_call(flow_kernel, out_shape=(jax.ShapeDtypeStruct((nodes, width...]
    pallas_call x1, Pallas kernels: 3.79 us -> 2.99 us  [tile_products(): pl.pallas_call(tile_kernel, out_shape=(jax.ShapeDtypeStruct((out_tiles *...]
where the time goes in v13:
time: 76.7 us; the launch traced here: 77 us
  Pallas kernels  75.7 us (99%)
  between operations  1.3 us (2%)
    pallas_call x1, Pallas kernels, flow(): pl.pallas_call(flow_kernel, out_shape=(jax.ShapeDtypeStruct((nodes, width...  67.3 us
    pallas_call x1, Pallas kernels, local_grads(): pl.pallas_call(grad_kernel, out_shape=(jax.ShapeDtypeStruct((2 * own_tile...  4.42 us
    pallas_call x1, Pallas kernels, tile_products(): pl.pallas_call(tile_kernel, out_shape=(jax.ShapeDtypeStruct((out_tiles *...  2.99 us

profile of v13, /device:TPU:1, one launch (start us, length us, event | category | flops | bytes accessed | tf_op | source)
XLA Modules:
  0.0 77.0 jit_solution(3179899969375415002)
XLA Ops:
  1.3 4.4 %local_grads.1 = (bf16[16,128,256]{2,1,0:T(8,128)(2,1)S(1)}, bf16[64,256,256]{2,1,0:T(8,128)(2,1)S(1)}, f32[65,128,256]{2,1,0:T(8,128)S(1)}, s32[1,1,128]{2,1,0:T(1,128)S(1)}, s32[1,1,128]{2,1,0:T(1,128)S(1)}) custom-call(bf16[2048,128]{1,0:T(8,128)(2,1)} %pre_hbm.1, bf16[2048,128]{1,0:T(8,128)(2,1)} %out_grad_hbm.1, bf16[128,256,256]{2,1,0:T(8,128)(2,1)} %bitcast.1, ...), custom_call_target="tpu_custom_call" | custom-call | flops 2621440 | bytes 2097152 | tf_op jit(solution)/shard_map/local_grads/pallas_call | solution.py:109
  5.7 3.0 %tile_products.1 = (bf16[128,128,128]{2,1,0:T(8,128)(2,1)S(1)}, f32[65,128,256]{2,1,0:T(8,128)S(1)}) custom-call(s32[1,1,128]{2,1,0:T(1,128)S(1)} %get-tuple-element.10.rows_ref, s32[1,1,128]{2,1,0:T(1,128)S(1)} %get-tuple-element.11.cols_ref, s32[1,1]{1,0:T(1,128)S(6)} %copy.12.count_ref, ...), custom_call_target="tpu_custom_call", output_to_operand_aliasing={{1}: (5, {})} | custom-call | flops 2147483648 | bytes 16777216 | tf_op jit(solution)/shard_map/tile_products/pallas_call | solution.py:186
  8.7 67.3 %flow.1 = (bf16[2048,128]{1,0:T(8,128)(2,1)S(1)}, bf16[2,8,4,16,128]{4,3,2,1,0:T(8,128)(2,1)S(1)}) custom-call(bf16[128,128,128]{2,1,0:T(8,128)(2,1)S(1)} %get-tuple-element.15.part_all, bf16[128,1024]{1,0:T(8,128)(2,1)} %weight_hbm.1, bf16[2048,128]{1,0:T(8,128)(2,1)} %feat_hbm.1), custom_call_target="tpu_custom_call" | custom-call | flops 1073741824 | bytes 16777216 | tf_op jit(solution)/shard_map/flow/pallas_call | solution.py:562
  76.0 1.0 %finish.1 = (bf16[2048,128]{1,0:T(8,128)(2,1)}, f32[128,1024]{1,0:T(8,128)}) custom-call(bf16[2048,128]{1,0:T(8,128)(2,1)S(1)} %get-tuple-element.16.gf_ref, bf16[2,8,4,16,128]{4,3,2,1,0:T(8,128)(2,1)S(1)} %get-tuple-element.17.gw_ref), custom_call_target="tpu_custom_call" | custom-call | bytes 1048576 | tf_op jit(solution)/shard_map/finish/pallas_call | solution.py:627
